TPU v7x, 32 devices: a whole 2x2x4 slice. The times are simulated.
32 devices in a mesh: dp: 8 (over y, x, core), blk: 4 (over z).
Axes of the slice: x: 2, y: 2, z: 4, core: 2. Of those that a mesh axis runs over, the one named last changes fastest.
Arguments:
- bytes_in: bfloat16 [131072, 512], P(('dp', 'blk')), may hold values from -16 to 16
- flags: int32 [131072], P(('dp', 'blk')), may hold values from 0 to 1, as said below
- lengths: int32 [8, 4], P('dp'), may hold values from 1024 to 13312, as said below
- cotangent: float32 [16384, 512], P(('dp', 'blk')), may hold values from -6 to 6
- w_query: bfloat16 [512, 512], replicated, may hold values from -0.25 to 0.25
- w_key: bfloat16 [512, 512], replicated, may hold values from -0.25 to 0.25
- w_value: bfloat16 [512, 512], replicated, may hold values from -0.25 to 0.25
- w_out: bfloat16 [512, 512], replicated, may hold values from -2 to 2
- w_up: bfloat16 [512, 2048], replicated, may hold values from -0.25 to 0.25
- w_down: bfloat16 [2048, 512], replicated, may hold values from -0.125 to 0.125
- gain_attn: float32 [512], replicated, may hold values from 0.5 to 1.5
- gain_ffn: float32 [512], replicated, may hold values from 0.5 to 1.5
Outputs:
- output: float32 [16384, 512], P(('dp', 'blk'))
- grad_bytes: float32 [131072, 512], P(('dp', 'blk'))
- grad_w_query: float32 [512, 512], replicated
- grad_w_key: float32 [512, 512], replicated
- grad_w_value: float32 [512, 512], replicated
- grad_w_out: float32 [512, 512], replicated
- grad_w_up: float32 [512, 2048], replicated
- grad_w_down: float32 [2048, 512], replicated
- grad_gain_attn: float32 [512], replicated
- grad_gain_ffn: float32 [512], replicated
Inputs may be any that keep to these rules, and one draw needn't show every extreme that they name: `flags`: each aligned cell of 8 bytes holds at most one 1; the first cell of every block of 4096 bytes holds one; the first byte of every sequence is a 1; in each group some block of 4096 bytes holds exactly 512 ones. The lengths of a group add up to 16384; one of them is 13312, the others 1024.
All inputs are finite; a program needn't handle non-finite values.
Results may differ from a plain program's by a relative error of at most 0.015.
Values may be sent and summed in bfloat16 or wider, within the bound.
A program may use at most 320 MiB of HBM per device.

v0:
```python
import jax
import jax.numpy as jnp
from jax import lax
from jax.sharding import PartitionSpec as P

HEADS = 8
HEAD_DIM = 64


EPSILON = 1e-05
ROTARY_BASE = 10000.0
NEGATIVE = -1e30


def passed_along(block, axis, distance):
    devices = range(lax.axis_size(axis))
    route = [((i - distance) % len(devices), i) for i in devices]
    return lax.ppermute(block, axis, route)


def from_behind(value, axis, by):
    count = lax.axis_size(axis)
    pairs = [(i, i + by) for i in range(count) if 0 <= i + by < count]
    return lax.ppermute(value, axis, pairs)


def rotate(vectors, positions, direction):
    half_dim = vectors.shape[-1] // 2
    freqs = ROTARY_BASE ** (-2.0 * jnp.arange(half_dim, dtype=jnp.float32) / vectors.shape[-1])
    angles = positions.astype(jnp.float32)[:, None] * freqs[None, :]
    cosine = jnp.cos(angles)[:, None, :]
    sine = direction * jnp.sin(angles)[:, None, :]
    first_half = vectors[..., :half_dim]
    second_half = vectors[..., half_dim:]
    return jnp.concatenate(
        [first_half * cosine - second_half * sine, second_half * cosine + first_half * sine],
        axis=-1,
    )


def layer_norm_parts(values, gain):
    center = values - jnp.mean(values, axis=-1, keepdims=True)
    spread = jnp.mean(center * center, axis=-1, keepdims=True)
    inverse = lax.rsqrt(spread + EPSILON)
    normed = center * inverse
    return (normed * gain, normed, inverse)


def layer_norm_back(grad_in, normed, inverse, gain):
    scaled = grad_in * gain
    grad_values = inverse * (
        scaled
        - jnp.mean(scaled, axis=-1, keepdims=True)
        - normed * jnp.mean(scaled * normed, axis=-1, keepdims=True)
    )
    grad_gain = jnp.sum(grad_in * normed, axis=0)
    return (grad_values, grad_gain)


def pass_grads(grad_key, grad_value):
    return (
        passed_along(grad_key.astype(jnp.bfloat16), "blk", 1).astype(grad_key.dtype),
        passed_along(grad_value.astype(jnp.bfloat16), "blk", 1).astype(grad_value.dtype),
    )


def local(
    bytes_in,
    flags,
    lengths,
    cotangent,
    w_query,
    w_key,
    w_value,
    w_out,
    w_up,
    w_down,
    gain_attn,
    gain_ffn,
):
    blocks = lax.axis_size("blk")
    own_index = lax.axis_index("blk")
    seg_rows = cotangent.shape[0]
    byte_rows = bytes_in.shape[0]
    features = bytes_in.shape[1]
    scale = HEAD_DIM ** (-0.5)
    running = jnp.cumsum(flags)
    slot_of = running - 1
    seg_count = running[-1]
    slot_ids = jnp.arange(seg_rows, dtype=jnp.int32)
    member = (slot_of[None, :] == slot_ids[:, None]).astype(jnp.bfloat16)
    seg_sums = jnp.dot(member, bytes_in, preferred_element_type=jnp.float32)
    seg_tally = jnp.sum(member, axis=1, dtype=jnp.float32)
    leading = slot_of < 0
    tail_sum = jnp.dot(
        leading.astype(jnp.bfloat16)[None, :], bytes_in, preferred_element_type=jnp.float32
    )
    tail_count = jnp.sum(leading.astype(jnp.float32), keepdims=True)
    got_sum, got_count = from_behind((tail_sum, tail_count), "blk", -1)
    last_slot = slot_ids == seg_count - 1
    seg_sums = seg_sums + jnp.where(last_slot[:, None], got_sum, 0.0)
    seg_tally = seg_tally + jnp.where(last_slot, got_count[0], 0.0)
    divisor = jnp.maximum(seg_tally, 1.0)
    pooled = seg_sums / divisor[:, None]
    starts = jnp.cumsum(lengths[0]) - lengths[0]
    byte_at = own_index * byte_rows + jnp.arange(byte_rows, dtype=jnp.int32)
    prior_flags = jnp.sum(
        flags[None, :] * (byte_at[None, :] < starts[:, None]).astype(jnp.int32), axis=1
    )
    all_counts, all_prior = (
        lax.all_gather(seg_count[None], "blk", axis=0, tiled=True),
        lax.all_gather(prior_flags[None, :], "blk", axis=0, tiled=True),
    )
    offsets = jnp.cumsum(all_counts) - all_counts
    seq_first = jnp.sum(all_prior, axis=0)
    dev_ids = jnp.arange(blocks, dtype=jnp.int32)

    def layout(first_row, row_count):
        row_index = first_row + jnp.arange(row_count, dtype=jnp.int32)
        owner_dev = row_index // seg_rows
        within = row_index % seg_rows
        dev_pick = owner_dev[:, None] == dev_ids[None, :]
        dev_base = jnp.sum(jnp.where(dev_pick, offsets[None, :], 0), axis=1)
        dev_have = jnp.sum(jnp.where(dev_pick, all_counts[None, :], 0), axis=1)
        return (dev_base + jnp.minimum(within, dev_have - 1), within < dev_have)

    query_pos, query_live = layout(own_index * seg_rows, seg_rows)
    query_first = jnp.max(
        jnp.where(seq_first[None, :] <= query_pos[:, None], seq_first[None, :], 0), axis=1
    )

    def visible(first_row, row_count):
        key_pos, key_live = layout(first_row, row_count)
        return (
            (key_pos[None, :] <= query_pos[:, None])
            & (key_pos[None, :] >= query_first[:, None])
            & key_live[None, :]
        )

    normed_attn, unit_attn, scale_attn = layer_norm_parts(pooled, gain_attn)
    n_one = normed_attn.astype(jnp.bfloat16)
    query_pre = jnp.dot(n_one, w_query, preferred_element_type=jnp.float32)
    query_rot = rotate(query_pre.reshape(seg_rows, HEADS, HEAD_DIM), query_pos, 1.0).astype(
        jnp.bfloat16
    )
    key_pre = jnp.dot(n_one, w_key, preferred_element_type=jnp.float32)
    key_rot = (
        rotate(key_pre.reshape(seg_rows, HEADS, HEAD_DIM), query_pos, 1.0)
        .reshape(seg_rows, features)
        .astype(jnp.bfloat16)
    )
    value_low = jnp.dot(n_one, w_value, preferred_element_type=jnp.float32).astype(jnp.bfloat16)
    start_state = (
        jnp.full((HEADS, seg_rows), NEGATIVE, jnp.float32),
        jnp.zeros((HEADS, seg_rows), jnp.float32),
        jnp.zeros((seg_rows, HEADS, HEAD_DIM), jnp.float32),
    )
    key_piece = lax.all_gather(key_rot, "blk", axis=0, tiled=True)
    value_piece = lax.all_gather(value_low, "blk", axis=0, tiled=True)
    row_count = key_piece.shape[0]
    allowed = visible(jnp.int32(0), row_count)

    def absorb_update(running_state):
        row_max, row_sum, weighted = running_state
        scores = (
            jnp.einsum(
                "qhe,khe->hqk",
                query_rot,
                key_piece.reshape(row_count, HEADS, HEAD_DIM),
                preferred_element_type=jnp.float32,
            )
            * scale
        )
        scores = jnp.where(allowed[None], scores, NEGATIVE)
        new_max = jnp.maximum(row_max, jnp.max(scores, axis=-1))
        weights = jnp.where(allowed[None], jnp.exp(scores - new_max[:, :, None]), 0.0)
        shrink = jnp.exp(row_max - new_max)
        row_sum = jnp.sum(weights, axis=-1)
        weighted = weighted * shrink.T[:, :, None] + jnp.einsum(
            "hqk,khe->qhe",
            weights.astype(jnp.bfloat16),
            value_piece.reshape(row_count, HEADS, HEAD_DIM),
            preferred_element_type=jnp.float32,
        )
        return (new_max, row_sum, weighted)

    row_max, row_sum, weighted = lax.cond(
        jnp.any(allowed), absorb_update, lambda unchanged: unchanged, start_state
    )
    log_total = row_max + jnp.log(row_sum)
    attended_full = weighted / row_sum.T[:, :, None]
    attended = attended_full.reshape(seg_rows, features).astype(jnp.bfloat16)
    middle = pooled + jnp.dot(attended, w_out, preferred_element_type=jnp.float32)
    normed_ffn, unit_ffn, scale_ffn = layer_norm_parts(middle, gain_ffn)
    n_two = normed_ffn.astype(jnp.bfloat16)
    up_proj = jnp.dot(n_two, w_up, preferred_element_type=jnp.float32)
    act_full, gelu_back = jax.vjp(lambda inner: jax.nn.gelu(inner, approximate=False), up_proj)
    act_low = act_full.astype(jnp.bfloat16)
    result = middle + jnp.dot(act_low, w_down, preferred_element_type=jnp.float32)
    live_rows = query_live.astype(jnp.float32)[:, None]
    output = result * live_rows
    grad_out = cotangent * live_rows
    grad_branch = grad_out.astype(jnp.bfloat16)
    grad_w_down = jnp.einsum("sf,sd->fd", act_low, grad_branch, preferred_element_type=jnp.float32)
    grad_act = jnp.einsum("sd,fd->sf", grad_branch, w_down, preferred_element_type=jnp.float32)
    grad_up = gelu_back(grad_act)[0].astype(jnp.bfloat16)
    grad_w_up = jnp.einsum("sd,sf->df", n_two, grad_up, preferred_element_type=jnp.float32)
    grad_n_two = jnp.einsum("sf,df->sd", grad_up, w_up, preferred_element_type=jnp.float32)
    grad_mid_norm, grad_gain_ffn = layer_norm_back(grad_n_two, unit_ffn, scale_ffn, gain_ffn)
    grad_middle = grad_out + grad_mid_norm
    grad_attn_branch = grad_middle.astype(jnp.bfloat16)
    grad_w_out = jnp.einsum(
        "sd,se->de", attended, grad_attn_branch, preferred_element_type=jnp.float32
    )
    grad_attended = jnp.einsum(
        "se,de->sd", grad_attn_branch, w_out, preferred_element_type=jnp.float32
    ).astype(jnp.bfloat16)
    grad_att_three = grad_attended.reshape(seg_rows, HEADS, HEAD_DIM)
    row_dot = jnp.sum(grad_att_three.astype(jnp.float32) * attended_full, axis=-1).T

    def block_grads(key_piece, value_piece, source, grad_parts):
        allowed = visible(source * seg_rows, seg_rows)

        def block_update(grad_parts):
            grad_key, grad_value, grad_query = grad_parts
            key_three = key_piece.reshape(seg_rows, HEADS, HEAD_DIM)
            value_three = value_piece.reshape(seg_rows, HEADS, HEAD_DIM)
            scores = (
                jnp.einsum("qhe,khe->hqk", query_rot, key_three, preferred_element_type=jnp.float32)
                * scale
            )
            prob_full = jnp.where(allowed[None], jnp.exp(scores - log_total[:, :, None]), 0.0)
            grad_value = grad_value + jnp.einsum(
                "hqk,qhe->khe",
                prob_full.astype(jnp.bfloat16),
                grad_att_three,
                preferred_element_type=jnp.float32,
            ).reshape(seg_rows, features)
            grad_prob = jnp.einsum(
                "qhe,khe->hqk", grad_att_three, value_three, preferred_element_type=jnp.float32
            )
            grad_scores = (prob_full * (grad_prob - row_dot[:, :, None])).astype(jnp.bfloat16)
            grad_query = (
                grad_query
                + jnp.einsum(
                    "hqk,khe->qhe", grad_scores, key_three, preferred_element_type=jnp.float32
                )
                * scale
            )
            grad_key = grad_key + (
                jnp.einsum(
                    "hqk,qhe->khe", grad_scores, query_rot, preferred_element_type=jnp.float32
                )
                * scale
            ).reshape(seg_rows, features)
            return (grad_key, grad_value, grad_query)

        return lax.cond(jnp.any(allowed), block_update, lambda unchanged: unchanged, grad_parts)

    zero_rows = jnp.zeros((seg_rows, features), jnp.float32)
    zero_query = jnp.zeros((seg_rows, HEADS, HEAD_DIM), jnp.float32)

    def visit(visit_no, loop_state):
        key_piece, value_piece, grad_key, grad_value, grad_query = loop_state
        source = (own_index - visit_no) % blocks
        grad_key, grad_value, grad_query = block_grads(
            key_piece, value_piece, source, (grad_key, grad_value, grad_query)
        )
        key_piece, value_piece = from_behind((key_piece, value_piece), "blk", 1)
        grad_key, grad_value = pass_grads(grad_key, grad_value)
        return (key_piece, value_piece, grad_key, grad_value, grad_query)

    loop_out = lax.fori_loop(
        0, blocks, visit, (key_rot, value_low, zero_rows, zero_rows, zero_query)
    )
    grad_key_sum, grad_value_sum, grad_query_rot = (loop_out[2], loop_out[3], loop_out[4])
    grad_query = (
        rotate(grad_query_rot, query_pos, -1.0).reshape(seg_rows, features).astype(jnp.bfloat16)
    )
    grad_key = (
        rotate(grad_key_sum.reshape(seg_rows, HEADS, HEAD_DIM), query_pos, -1.0)
        .reshape(seg_rows, features)
        .astype(jnp.bfloat16)
    )
    grad_value_low = grad_value_sum.astype(jnp.bfloat16)
    grad_w_query = jnp.einsum("sd,se->de", n_one, grad_query, preferred_element_type=jnp.float32)
    grad_w_key = jnp.einsum("sd,se->de", n_one, grad_key, preferred_element_type=jnp.float32)
    grad_w_value = jnp.einsum(
        "sd,se->de", n_one, grad_value_low, preferred_element_type=jnp.float32
    )
    grad_n_one = jnp.einsum("se,de->sd", grad_query, w_query, preferred_element_type=jnp.float32)
    grad_n_one = grad_n_one + jnp.einsum(
        "se,de->sd", grad_key, w_key, preferred_element_type=jnp.float32
    )
    grad_n_one = grad_n_one + jnp.einsum(
        "se,de->sd", grad_value_low, w_value, preferred_element_type=jnp.float32
    )
    grad_pool_norm, grad_gain_attn = layer_norm_back(grad_n_one, unit_attn, scale_attn, gain_attn)
    grad_pooled = grad_middle + grad_pool_norm
    grad_sums = (grad_pooled / divisor[:, None]).astype(jnp.bfloat16)
    last_grad = jnp.dot(
        last_slot.astype(jnp.bfloat16)[None, :], grad_sums, preferred_element_type=jnp.float32
    ).astype(jnp.bfloat16)
    came_grad = from_behind(last_grad, "blk", 1)
    spread_rows = jnp.take(grad_sums, jnp.maximum(slot_of, 0), axis=0)
    grad_bytes = jnp.where(leading[:, None], came_grad, spread_rows).astype(jnp.float32)
    (
        grad_w_query,
        grad_w_key,
        grad_w_value,
        grad_w_out,
        grad_w_up,
        grad_w_down,
        grad_gain_attn,
        grad_gain_ffn,
    ) = lax.psum(
        (
            grad_w_query,
            grad_w_key,
            grad_w_value,
            grad_w_out,
            grad_w_up,
            grad_w_down,
            grad_gain_attn,
            grad_gain_ffn,
        ),
        ("dp", "blk"),
    )
    return (
        output,
        grad_bytes,
        grad_w_query,
        grad_w_key,
        grad_w_value,
        grad_w_out,
        grad_w_up,
        grad_w_down,
        grad_gain_attn,
        grad_gain_ffn,
    )


def solution(mesh):
    return jax.shard_map(
        local,
        mesh=mesh,
        in_specs=(
            P(("dp", "blk"), None),
            P(("dp", "blk")),
            P("dp", None),
            P(("dp", "blk"), None),
            P(),
            P(),
            P(),
            P(),
            P(),
            P(),
            P(),
            P(),
        ),
        out_specs=(
            P(("dp", "blk"), None),
            P(("dp", "blk"), None),
            P(),
            P(),
            P(),
            P(),
            P(),
            P(),
            P(),
            P(),
        ),
        check_vma=False,
    )
```

profile of v0, /device:TPU:9, one launch (start us, length us, event | category | flops | bytes accessed | tf_op | source)
XLA Modules:
  0.0 735.9 jit_solution(15864959008872164530)
XLA Ops:
  12.0 2.8 fusion.74
  14.8 1.9 collective-permute-start.4
  21.5 6.7 all-reduce.2
  30.2 4.7 fusion.70
  38.9 2.3 convolution_convert_fusion.1
  41.7 2.7 fusion.71
  45.0 2.5 copy.36
  47.6 2.1 copy.37
  49.7 35.1 %all-gather.4.cloned.1.call-done = bf16[2048,512]{0,1:T(8,128)(2,1)} async-done(((bf16[512,512]{0,1:T(8,128)(2,1)}), bf16[2048,512]{0,1:T(8,128)(2,1)}) %all-gather.4.cloned.1.call-update) | async-done | bytes 2097168 | tf_op jit(solution)/shard_map/all_gather | solution.py:158
  84.8 46.8 %all-gather.6.cloned.1.call-done = bf16[2048,512]{1,0:T(8,128)(2,1)} async-done(((bf16[512,512]{1,0:T(8,128)(2,1)}), bf16[2048,512]{1,0:T(8,128)(2,1)}) %all-gather.6.cloned.1.call-update) | async-done | bytes 2097168 | tf_op jit(solution)/shard_map/all_gather | solution.py:159
  131.6 54.0 %conditional.2 = (f32[8,512]{1,0:T(8,128)}, f32[8,512]{1,0:T(8,128)}, f32[512,8,64]{0,2,1:T(8,128)}, f32[8,512]{1,0:T(8,128)S(1)}) conditional(s32[]{:T(128)} %convert_element_type.161, () %tuple.50, (pred[512,2048]{1,0:T(8,128)(4,1)}, bf16[2048,512]{0,1:T(8,128)(2,1)}, bf16[512,8,64]{0,2,1:T(8,128)(2,1)S(1)}, bf16[2048,512]{1,0:T(8,128)(2,1)}) %tuple.51), branch_computations={%region_16.17_spmd, %region_17.20_spmd} | conditional | flops 2256801792 | bytes 113934368 | solution.py:187
  132.1 15.6 %fusion.2 = (f32[8,512]{1,0:T(8,128)S(1)}, f32[8,512,2048]{2,1,0:T(8,128)}) fusion(pred[512,2048]{1,0:T(8,128)(4,1)} %get-tuple-element.450, bf16[512,8,64]{0,2,1:T(8,128)(2,1)S(1)} %get-tuple-element.451, bf16[2048,8,64]{0,2,1:T(8,128)(2,1)} %bitcast.112), kind=kOutput, calls=%fused_computation.4 | convolution fusion | flops 1098903552 | bytes 37240832 | tf_op jit(solution)/shard_map/cond/branch_1_fun/qhe,khe->hqk/dot_general | solution.py:166
  148.3 3.9 copy.34
  152.2 16.3 %fusion.11 = f32[512,8,64]{0,2,1:T(8,128)} fusion(bf16[2048,8,64]{0,2,1:T(8,128)(2,1)} %bitcast.115, f32[8,512,2048]{2,1,0:T(8,128)} %get-tuple-element.717, f32[8,512]{1,0:T(8,128)} %get-tuple-element.865, pred[512,2048]{1,0:T(8,128)(4,1)} %get-tuple-element.450, f32[512,8]{0,1:T(8,128)S(1)} %get-tuple-element.700), kind=kOutput, calls=%fused_computation.10 | convolution fusion | flops 1115947008 | bytes 37781504 | tf_op jit(solution)/shard_map/cond/branch_1_fun/hqk,khe->qhe/dot_general | solution.py:179
  168.5 16.3 %fusion.4 = f32[8,512]{1,0:T(8,128)} fusion(f32[8,512,2048]{2,1,0:T(8,128)} %get-tuple-element.717, f32[8,512]{1,0:T(8,128)} %get-tuple-element.865, pred[512,2048]{1,0:T(8,128)(4,1)} %get-tuple-element.450), kind=kLoop, calls=%fused_computation.6 | loop fusion | flops 41938944 | bytes 34635776 | tf_op jit(solution)/shard_map/cond/branch_1_fun/reduce_sum | solution.py:178
  189.0 11.3 %multiply_convert_fusion.1 = (bf16[512,2048]{1,0:T(8,128)(2,1)}, f32[512,2048]{1,0:T(8,128)S(1)}, f32[512,2048]{1,0:T(8,128)S(1)}) fusion(bf16[512,2048]{1,0:T(8,128)(2,1)S(1)} %copy-done, f32[512,512]{0,1:T(8,128)S(1)} %get-tuple-element.738, f32[512]{0:T(512)S(1)} %copy-done.34, f32[512]{0:T(512)S(1)} %add_rsqrt_fusion, f32[512]{0:T(512)S(1)} %broadcast_multiply_fusion.5), kind=kOutput, calls=%fused_computation.57 | convolution fusion | flops 1142947840 | bytes 13637632 | tf_op jit(solution)/shard_map/dot_general | solution.py:196
  200.3 2.8 add_convert_fusion
  203.2 2.1 multiply_reduce_fusion
  205.3 3.3 fusion.65
  209.0 3.5 multiply_reduce_fusion.3
  216.4 237.9 %while.25 = (s32[]{:T(128)}, bf16[512,512]{0,1:T(8,128)(2,1)S(1)}, bf16[512,512]{0,1:T(8,128)(2,1)S(1)}, f32[512,512]{0,1:T(8,128)}, f32[512,512]{0,1:T(8,128)},...) while((s32[]{:T(128)}, bf16[512,512]{0,1:T(8,128)(2,1)S(1)}, ...), condition=%wide.region_31.32_spmd.clone, body=%wide.region_25.31_spmd.clone.sunk | while | flops 1367374848 | bytes 78061328 | solution.py:273
  219.5 11.7 %conditional.5 = ((f32[512,512]{0,1:T(8,128)S(1)}, f32[512,512]{0,1:T(8,128)S(1)}, f32[512,8,64]{0,2,1:T(8,128)})) conditional(s32[]{:T(128)} %convert_element_type.240, (f32[512,512]{0,1:T(8,128)S(1)}, f32[512,512]{0,1:T(8,128)S(1)}, f32[512,8,64]{0,2,1:T(8,128)}) %tuple.119, (pred[512,512]{1,0:T(8,128)(4,1)S(1)}, ...), branch_computations={%region_29.29_spmd, %region_30.30_spmd} | conditional | flops 1364459520 | bytes 56803472 | solution.py:258
  220.9 3.5 multiply_convert_fusion
  227.6 3.6 fusion.22
  234.5 4.1 collective-permute-start
  238.5 1.9 collective-permute-start.1
  240.5 5.5 collective-permute-done.2
  247.1 10.2 %collective-permute-done.3 = bf16[512,512]{0,1:T(8,128)(2,1)} collective-permute-done((bf16[512,512]{0,1:T(8,128)(2,1)S(1)}, bf16[512,512]{0,1:T(8,128)(2,1)}, u32[]{:S(2)}, u32[]{:S(2)}) %collective-permute-start.3) | collective-permute-done | bytes 524320 | tf_op jit(solution)/shard_map/while/body/eval_jaxpr/ppermute | solution.py:18
  257.3 2.1 convert_element_type.244
  259.5 9.0 %collective-permute-done = bf16[512,512]{0,1:T(8,128)(2,1)S(1)} collective-permute-done((bf16[512,512]{0,1:T(8,128)(2,1)S(1)}, bf16[512,512]{0,1:T(8,128)(2,1)S(1)}, u32[]{:S(2)}, u32[]{:S(2)}) %collective-permute-start) | collective-permute-done | bytes 524320 | tf_op jit(solution)/shard_map/while/body/eval_jaxpr/ppermute | solution.py:24
  268.5 11.2 %collective-permute-done.1 = bf16[512,512]{0,1:T(8,128)(2,1)S(1)} collective-permute-done((bf16[512,512]{0,1:T(8,128)(2,1)}, bf16[512,512]{0,1:T(8,128)(2,1)S(1)}, u32[]{:S(2)}, u32[]{:S(2)}) %collective-permute-start.1) | collective-permute-done | bytes 524320 | tf_op jit(solution)/shard_map/while/body/eval_jaxpr/ppermute | solution.py:24
  284.2 11.7 %conditional.5 = ((f32[512,512]{0,1:T(8,128)S(1)}, f32[512,512]{0,1:T(8,128)S(1)}, f32[512,8,64]{0,2,1:T(8,128)})) conditional(s32[]{:T(128)} %convert_element_type.240, (f32[512,512]{0,1:T(8,128)S(1)}, f32[512,512]{0,1:T(8,128)S(1)}, f32[512,8,64]{0,2,1:T(8,128)}) %tuple.119, (pred[512,512]{1,0:T(8,128)(4,1)S(1)}, ...), branch_computations={%region_29.29_spmd, %region_30.30_spmd} | conditional | flops 1364459520 | bytes 56803472 | solution.py:258
  285.6 3.5 multiply_convert_fusion
  292.3 3.6 fusion.22
  298.5 1.9 collective-permute-start
  300.4 4.1 collective-permute-start.1
  304.6 4.6 collective-permute-done.2
  310.3 10.2 %collective-permute-done.3 = bf16[512,512]{0,1:T(8,128)(2,1)} collective-permute-done((bf16[512,512]{0,1:T(8,128)(2,1)S(1)}, bf16[512,512]{0,1:T(8,128)(2,1)}, u32[]{:S(2)}, u32[]{:S(2)}) %collective-permute-start.3) | collective-permute-done | bytes 524320 | tf_op jit(solution)/shard_map/while/body/eval_jaxpr/ppermute | solution.py:18
  320.5 2.1 convert_element_type.244
  322.7 9.0 %collective-permute-done = bf16[512,512]{0,1:T(8,128)(2,1)S(1)} collective-permute-done((bf16[512,512]{0,1:T(8,128)(2,1)S(1)}, bf16[512,512]{0,1:T(8,128)(2,1)S(1)}, u32[]{:S(2)}, u32[]{:S(2)}) %collective-permute-start) | collective-permute-done | bytes 524320 | tf_op jit(solution)/shard_map/while/body/eval_jaxpr/ppermute | solution.py:24
  331.6 11.2 %collective-permute-done.1 = bf16[512,512]{0,1:T(8,128)(2,1)S(1)} collective-permute-done((bf16[512,512]{0,1:T(8,128)(2,1)}, bf16[512,512]{0,1:T(8,128)(2,1)S(1)}, u32[]{:S(2)}, u32[]{:S(2)}) %collective-permute-start.1) | collective-permute-done | bytes 524320 | tf_op jit(solution)/shard_map/while/body/eval_jaxpr/ppermute | solution.py:24
  348.3 12.1 %collective-permute-start.2 = (bf16[512,512]{0,1:T(8,128)(2,1)}, bf16[512,512]{0,1:T(8,128)(2,1)S(1)}, u32[]{:S(2)}, u32[]{:S(2)}) collective-permute-start(bf16[512,512]{0,1:T(8,128)(2,1)} %convert_element_type.241), channel_id=1, source_target_pairs={{3,0},{0,1},{1,2},{2,3},{7,4},{4,5},{5,6},{6,7},{11,8},{8,9},{9,10... | collective-permute-start | bytes 1572872 | tf_op jit(solution)/shard_map/while/body/eval_jaxpr/ppermute | solution.py:18
  365.5 4.0 collective-permute-done.2
  370.5 10.0 %collective-permute-done.3 = bf16[512,512]{0,1:T(8,128)(2,1)} collective-permute-done((bf16[512,512]{0,1:T(8,128)(2,1)S(1)}, bf16[512,512]{0,1:T(8,128)(2,1)}, u32[]{:S(2)}, u32[]{:S(2)}) %collective-permute-start.3) | collective-permute-done | bytes 524320 | tf_op jit(solution)/shard_map/while/body/eval_jaxpr/ppermute | solution.py:18
  380.6 2.1 convert_element_type.244
  382.7 9.1 %collective-permute-done = bf16[512,512]{0,1:T(8,128)(2,1)S(1)} collective-permute-done((bf16[512,512]{0,1:T(8,128)(2,1)S(1)}, bf16[512,512]{0,1:T(8,128)(2,1)S(1)}, u32[]{:S(2)}, u32[]{:S(2)}) %collective-permute-start) | collective-permute-done | bytes 524320 | tf_op jit(solution)/shard_map/while/body/eval_jaxpr/ppermute | solution.py:24
  391.8 11.3 %collective-permute-done.1 = bf16[512,512]{0,1:T(8,128)(2,1)S(1)} collective-permute-done((bf16[512,512]{0,1:T(8,128)(2,1)}, bf16[512,512]{0,1:T(8,128)(2,1)S(1)}, u32[]{:S(2)}, u32[]{:S(2)}) %collective-permute-start.1) | collective-permute-done | bytes 524320 | tf_op jit(solution)/shard_map/while/body/eval_jaxpr/ppermute | solution.py:24
  408.6 2.1 collective-permute-start.2
  410.7 13.1 %collective-permute-start.3 = (bf16[512,512]{0,1:T(8,128)(2,1)S(1)}, bf16[512,512]{0,1:T(8,128)(2,1)}, u32[]{:S(2)}, u32[]{:S(2)}) collective-permute-start(bf16[512,512]{0,1:T(8,128)(2,1)S(1)} %convert_element_type.243), channel_id=1, source_target_pairs={{3,0},{0,1},{1,2},{2,3},{7,4},{4,5},{5,6},{6,7},{11,8},{8,9},{9,10... | collective-permute-start | bytes 1572872 | tf_op jit(solution)/shard_map/while/body/eval_jaxpr/ppermute | solution.py:18
  428.8 2.8 collective-permute-done.3
  431.6 2.1 convert_element_type.244
  433.7 9.1 %collective-permute-done = bf16[512,512]{0,1:T(8,128)(2,1)S(1)} collective-permute-done((bf16[512,512]{0,1:T(8,128)(2,1)S(1)}, bf16[512,512]{0,1:T(8,128)(2,1)S(1)}, u32[]{:S(2)}, u32[]{:S(2)}) %collective-permute-start) | collective-permute-done | bytes 524320 | tf_op jit(solution)/shard_map/while/body/eval_jaxpr/ppermute | solution.py:24
  442.8 11.3 %collective-permute-done.1 = bf16[512,512]{0,1:T(8,128)(2,1)S(1)} collective-permute-done((bf16[512,512]{0,1:T(8,128)(2,1)}, bf16[512,512]{0,1:T(8,128)(2,1)S(1)}, u32[]{:S(2)}, u32[]{:S(2)}) %collective-permute-start.1) | collective-permute-done | bytes 524320 | tf_op jit(solution)/shard_map/while/body/eval_jaxpr/ppermute | solution.py:24
  454.4 2.0 subtract_convert_fusion
  460.9 3.3 fusion.50
  469.7 13.7 %collective-permute-start.6 = (bf16[1,512]{1,0:T(2,128)(2,1)S(1)}, bf16[1,512]{1,0:T(2,128)(2,1)S(1)}, u32[]{:S(2)}, u32[]{:S(2)}) collective-permute-start(bf16[1,512]{1,0:T(2,128)(2,1)S(1)} %convert_element_type.181), channel_id=1, source_target_pairs={{0,1},{1,2},{2,3},{4,5},{5,6},{6,7},{8,9},{9,10},{10,11},{12,13},{... | collective-permute-start | bytes 3080 | tf_op jit(solution)/shard_map/ppermute | solution.py:24
  486.2 17.3 %gather_fusion = bf16[4096,512]{1,0:T(8,128)(2,1)} fusion(bf16[512,512]{1,0:T(8,128)(2,1)S(1)} %copy.38, s32[4096]{0:T(1024)S(1)} %bitcast_clamp_fusion), kind=kCustom, calls=%fused_computation | custom fusion | bytes 8404992 | tf_op jit(solution)/shard_map/jit(_take)/gather | solution.py:305
  503.5 45.0 %all-reduce.3 = (f32[512]{0:T(512)}, f32[512]{0:T(512)}) all-reduce(f32[512]{0:T(512)S(1)} %get-tuple-element.652, f32[512]{0:T(512)S(1)} %copy-done.52), channel_id=1, replica_groups=mesh['dp'=8,'blk'=4] {'dp','blk'}, use_global_device_ids=true, to_apply=%region_41.42 | all-reduce | flops 1024 | bytes 8192 | tf_op jit(solution)/shard_map/psum | solution.py:316
  548.5 7.8 %select_convert_fusion = f32[4096,512]{1,0:T(8,128)} fusion(bf16[4096,512]{1,0:T(8,128)(2,1)} %gather_fusion, pred[4096]{0:T(1024)(128)(4,1)S(1)} %copy-done.46, pred[4096]{0:T(1024)(128)(4,1)S(1)} %copy-done.38, bf16[512]{0:T(512)(128)(2,1)S(1)} %reduce.2), kind=kLoop, calls=%fused_computation.55 | loop fusion | flops 6291456 | bytes 12592128 | tf_op jit(solution)/shard_map/convert_element_type | solution.py:306
  556.4 160.1 %all-reduce.7.cloned.1.call-done = (f32[512,512]{1,0:T(8,128)}, f32[512,512]{1,0:T(8,128)}, f32[512,512]{1,0:T(8,128)}, f32[512,512]{1,0:T(8,128)}, f32[512,2048]{1,0:T(8,128)}, /*index=5*/f32[2048,512]{1,0:T(8,128)}) async-done(((f32[512,512]{1,0:T(8,128)}, f32[512,512]{1,0:T(8,128)}, f32[512,512]{1,0:T(8,128)}, f32[512,512]{1,0:T(8,128)}, f32[512,2048]{1,0:T(8,128)}, /*index=5*/f32[2048,512]{1,0:T(8,128)}), ...) | async-done | bytes 12582928 | tf_op jit(solution)/shard_map/psum | solution.py:316
  716.5 2.4 copy.81
  718.9 2.4 copy.82
  723.2 2.1 copy.85
  726.9 2.0 copy.86
  (281 shorter events, 83.2 us)
Async XLA Ops:
  7.2 181.8 %copy-start = (bf16[512,2048]{1,0:T(8,128)(2,1)S(1)}, bf16[512,2048]{1,0:T(8,128)(2,1)}, u32[]{:S(2)}) copy-start(bf16[512,2048]{1,0:T(8,128)(2,1)} %param.26) | copy-start | bytes 6291460
  7.2 10.5 %copy-start.58 = (u32[32]{0:T(128)S(1)}, u32[32]{0:T(128)}, u32[]{:S(2)}) copy-start(u32[32]{0:T(128)} %constant.316) | copy-start | bytes 388
  7.2 13.9 %copy-start.33 = (s32[4096]{0:T(1024)S(1)}, s32[4096]{0:T(1024)}, u32[]{:S(2)}) copy-start(s32[4096]{0:T(1024)} %param.19) | copy-start | bytes 49156
  7.2 13.0 %copy-start.57 = (s32[1,4]{1,0:T(1,128)S(1)}, s32[1,4]{1,0:T(1,128)}, u32[]{:S(2)}) copy-start(s32[1,4]{1,0:T(1,128)} %param.20) | copy-start | bytes 52
  7.2 77.6 %all-gather.4.cloned.1.call-start = ((), (), s32[]{:S(2)}) async-start(), calls=%async_computation | async-start | bytes 2621440 | tf_op jit(solution)/shard_map/all_gather | solution.py:158
  8.4 26.5 %copy-start.30 = (s32[32,128]{1,0:T(8,128)}, s32[32,128]{1,0:T(8,128)S(1)}, u32[]{:S(2)}) copy-start(s32[32,128]{1,0:T(8,128)S(1)} %reduce-window.28) | copy-start | bytes 49156
  8.7 8.1 %copy-start.48 = (s32[32]{0:T(128)}, s32[32]{0:T(128)S(1)}, u32[]{:S(2)}) copy-start(s32[32]{0:T(128)S(1)} %slice_reduce_fusion) | copy-start | bytes 388
  9.3 20.2 %collective-permute-start.5 = (f32[1]{0:T(128)}, f32[1]{0:T(128)}, u32[]{:S(2)}, u32[]{:S(2)}) collective-permute-start(f32[1]{0:T(128)} %bitcast.16), channel_id=1, source_target_pairs={{1,0},{2,1},{3,2},{5,4},{6,5},{7,6},{9,8},{10,9},{11,10},{13,12},{... | collective-permute-start | bytes 20 | tf_op jit(solution)/shard_map/ppermute | solution.py:24
  11.9 23.0 %copy-start.37 = (pred[4096]{0:T(1024)(128)(4,1)}, pred[4096]{0:T(1024)(128)(4,1)S(1)}, u32[]{:S(2)}) copy-start(pred[4096]{0:T(1024)(128)(4,1)S(1)} %broadcast_compare_fusion) | copy-start | bytes 12292
  14.8 15.4 %collective-permute-start.4 = (f32[1,512]{1,0:T(1,128)S(1)}, f32[1,512]{1,0:T(1,128)S(1)}, u32[]{:S(2)}, u32[]{:S(2)}) collective-permute-start(f32[1,512]{1,0:T(1,128)S(1)} %fusion.74), channel_id=1, source_target_pairs={{1,0},{2,1},{3,2},{5,4},{6,5},{7,6},{9,8},{10,9},{11,10},{13,12},{... | collective-permute-start | bytes 6152 | tf_op jit(solution)/shard_map/ppermute | solution.py:24
  20.2 14.7 %copy-start.53 = (pred[512]{0:T(512)(128)(4,1)}, pred[512]{0:T(512)(128)(4,1)S(1)}, u32[]{:S(2)}) copy-start(pred[512]{0:T(512)(128)(4,1)S(1)} %iota_compare_fusion.5) | copy-start | bytes 1540
  29.5 7.4 %copy-start.26 = (f32[512,32]{0,1:T(8,128)}, f32[512,32]{0,1:T(8,128)S(1)}, u32[]{:S(2)}) copy-start(f32[512,32]{0,1:T(8,128)S(1)} %get-tuple-element.736) | copy-start | bytes 196612
  30.2 4.8 copy-start.50
  30.2 5.0 copy-start.41
  30.2 5.1 copy-start.22
  35.4 3.6 copy-start.7
  38.9 92.8 %all-gather.6.cloned.1.call-start = ((), (), s32[]{:S(2)}) async-start(), calls=%async_computation.1 | async-start | bytes 2621440 | tf_op jit(solution)/shard_map/all_gather | solution.py:159
  41.2 8.5 %copy-start.25 = (bf16[512,8,32]{0,2,1:T(8,128)(2,1)S(1)}, bf16[512,8,32]{0,2,1:T(8,128)(2,1)}, u32[]{:S(2)}) copy-start(bf16[512,8,32]{0,2,1:T(8,128)(2,1)} %get-tuple-element.725) | copy-start | bytes 786436
  41.3 675.2 %all-reduce.7.cloned.1.call-start = ((), (), s32[]{:S(2)}) async-start(), calls=%async_computation.2 | async-start | bytes 25165824 | tf_op jit(solution)/shard_map/psum | solution.py:316
  47.6 161.1 %copy-start.43 = (f32[512]{0:T(512)}, f32[512]{0:T(512)S(1)}, u32[]{:S(2)}) copy-start(f32[512]{0:T(512)S(1)} %compare_convert_fusion) | copy-start | bytes 6148
  131.6 55.4 %copy-start.20 = (bf16[512,512]{1,0:T(8,128)(2,1)S(1)}, bf16[512,512]{1,0:T(8,128)(2,1)}, u32[]{:S(2)}) copy-start(bf16[512,512]{1,0:T(8,128)(2,1)} %param.25) | copy-start | bytes 1572868
  185.6 3.3 copy-start.34
  188.7 19.9 %copy-start.9 = (f32[512,512]{0,1:T(8,128)}, f32[512,512]{0,1:T(8,128)S(1)}, u32[]{:S(2)}) copy-start(f32[512,512]{0,1:T(8,128)S(1)} %get-tuple-element.738) | copy-start | bytes 3145732
  189.0 11.4 %copy-start.14 = (f32[512,512]{0,1:T(8,128)S(1)}, f32[512,512]{0,1:T(8,128)}, u32[]{:S(2)}) copy-start(f32[512,512]{0,1:T(8,128)} %copy.36) | copy-start | bytes 3145732
  189.0 11.4 %copy-start.55 = (bf16[2048,512]{1,0:T(8,128)(2,1)S(1)}, bf16[2048,512]{1,0:T(8,128)(2,1)}, u32[]{:S(2)}) copy-start(bf16[2048,512]{1,0:T(8,128)(2,1)} %param.27) | copy-start | bytes 6291460
  209.0 7.4 %copy-start.11 = (f32[512,512]{0,1:T(8,128)}, f32[512,512]{0,1:T(8,128)S(1)}, u32[]{:S(2)}) copy-start(f32[512,512]{0,1:T(8,128)S(1)} %multiply_add_fusion) | copy-start | bytes 3145732
  209.0 7.4 %copy-start.5 = (bf16[512,8,64]{0,2,1:T(8,128)(2,1)S(1)}, bf16[512,8,64]{0,2,1:T(8,128)(2,1)}, u32[]{:S(2)}) copy-start(bf16[512,8,64]{0,2,1:T(8,128)(2,1)} %pad_maximum_fusion) | copy-start | bytes 1572868
  209.0 7.4 %copy-start.6 = (bf16[512,512]{0,1:T(8,128)(2,1)S(1)}, bf16[512,512]{0,1:T(8,128)(2,1)}, u32[]{:S(2)}) copy-start(bf16[512,512]{0,1:T(8,128)(2,1)} %copy.37) | copy-start | bytes 1572868
  216.4 238.0 %copy-start.27 = (f32[512,32]{0,1:T(8,128)S(1)}, f32[512,32]{0,1:T(8,128)}, u32[]{:S(2)}) copy-start(f32[512,32]{0,1:T(8,128)} %copy-done.26) | copy-start | bytes 196612
  216.4 238.0 %copy-start.32 = (f32[512,32]{0,1:T(8,128)S(1)}, f32[512,32]{0,1:T(8,128)}, u32[]{:S(2)}) copy-start(f32[512,32]{0,1:T(8,128)} %get-tuple-element.734) | copy-start | bytes 196612
  232.0 14.0 %collective-permute-start.2 = (bf16[512,512]{0,1:T(8,128)(2,1)}, bf16[512,512]{0,1:T(8,128)(2,1)S(1)}, u32[]{:S(2)}, u32[]{:S(2)}) collective-permute-start(bf16[512,512]{0,1:T(8,128)(2,1)} %convert_element_type.241), channel_id=1, source_target_pairs={{3,0},{0,1},{1,2},{2,3},{7,4},{4,5},{5,6},{6,7},{11,8},{8,9},{9,10... | collective-permute-start | bytes 1572872 | tf_op jit(solution)/shard_map/while/body/eval_jaxpr/ppermute | solution.py:18
  233.8 23.5 %collective-permute-start.3 = (bf16[512,512]{0,1:T(8,128)(2,1)S(1)}, bf16[512,512]{0,1:T(8,128)(2,1)}, u32[]{:S(2)}, u32[]{:S(2)}) collective-permute-start(bf16[512,512]{0,1:T(8,128)(2,1)S(1)} %convert_element_type.243), channel_id=1, source_target_pairs={{3,0},{0,1},{1,2},{2,3},{7,4},{4,5},{5,6},{6,7},{11,8},{8,9},{9,10... | collective-permute-start | bytes 1572872 | tf_op jit(solution)/shard_map/while/body/eval_jaxpr/ppermute | solution.py:18
  234.5 34.0 %collective-permute-start = (bf16[512,512]{0,1:T(8,128)(2,1)S(1)}, bf16[512,512]{0,1:T(8,128)(2,1)S(1)}, u32[]{:S(2)}, u32[]{:S(2)}) collective-permute-start(bf16[512,512]{0,1:T(8,128)(2,1)S(1)} %copy.64), channel_id=1, source_target_pairs={{0,1},{1,2},{2,3},{4,5},{5,6},{6,7},{8,9},{9,10},{10,11},{12,13},{... | collective-permute-start | bytes 1572872 | tf_op jit(solution)/shard_map/while/body/eval_jaxpr/ppermute | solution.py:24
  238.5 41.2 %collective-permute-start.1 = (bf16[512,512]{0,1:T(8,128)(2,1)}, bf16[512,512]{0,1:T(8,128)(2,1)S(1)}, u32[]{:S(2)}, u32[]{:S(2)}) collective-permute-start(bf16[512,512]{0,1:T(8,128)(2,1)} %copy.65), channel_id=1, source_target_pairs={{0,1},{1,2},{2,3},{4,5},{5,6},{6,7},{8,9},{9,10},{10,11},{12,13},{... | collective-permute-start | bytes 1572872 | tf_op jit(solution)/shard_map/while/body/eval_jaxpr/ppermute | solution.py:24
  296.8 12.4 %collective-permute-start.2 = (bf16[512,512]{0,1:T(8,128)(2,1)}, bf16[512,512]{0,1:T(8,128)(2,1)S(1)}, u32[]{:S(2)}, u32[]{:S(2)}) collective-permute-start(bf16[512,512]{0,1:T(8,128)(2,1)} %convert_element_type.241), channel_id=1, source_target_pairs={{3,0},{0,1},{1,2},{2,3},{7,4},{4,5},{5,6},{6,7},{11,8},{8,9},{9,10... | collective-permute-start | bytes 1572872 | tf_op jit(solution)/shard_map/while/body/eval_jaxpr/ppermute | solution.py:18
  297.6 22.9 %collective-permute-start.3 = (bf16[512,512]{0,1:T(8,128)(2,1)S(1)}, bf16[512,512]{0,1:T(8,128)(2,1)}, u32[]{:S(2)}, u32[]{:S(2)}) collective-permute-start(bf16[512,512]{0,1:T(8,128)(2,1)S(1)} %convert_element_type.243), channel_id=1, source_target_pairs={{3,0},{0,1},{1,2},{2,3},{7,4},{4,5},{5,6},{6,7},{11,8},{8,9},{9,10... | collective-permute-start | bytes 1572872 | tf_op jit(solution)/shard_map/while/body/eval_jaxpr/ppermute | solution.py:18
  298.5 33.1 %collective-permute-start = (bf16[512,512]{0,1:T(8,128)(2,1)S(1)}, bf16[512,512]{0,1:T(8,128)(2,1)S(1)}, u32[]{:S(2)}, u32[]{:S(2)}) collective-permute-start(bf16[512,512]{0,1:T(8,128)(2,1)S(1)} %copy.64), channel_id=1, source_target_pairs={{0,1},{1,2},{2,3},{4,5},{5,6},{6,7},{8,9},{9,10},{10,11},{12,13},{... | collective-permute-start | bytes 1572872 | tf_op jit(solution)/shard_map/while/body/eval_jaxpr/ppermute | solution.py:24
  300.4 42.4 %collective-permute-start.1 = (bf16[512,512]{0,1:T(8,128)(2,1)}, bf16[512,512]{0,1:T(8,128)(2,1)S(1)}, u32[]{:S(2)}, u32[]{:S(2)}) collective-permute-start(bf16[512,512]{0,1:T(8,128)(2,1)} %copy.65), channel_id=1, source_target_pairs={{0,1},{1,2},{2,3},{4,5},{5,6},{6,7},{8,9},{9,10},{10,11},{12,13},{... | collective-permute-start | bytes 1572872 | tf_op jit(solution)/shard_map/while/body/eval_jaxpr/ppermute | solution.py:24
  348.3 21.2 %collective-permute-start.2 = (bf16[512,512]{0,1:T(8,128)(2,1)}, bf16[512,512]{0,1:T(8,128)(2,1)S(1)}, u32[]{:S(2)}, u32[]{:S(2)}) collective-permute-start(bf16[512,512]{0,1:T(8,128)(2,1)} %convert_element_type.241), channel_id=1, source_target_pairs={{3,0},{0,1},{1,2},{2,3},{7,4},{4,5},{5,6},{6,7},{11,8},{8,9},{9,10... | collective-permute-start | bytes 1572872 | tf_op jit(solution)/shard_map/while/body/eval_jaxpr/ppermute | solution.py:18
  360.5 20.1 %collective-permute-start.3 = (bf16[512,512]{0,1:T(8,128)(2,1)S(1)}, bf16[512,512]{0,1:T(8,128)(2,1)}, u32[]{:S(2)}, u32[]{:S(2)}) collective-permute-start(bf16[512,512]{0,1:T(8,128)(2,1)S(1)} %convert_element_type.243), channel_id=1, source_target_pairs={{3,0},{0,1},{1,2},{2,3},{7,4},{4,5},{5,6},{6,7},{11,8},{8,9},{9,10... | collective-permute-start | bytes 1572872 | tf_op jit(solution)/shard_map/while/body/eval_jaxpr/ppermute | solution.py:18
  361.6 30.2 %collective-permute-start = (bf16[512,512]{0,1:T(8,128)(2,1)S(1)}, bf16[512,512]{0,1:T(8,128)(2,1)S(1)}, u32[]{:S(2)}, u32[]{:S(2)}) collective-permute-start(bf16[512,512]{0,1:T(8,128)(2,1)S(1)} %copy.64), channel_id=1, source_target_pairs={{0,1},{1,2},{2,3},{4,5},{5,6},{6,7},{8,9},{9,10},{10,11},{12,13},{... | collective-permute-start | bytes 1572872 | tf_op jit(solution)/shard_map/while/body/eval_jaxpr/ppermute | solution.py:24
  363.5 39.6 %collective-permute-start.1 = (bf16[512,512]{0,1:T(8,128)(2,1)}, bf16[512,512]{0,1:T(8,128)(2,1)S(1)}, u32[]{:S(2)}, u32[]{:S(2)}) collective-permute-start(bf16[512,512]{0,1:T(8,128)(2,1)} %copy.65), channel_id=1, source_target_pairs={{0,1},{1,2},{2,3},{4,5},{5,6},{6,7},{8,9},{9,10},{10,11},{12,13},{... | collective-permute-start | bytes 1572872 | tf_op jit(solution)/shard_map/while/body/eval_jaxpr/ppermute | solution.py:24
  408.6 19.1 %collective-permute-start.2 = (bf16[512,512]{0,1:T(8,128)(2,1)}, bf16[512,512]{0,1:T(8,128)(2,1)S(1)}, u32[]{:S(2)}, u32[]{:S(2)}) collective-permute-start(bf16[512,512]{0,1:T(8,128)(2,1)} %convert_element_type.241), channel_id=1, source_target_pairs={{3,0},{0,1},{1,2},{2,3},{7,4},{4,5},{5,6},{6,7},{11,8},{8,9},{9,10... | collective-permute-start | bytes 1572872 | tf_op jit(solution)/shard_map/while/body/eval_jaxpr/ppermute | solution.py:18
  410.7 20.9 %collective-permute-start.3 = (bf16[512,512]{0,1:T(8,128)(2,1)S(1)}, bf16[512,512]{0,1:T(8,128)(2,1)}, u32[]{:S(2)}, u32[]{:S(2)}) collective-permute-start(bf16[512,512]{0,1:T(8,128)(2,1)S(1)} %convert_element_type.243), channel_id=1, source_target_pairs={{3,0},{0,1},{1,2},{2,3},{7,4},{4,5},{5,6},{6,7},{11,8},{8,9},{9,10... | collective-permute-start | bytes 1572872 | tf_op jit(solution)/shard_map/while/body/eval_jaxpr/ppermute | solution.py:18
  423.8 19.0 %collective-permute-start = (bf16[512,512]{0,1:T(8,128)(2,1)S(1)}, bf16[512,512]{0,1:T(8,128)(2,1)S(1)}, u32[]{:S(2)}, u32[]{:S(2)}) collective-permute-start(bf16[512,512]{0,1:T(8,128)(2,1)S(1)} %copy.64), channel_id=1, source_target_pairs={{0,1},{1,2},{2,3},{4,5},{5,6},{6,7},{8,9},{9,10},{10,11},{12,13},{... | collective-permute-start | bytes 1572872 | tf_op jit(solution)/shard_map/while/body/eval_jaxpr/ppermute | solution.py:24
  425.7 28.4 %collective-permute-start.1 = (bf16[512,512]{0,1:T(8,128)(2,1)}, bf16[512,512]{0,1:T(8,128)(2,1)S(1)}, u32[]{:S(2)}, u32[]{:S(2)}) collective-permute-start(bf16[512,512]{0,1:T(8,128)(2,1)} %copy.65), channel_id=1, source_target_pairs={{0,1},{1,2},{2,3},{4,5},{5,6},{6,7},{8,9},{9,10},{10,11},{12,13},{... | collective-permute-start | bytes 1572872 | tf_op jit(solution)/shard_map/while/body/eval_jaxpr/ppermute | solution.py:24
  454.4 5.0 copy-start.2
  456.4 4.5 copy-start.15
  456.4 4.5 copy-start.18
  456.5 4.5 copy-start.44
  464.9 3.3 copy-start.40
  464.9 3.3 copy-start.42
  468.2 15.1 %copy-start.10 = (f32[512,512]{0,1:T(8,128)S(1)}, f32[512,512]{0,1:T(8,128)}, u32[]{:S(2)}) copy-start(f32[512,512]{0,1:T(8,128)} %copy-done.9) | copy-start | bytes 3145732
  468.2 15.1 %copy-start.19 = (bf16[512,2048]{1,0:T(8,128)(2,1)S(1)}, bf16[512,2048]{1,0:T(8,128)(2,1)}, u32[]{:S(2)}) copy-start(bf16[512,2048]{1,0:T(8,128)(2,1)} %get-tuple-element.706) | copy-start | bytes 6291460
  468.2 15.1 %copy-start.56 = (bf16[2048,512]{1,0:T(8,128)(2,1)S(1)}, bf16[2048,512]{1,0:T(8,128)(2,1)}, u32[]{:S(2)}) copy-start(bf16[2048,512]{1,0:T(8,128)(2,1)} %param.27) | copy-start | bytes 6291460
  469.7 78.8 %collective-permute-start.6 = (bf16[1,512]{1,0:T(2,128)(2,1)S(1)}, bf16[1,512]{1,0:T(2,128)(2,1)S(1)}, u32[]{:S(2)}, u32[]{:S(2)}) collective-permute-start(bf16[1,512]{1,0:T(2,128)(2,1)S(1)} %convert_element_type.181), channel_id=1, source_target_pairs={{0,1},{1,2},{2,3},{4,5},{5,6},{6,7},{8,9},{9,10},{10,11},{12,13},{... | collective-permute-start | bytes 3080 | tf_op jit(solution)/shard_map/ppermute | solution.py:24
  486.2 17.3 %copy-start.52 = (f32[512]{0:T(512)S(1)}, f32[512]{0:T(512)}, u32[]{:S(2)}) copy-start(f32[512]{0:T(512)} %get-tuple-element.650) | copy-start | bytes 6148
  486.2 62.3 %copy-start.38 = (pred[4096]{0:T(1024)(128)(4,1)S(1)}, pred[4096]{0:T(1024)(128)(4,1)}, u32[]{:S(2)}) copy-start(pred[4096]{0:T(1024)(128)(4,1)} %copy-done.37) | copy-start | bytes 12292
  486.2 62.3 %copy-start.46 = (pred[4096]{0:T(1024)(128)(4,1)S(1)}, pred[4096]{0:T(1024)(128)(4,1)}, u32[]{:S(2)}) copy-start(pred[4096]{0:T(1024)(128)(4,1)} %get-tuple-element.704) | copy-start | bytes 12292
  716.5 4.8 copy-start.24
  716.5 5.8 copy-start.23
  716.5 6.7 copy-start.17
  723.2 3.7 copy-start.16
  723.2 5.7 copy-start.1
  (21 other events, 37.8 us)
Sparse Core Ops, SparseCore 0:
  39.0 45.7 all-gather.3
  87.0 44.6 all-gather.5
  464.4 252.0 all-reduce.6
where the time goes:
time: 746 us; the launch traced here: 736 us
  waiting for transfers between devices  371 us (50%)
  matrix products  104 us (14%)
  starting transfers between devices  69.8 us (9%)
  other arithmetic  69.7 us (9%)
  blocking collectives  51.7 us (7%)
  local copies, waits for them, and re-layouts  48.9 us (7%)
  between operations  17 us (2%)
    psum x1, waiting for transfers between devices, local(): lax.psum((grad_w_query, grad_w_key, grad_w_value, grad_w_out, grad_w_up,...  160 us
    ppermute x11, waiting for transfers between devices, from_behind(): return lax.ppermute(value, axis, pairs)  81.3 us
    ppermute x8, waiting for transfers between devices, passed_along(): return lax.ppermute(block, axis, route)  47.4 us
    all_gather x1, waiting for transfers between devices, local(): value_piece = lax.all_gather(value_low, 'blk', axis=0, tiled=True)  46.8 us
    psum x1, blocking collectives, local(): lax.psum((grad_w_query, grad_w_key, grad_w_value, grad_w_out, grad_w_up,...  45 us
    ppermute x11, starting transfers between devices, from_behind(): return lax.ppermute(value, axis, pairs)  37.2 us
    all_gather x1, waiting for transfers between devices, local(): key_piece = lax.all_gather(key_rot, 'blk', axis=0, tiled=True)  35.1 us
    ppermute x8, starting transfers between devices, passed_along(): return lax.ppermute(block, axis, route)  32.4 us
  transfers between devices with their start and end apart: 22, of which 18 were waited for; matrix products, arithmetic and copies ran while one was open for 9% of the time, Pallas kernels for 0%

commit v1 on v0

--- a/solution.py
+++ b/solution.py
@@ -1,15 +1,1199 @@
+import functools
+import math
+
 import jax
 import jax.numpy as jnp
+import numpy as np
 from jax import lax
+from jax.experimental import pallas as pl
+from jax.experimental.pallas import tpu as pltpu
 from jax.sharding import PartitionSpec as P
 
 HEADS = 8
 HEAD_DIM = 64
-
-
 EPSILON = 1e-05
 ROTARY_BASE = 10000.0
 NEGATIVE = -1e30
+LOG2E = math.log2(math.e)
+
+MESH = pl.DeviceIdType.MESH
+F32 = jnp.float32
+BF16 = jnp.bfloat16
+NN = (((1,), (0,)), ((), ()))
+NT = (((1,), (1,)), ((), ()))
+TN = (((0,), (0,)), ((), ()))
+
+
+def mm(a, b, dims):
+    return lax.dot_general(a, b, dims, preferred_element_type=F32)
+
+
+def iota(shape, dim):
+    return lax.broadcasted_iota(jnp.int32, shape, dim)
+
+
+class Copy:
+    def __init__(self, src, dst, send_sem, recv_sem, device, cond=None):
+        self.parts = (src, dst, send_sem, recv_sem)
+        self.device = device
+        self.cond = cond
+
+    def _do(self, act):
+        def run():
+            src, dst, send_sem, recv_sem = self.parts
+            act(
+                pltpu.make_async_remote_copy(
+                    src_ref=src,
+                    dst_ref=dst,
+                    send_sem=send_sem,
+                    recv_sem=recv_sem,
+                    device_id=self.device,
+                    device_id_type=MESH,
+                )
+            )
+
+        if self.cond is None:
+            run()
+        else:
+            pl.when(self.cond)(run)
+
+    def start(self):
+        self._do(lambda d: d.start())
+
+    def wait_send(self):
+        self._do(lambda d: d.wait_send())
+
+    def wait_recv(self):
+        self._do(lambda d: d.wait_recv())
+
+
+CHUNKS = ((0, 4), (4, 9), (9, 12))
+SEMS_AR = 22
+
+
+def layer_kernel(
+    bytes_hbm,
+    flags_ref,
+    lengths_ref,
+    cot_hbm,
+    wq_hbm,
+    wk_hbm,
+    wv_hbm,
+    wo_hbm,
+    wup_hbm,
+    wdn_hbm,
+    gains_ref,
+    freq_ref,
+    out_ref,
+    gs_ref,
+    came_ref,
+    slots_ref,
+    wgrad_hbm,
+    ggain_ref,
+    bytes_v,
+    weights,
+    wup,
+    wdn,
+    meta,
+    tail,
+    slot_sc,
+    p_own,
+    relay,
+    p_all,
+    n1,
+    k_t,
+    v_t,
+    q_t,
+    tab_c,
+    tab_s,
+    pos,
+    gcol,
+    cot_own,
+    cot_w,
+    o_acc,
+    m_sc,
+    l_sc,
+    att,
+    gb,
+    hat2,
+    d_o,
+    d_sc,
+    gmid,
+    dk,
+    dv,
+    dq,
+    gwqkv,
+    big,
+    wg,
+    r1,
+    r2,
+    r3,
+    r4,
+    ppart,
+    rc,
+    rz,
+    gfin,
+    out_s,
+    out_r,
+    rdiv,
+    last_s,
+    last_r,
+    gain_acc,
+    gain_s,
+    gain_r,
+    ss,
+    rs,
+    ls,
+):
+    cot_v, acc = hat2, big.at[0]
+    dp = lax.axis_index("dp")
+    z = lax.axis_index("blk")
+    feat = 512
+    half = 256
+    nblk = 4
+    c = lax.rem(dp, 2)
+    x = lax.rem(lax.div(dp, 2), 2)
+    y = lax.div(dp, 4)
+    sib = (dp + 1 - 2 * c, z)
+    xnb = (dp + 2 - 4 * x, z)
+    ynb = (dp + 4 - 8 * y, z)
+    g = lax.div(z, 2)
+    zl = lax.rem(z, 2)
+    w = 2 * zl + c
+    zo = 4 * g + 1 - z
+    near = 1 + g
+    is_near = z == near
+    own_worker = g == c
+
+    def dev(core, zz):
+        return (dp - c + core, zz)
+
+    counter = {"s": 0, "r": 0, "l": 0}
+
+    def ids(kind, n):
+        first = counter[kind]
+        counter[kind] = first + n
+        return first
+
+    sends = []
+
+    def go(copy):
+        copy.start()
+        sends.append(copy)
+
+    l_bytes = ids("l", 8)
+    rows_chunk = bytes_v.shape[1]
+    loads_bytes = [
+        pltpu.make_async_copy(
+            bytes_hbm.at[pl.ds(i * rows_chunk, rows_chunk)], bytes_v.at[i], ls.at[l_bytes + i]
+        )
+        for i in range(8)
+    ]
+    for d in loads_bytes:
+        d.start()
+    l_cot = ids("l", 1)
+    load_cot = pltpu.make_async_copy(cot_hbm, cot_v, ls.at[l_cot])
+    load_cot.start()
+    l_w = ids("l", 4)
+    loads_w = [
+        pltpu.make_async_copy(src, weights.at[i], ls.at[l_w + i])
+        for i, src in enumerate((wq_hbm, wk_hbm, wv_hbm, wo_hbm))
+    ]
+    for d in loads_w:
+        d.start()
+    l_f = ids("l", 8)
+    loads_f = []
+    for j in range(4):
+        loads_f.append(
+            pltpu.make_async_copy(
+                wup_hbm.at[:, pl.ds(j * feat, feat)], wup.at[j], ls.at[l_f + 2 * j]
+            )
+        )
+        loads_f.append(
+            pltpu.make_async_copy(
+                wdn_hbm.at[pl.ds(j * feat, feat)], wdn.at[j], ls.at[l_f + 2 * j + 1]
+            )
+        )
+    for d in loads_f:
+        d.start()
+
+    barrier = pltpu.get_barrier_semaphore()
+    me_line = c * nblk + z
+    line = []
+    for k in range(1, 8):
+        t = lax.rem(me_line + k, 8)
+        line.append((lax.div(t, nblk), lax.rem(t, nblk)))
+    for core, zz in line:
+        pl.semaphore_signal(barrier, inc=1, device_id=dev(core, zz), device_id_type=MESH)
+    for d in (xnb, ynb):
+        pl.semaphore_signal(barrier, inc=1, device_id=d, device_id_type=MESH)
+    pl.semaphore_wait(barrier, 9)
+
+    meta[c, z, 0:32, :] = flags_ref[...]
+    meta[c, z, 32:40, :] = lengths_ref[...]
+    s_meta, r_meta = ids("s", 7), ids("r", 8)
+    for k, (core, zz) in enumerate(line):
+        go(
+            Copy(
+                meta.at[c, z],
+                meta.at[c, z],
+                ss.at[s_meta + k],
+                rs.at[r_meta + me_line],
+                dev(core, zz),
+            )
+        )
+    s_tail, r_tail = ids("s", 1), ids("r", 1)
+    copy_tail = Copy(
+        bytes_hbm.at[pl.ds(0, 16)],
+        tail,
+        ss.at[s_tail],
+        rs.at[r_tail],
+        (dp, lax.rem(z + nblk - 1, nblk)),
+        z > 0,
+    )
+    go(copy_tail)
+
+    @pl.when(z == nblk - 1)
+    def _():
+        tail[...] = jnp.zeros_like(tail)
+
+    upper = (iota((128, 128), 0) <= iota((128, 128), 1)).astype(F32).astype(BF16)
+    ones_sq = jnp.ones((128, 128), BF16)
+    below = (iota((32, 32), 1) < iota((32, 32), 0)).astype(F32).astype(BF16)
+    own_flags = flags_ref[...].astype(F32)
+    flags_low = own_flags.astype(BF16)
+    within = mm(flags_low, upper, NN)
+    row_sums = mm(flags_low, ones_sq, NN)
+    row_base = mm(below, row_sums.astype(BF16), NN)
+    slot_of = within + row_base - 1.0
+    for k in range(8):
+        slot_sc[k] = slot_of[4 * k : 4 * k + 4, :]
+    slots_ref[...] = slot_of
+    cnt = jnp.sum(own_flags)
+
+    acc[...] = jnp.zeros_like(acc)
+    rdiv[...] = jnp.zeros_like(rdiv)
+    slot_iota = iota((feat, 128), 0).astype(F32)
+    ones_rows = jnp.ones((16, feat), BF16)
+
+    def pool(k, carry):
+        pltpu.make_async_copy(
+            bytes_hbm.at[pl.ds(0, rows_chunk)], bytes_v.at[k], ls.at[l_bytes + k]
+        ).wait()
+        rows = slot_sc[k]
+        member = jnp.concatenate(
+            [
+                (slot_iota == rows[r : r + 1, :]).astype(F32).astype(BF16)
+                for r in range(4)
+            ],
+            axis=1,
+        )
+        acc[...] += mm(member, bytes_v[k], NN)
+        rdiv[...] += mm(ones_rows, member, NT)
+        return carry
+
+    lax.fori_loop(0, 8, pool, 0)
+
+    for i in range(2):
+        row = jnp.broadcast_to(gains_ref[i : i + 1, :], (128, feat))
+        col = row.T
+        gcol[i] = jnp.concatenate([col, col], axis=1)
+
+    for core, zz in line:
+        Copy(
+            meta.at[core, zz],
+            meta.at[core, zz],
+            ss.at[0],
+            rs.at[r_meta + core * nblk + zz],
+            sib,
+        ).wait_recv()
+    Copy(tail, tail, ss.at[0], rs.at[r_tail], sib, z < nblk - 1).wait_recv()
+    zn = jnp.minimum(z + 1, nblk - 1)
+    next_flags = meta[c, zn, 0:16, :].astype(F32).astype(BF16)
+    next_within = mm(next_flags, upper, NN)
+    has_next = (z < nblk - 1).astype(F32)
+    lead = jnp.where(next_within[0:1, :] < 0.5, 1.0, 0.0) * has_next
+    is_last16 = iota((feat, 16), 0).astype(F32) == cnt - 1.0
+    member_tail = jnp.where(is_last16, lead[:, 0:16], 0.0).astype(BF16)
+    sums = acc[...] + mm(member_tail, tail[...], NN)
+    lane_row = iota((1, feat), 1).astype(F32)
+    tally = rdiv[0:1, :] + jnp.where(lane_row == cnt - 1.0, jnp.sum(lead), 0.0)
+    inverse_tally = 1.0 / jnp.maximum(tally, 1.0)
+    rdiv[0:1, :] = inverse_tally
+    live_row = jnp.where(lane_row < cnt, 1.0, 0.0)
+    rdiv[1:2, :] = live_row
+    pooled_t = (sums.T * inverse_tally).astype(BF16)
+    p_own[0] = pooled_t[:, 0:half]
+    p_own[1] = pooled_t[:, half:]
+
+    s_p, r_p, r_relay = ids("s", 9), ids("r", 8), ids("r", 1)
+    near_c = 1 + c
+
+    def p_copy(src, hb, slot, device, cond=None):
+        return Copy(src, p_all.at[hb], ss.at[s_p + slot], rs.at[r_p + hb], device, cond)
+
+    other_worker = jnp.logical_not(own_worker)
+    go(p_copy(p_own.at[c], 2 * z + c, 0, dev(c, zo), own_worker))
+    go(p_copy(p_own.at[1 - c], 2 * z + 1 - c, 1, sib, own_worker))
+    go(p_copy(p_own.at[c], 2 * z + c, 2, sib, own_worker))
+    go(
+        Copy(p_own.at[1 - c], relay, ss.at[s_p + 1], rs.at[r_relay], sib, other_worker)
+    )
+    go(p_copy(p_own.at[c], 2 * z + c, 2, dev(c, near_c), other_worker))
+
+    @pl.when(own_worker)
+    def _():
+        p_all[2 * z] = p_own[0]
+        p_all[2 * z + 1] = p_own[1]
+
+    Copy(relay, relay, ss.at[0], rs.at[r_relay], sib, own_worker).wait_recv()
+    go(p_copy(relay, 2 * z + c, 3, dev(c, 2 - c), own_worker))
+
+    def p_wait(hb, cond=None):
+        Copy(p_all.at[hb], p_all.at[hb], ss.at[0], rs.at[r_p + hb], sib, cond).wait_recv()
+
+    p_wait(2 * z + c, other_worker)
+    go(p_copy(p_all.at[2 * z + c], 2 * z + c, 0, dev(c, zo), other_worker))
+    p_wait(2 * z + 1 - c, other_worker)
+
+    load_cot.wait()
+    cot_t = (cot_v[...].T * live_row).astype(BF16)
+    cot_own[0] = cot_t[:, 0:half]
+    cot_own[1] = cot_t[:, half:]
+    s_cot, r_cot = ids("s", 2), ids("r", 2)
+    early = z < 2
+    slot_to = jnp.where(early, 0, 1)
+    chip_to = 2 * c + jnp.where(early, z, 3 - z)
+    for i in range(2):
+        core_to = jnp.where(early, i, 1 - i)
+        here = jnp.logical_and(core_to == c, chip_to == z)
+        go(
+            Copy(
+                cot_own.at[i],
+                cot_w.at[slot_to],
+                ss.at[s_cot + i],
+                rs.at[r_cot + slot_to],
+                dev(core_to, chip_to),
+                jnp.logical_not(here),
+            )
+        )
+
+        @pl.when(here)
+        def _():
+            cot_w[slot_to] = cot_own[i]
+
+    lo_here = jnp.logical_and(g == c, zl == z)
+    hi_here = jnp.logical_and(g == c, 3 - zl == z)
+
+    counts = []
+    for b in range(nblk):
+        counts.append(jnp.sum(meta[g, b, 0:32, :].astype(F32)))
+    offsets = [jnp.float32(0.0)]
+    for b in range(nblk):
+        offsets.append(offsets[-1] + counts[b])
+    lens = meta[g, z, 32:40, :].astype(F32)
+    first_row = iota((8, 128), 0) == 0
+    lane8 = iota((8, 128), 1)
+    byte_at = (iota((32, 128), 0) * 128 + iota((32, 128), 1)).astype(F32)
+    seq_first = [jnp.float32(0.0)]
+    for s in range(1, 4):
+        start = jnp.sum(jnp.where(jnp.logical_and(first_row, lane8 < s), lens, 0.0))
+        prior = jnp.zeros((32, 128), F32)
+        for b in range(nblk):
+            prior = prior + jnp.where(
+                byte_at + float(b * 4096) < start, meta[g, b, 0:32, :].astype(F32), 0.0
+            )
+        seq_first.append(jnp.sum(prior))
+
+    freq = jnp.concatenate([freq_ref[...], freq_ref[...]], axis=1)
+    lane_half = iota((1, half), 1).astype(F32)
+    for hb in range(8):
+        b = hb // 2
+        j = lane_half + float((hb % 2) * half)
+        p = offsets[b] + jnp.minimum(j, counts[b] - 1.0)
+        first = jnp.zeros_like(p)
+        for s in range(1, 4):
+            first = jnp.maximum(first, jnp.where(p >= seq_first[s], seq_first[s], 0.0))
+        pos[hb, 0:1, :] = p
+        pos[hb, 1:2, :] = first
+        angle = freq * p
+        tab_c[hb] = jnp.cos(angle)
+        tab_s[hb] = jnp.sin(angle)
+
+    def pick(values, b):
+        total = jnp.float32(0.0)
+        for i, v in enumerate(values):
+            total = total + jnp.where(b == i, v, 0.0)
+        return total
+
+    gain_col = gcol[0]
+
+    def norm_parts(values):
+        mean = jnp.mean(values, axis=0, keepdims=True)
+        center = values - mean
+        inverse = lax.rsqrt(jnp.mean(center * center, axis=0, keepdims=True) + EPSILON)
+        return center * inverse, inverse
+
+    def turned(values, hb, direction):
+        cos = tab_c[hb]
+        sin = tab_s[hb] * direction
+        parts = []
+        for h in range(HEADS):
+            a = values[64 * h : 64 * h + 32, :]
+            b = values[64 * h + 32 : 64 * h + 64, :]
+            parts.append(a * cos - b * sin)
+            parts.append(b * cos + a * sin)
+        return jnp.concatenate(parts, axis=0).astype(BF16)
+
+    for d in loads_w:
+        d.wait()
+
+    def keys_values(hb):
+        unit, _ = norm_parts(p_all[hb].astype(F32))
+        normed = (unit * gcol[0]).astype(BF16)
+        n1[hb] = normed
+        k_t[hb] = turned(mm(weights[1], normed, TN), hb, 1.0)
+        v_t[hb] = mm(weights[2], normed, TN).astype(BF16)
+
+    def both_halves(block):
+        def one(i, carry):
+            keys_values(2 * block + i)
+            return carry
+
+        lax.fori_loop(0, 2, one, 0)
+
+    both_halves(z)
+    for n, block in enumerate((zo, 2 - g, 3 - 3 * g)):
+        p_wait(2 * block + c)
+        if n > 0:
+            go(p_copy(p_all.at[2 * block + c], 2 * block + c, 6 + n, dev(c, zo), is_near))
+        go(p_copy(p_all.at[2 * block + c], 2 * block + c, 4 + n, sib))
+        p_wait(2 * block + 1 - c)
+        both_halves(block)
+
+    hq_of = (w, 7 - w)
+
+    def hq_at(slot):
+        return jnp.where(slot == 0, w, 7 - w)
+
+    for slot in range(2):
+        q_t[slot] = turned(mm(weights[0], n1[hq_of[slot]], TN), hq_of[slot], 1.0)
+    score_scale = HEAD_DIM ** (-0.5) * LOG2E
+
+    def bias_of(hq, kb):
+        b = lax.div(kb, 2)
+        j = (iota((half, half), 0) + lax.rem(kb, 2) * half).astype(F32)
+        kpos = j + pick(offsets[:nblk], b)
+        alive = j < pick(counts, b)
+        qpos = pos[hq, 0:1, :]
+        qfirst = pos[hq, 1:2, :]
+        allowed = jnp.logical_and(alive, jnp.logical_and(kpos <= qpos, kpos >= qfirst))
+        return jnp.where(allowed, 0.0, NEGATIVE)
+
+    o_acc[...] = jnp.zeros_like(o_acc)
+    l_sc[...] = jnp.zeros_like(l_sc)
+    m_sc[...] = jnp.full(m_sc.shape, NEGATIVE, F32)
+
+    def forward_step(t, carry):
+        low_half = t <= w
+        slot = jnp.where(low_half, 0, 1)
+        kb = jnp.where(low_half, t, t - w - 1)
+        hq = hq_at(slot)
+        bias = bias_of(hq, kb)
+        for h in range(HEADS):
+            part = slice(64 * h, 64 * h + 64)
+            s = mm(k_t[kb, part, :], q_t[slot, part, :], TN) * score_scale + bias
+            old = m_sc[slot, h : h + 1, :]
+            new = jnp.maximum(old, jnp.max(s, axis=0, keepdims=True))
+            prob = jnp.exp2(s - new)
+            shrink = jnp.exp2(old - new)
+            l_sc[slot, h : h + 1, :] = l_sc[slot, h : h + 1, :] * shrink + jnp.sum(
+                prob, axis=0, keepdims=True
+            )
+            m_sc[slot, h : h + 1, :] = new
+            o_acc[slot, part, :] = o_acc[slot, part, :] * shrink + mm(
+                v_t[kb, part, :], prob.astype(BF16), NN
+            )
+        return carry
+
+    lax.fori_loop(0, 9, forward_step, 0)
+
+    for slot in range(2):
+        total = l_sc[slot]
+        for h in range(HEADS):
+            part = slice(64 * h, 64 * h + 64)
+            o_acc[slot, part, :] = o_acc[slot, part, :] * (1.0 / total[h : h + 1, :])
+        att[:, slot * half : (slot + 1) * half] = o_acc[slot].astype(BF16)
+        m_sc[slot] = m_sc[slot] + jnp.log2(total)
+
+    own_pooled = jnp.concatenate([p_all[hq_of[0]], p_all[hq_of[1]]], axis=1).astype(F32)
+    middle = own_pooled + mm(weights[3], att[...], TN)
+    unit2, inverse2 = norm_parts(middle)
+    hat2[...] = unit2
+    gain_col2 = jnp.concatenate([gcol[1], gcol[1]], axis=1)
+    n2 = (unit2 * gain_col2).astype(BF16)
+    big[0] = middle
+    big[1] = jnp.zeros((feat, feat), F32)
+    Copy(cot_w.at[0], cot_w.at[0], ss.at[0], rs.at[r_cot], sib, jnp.logical_not(lo_here)).wait_recv()
+    Copy(cot_w.at[1], cot_w.at[1], ss.at[0], rs.at[r_cot + 1], sib, jnp.logical_not(hi_here)).wait_recv()
+    gb[...] = jnp.concatenate([cot_w[0], cot_w[1]], axis=1)
+    n2_ref = d_o
+    n2_ref[...] = n2
+
+    base1 = c * 256
+    keep2x, give2x = base1 + x * 128, base1 + (1 - x) * 128
+    keep2y, give2y = base1 + y * 128, base1 + (1 - y) * 128
+    keep3x, give3x = keep2x + y * 64, keep2x + (1 - y) * 64
+    keep3y, give3y = keep2y + x * 64, keep2y + (1 - x) * 64
+    lanes_x, lanes_y = pl.ds(0, 256), pl.ds(256, 256)
+
+    def rows_of(first, n):
+        return pl.ds(pl.multiple_of(first, 16), n)
+
+    class Reduce:
+        def __init__(self, chunk):
+            self.b0, self.b1 = CHUNKS[chunk]
+            self.nb = self.b1 - self.b0
+            self.s0, self.r0 = ids("s", SEMS_AR), ids("r", SEMS_AR)
+            self.blocks = pl.ds(self.b0, self.nb)
+            self.phases = {}
+
+        def _w(self, first, n, lanes):
+            return wg.at[self.blocks, rows_of(first, n), lanes]
+
+        def _list(self, phase):
+            every = pl.ds(0, 512)
+            b, s0, r0 = self.blocks, self.s0, self.r0
+
+            def copy(i, src, dst, device):
+                return Copy(src, dst, ss.at[s0 + i], rs.at[r0 + i], device)
+
+            if phase == 1:
+                return [copy(0, self._w((1 - c) * 256, 256, every), r1.at[b], sib)]
+            if phase == 2:
+                return [
+                    copy(1, self._w(give2x, 128, lanes_x), r2.at[b, :, lanes_x], xnb),
+                    copy(2, self._w(give2y, 128, lanes_y), r2.at[b, :, lanes_y], ynb),
+                ]
+            if phase == 3:
+                return [
+                    copy(3, self._w(give3x, 64, lanes_x), r3.at[b, :, lanes_x], ynb),
+                    copy(4, self._w(give3y, 64, lanes_y), r3.at[b, :, lanes_y], xnb),
+                ]
+            if phase == 4:
+                out = []
+                for k in range(1, 4):
+                    zt = lax.rem(z + k, nblk)
+                    out.append(
+                        copy(
+                            3 + 2 * k,
+                            self._w(keep3x + 16 * zt, 16, lanes_x),
+                            r4.at[k - 1, b, :, lanes_x],
+                            (dp, zt),
+                        )
+                    )
+                    out.append(
+                        copy(
+                            4 + 2 * k,
+                            self._w(keep3y + 16 * zt, 16, lanes_y),
+                            r4.at[k - 1, b, :, lanes_y],
+                            (dp, zt),
+                        )
+                    )
+                return out
+            if phase == 5:
+                out = []
+                for k in range(1, 4):
+                    zt = lax.rem(z + k, nblk)
+                    for i, (keep, lanes) in enumerate(((keep3x, lanes_x), (keep3y, lanes_y))):
+                        mine = self._f(keep + 16 * z, 16, lanes)
+                        out.append(copy(9 + 2 * k + i, mine, mine, (dp, zt)))
+                return out
+            if phase == 6:
+                mine_x, mine_y = self._f(keep3x, 64, lanes_x), self._f(keep3y, 64, lanes_y)
+                return [copy(17, mine_x, mine_x, ynb), copy(18, mine_y, mine_y, xnb)]
+            if phase == 7:
+                mine_x, mine_y = self._f(keep2x, 128, lanes_x), self._f(keep2y, 128, lanes_y)
+                return [copy(19, mine_x, mine_x, xnb), copy(20, mine_y, mine_y, ynb)]
+            return [copy(21, r1.at[b], self._out(base1), sib)]
+
+        def _f(self, first, n, lanes):
+            return r1.at[self.blocks, rows_of(first - base1, n), lanes]
+
+        def _out(self, first):
+            return wgrad_hbm.at[self.blocks, rows_of(first, 256), pl.ds(0, 512)]
+
+        def start(self, phase):
+            for one in self._list(phase):
+                one.start()
+
+        def finish(self, phase):
+            if phase == 8:
+                other = self._out((1 - c) * 256)
+                Copy(other, other, ss.at[0], rs.at[self.r0 + 21], sib).wait_recv()
+                return
+            for one in self._list(phase):
+                one.wait_recv()
+            if phase > 4:
+                return
+
+            def add(i, carry):
+                b = self.b0 + i
+                if phase == 1:
+                    here = (b, rows_of(base1, 256), slice(None))
+                    wg[here] = wg[here] + r1[b]
+                if phase == 2:
+                    for keep, lo in ((keep2x, 0), (keep2y, 256)):
+                        here = (b, rows_of(keep, 128), slice(lo, lo + 256))
+                        wg[here] = wg[here] + r2[b, :, lo : lo + 256]
+                if phase == 3:
+                    for keep, lo in ((keep3x, 0), (keep3y, 256)):
+                        here = (b, rows_of(keep, 64), slice(lo, lo + 256))
+                        wg[here] = wg[here] + r3[b, :, lo : lo + 256]
+                if phase == 4:
+                    for keep, lo in ((keep3x, 0), (keep3y, 256)):
+                        here = (b, rows_of(keep + 16 * z, 16), slice(lo, lo + 256))
+                        total = wg[here].astype(F32)
+                        for k in range(3):
+                            total = total + r4[k, b, :, lo : lo + 256].astype(F32)
+                        r1[b, rows_of(keep - base1 + 16 * z, 16), lo : lo + 256] = total.astype(BF16)
+                return carry
+
+            lax.fori_loop(0, self.nb, add, 0)
+
+        def step(self, phase):
+            self.finish(phase)
+            if phase < 8:
+                self.start(phase + 1)
+            if phase == 7:
+                self.store().start()
+
+        def store(self):
+            return pltpu.make_async_copy(r1.at[self.blocks], self._out(base1), ls.at[self.store_sem])
+
+        def wait_sends(self):
+            for phase in range(1, 9):
+                for one in self._list(phase):
+                    one.wait_send()
+
+    red = [Reduce(i) for i in range(3)]
+    for one in red:
+        one.store_sem = ids("l", 1)
+
+    for d in loads_f:
+        d.wait()
+
+    def ffn_chunk(j, carry):
+        up = mm(wup[j], n2_ref[...], TN)
+        size = jnp.abs(up) * (0.5**0.5)
+        t = 1.0 / (1.0 + 0.3275911 * size)
+        poly = t * (
+            0.254829592
+            + t * (-0.284496736 + t * (1.421413741 + t * (-1.453152027 + t * 1.061405429)))
+        )
+        decay = jnp.exp(-0.5 * up * up)
+        far = 0.5 * poly * decay
+        phi = jnp.where(up < 0.0, far, 1.0 - far)
+        slope = phi + up * decay * (1.0 / math.sqrt(2.0 * math.pi))
+        act = (up * phi).astype(BF16)
+        wg[2 * j] = mm(act, gb[...], NT).astype(BF16)
+        big[0] += mm(wdn[j], act, TN)
+        grad_up = (mm(wdn[j], gb[...], NN) * slope).astype(BF16)
+        wg[2 * j + 1] = mm(n2_ref[...], grad_up, NT).astype(BF16)
+        big[1] += mm(wup[j], grad_up, NN)
+
+        @pl.when(j == 1)
+        def _():
+            red[0].start(1)
+
+        return carry
+
+    lax.fori_loop(0, 4, ffn_chunk, 0)
+    red[0].step(1)
+
+    s_out, r_out = ids("s", 2), ids("r", 2)
+    res = big[0].astype(BF16)
+    owners = ((zl, c, lo_here), (3 - zl, 1 - c, hi_here))
+    for slot, (chip, i, here) in enumerate(owners):
+        out_s[slot] = res[:, slot * half : (slot + 1) * half]
+        go(
+            Copy(
+                out_s.at[slot],
+                out_r.at[i],
+                ss.at[s_out + slot],
+                rs.at[r_out + i],
+                dev(g, chip),
+                jnp.logical_not(here),
+            )
+        )
+
+        @pl.when(here)
+        def _():
+            out_r[i] = out_s[slot]
+
+    grad_n2 = big[1]
+    unit2 = hat2[...]
+    product = grad_n2 * unit2
+
+    def lane_fold(values):
+        total = values[:, 0:128]
+        for k in range(1, values.shape[1] // 128):
+            total = total + values[:, 128 * k : 128 * (k + 1)]
+        return total
+
+    gain_acc[1] = lane_fold(product)
+    e = grad_n2 * gain_col2
+    grad_mid = gb[...].astype(F32) + inverse2 * (
+        e
+        - jnp.mean(e, axis=0, keepdims=True)
+        - unit2 * jnp.mean(e * unit2, axis=0, keepdims=True)
+    )
+    gmid[0] = grad_mid[:, 0:half]
+    gmid[1] = grad_mid[:, half:]
+    branch = grad_mid.astype(BF16)
+    wg[8] = mm(att[...], branch, NT).astype(BF16)
+    red[1].start(1)
+    grad_att = mm(weights[3], branch, NN)
+    d_o[...] = grad_att.astype(BF16)
+    for slot in range(2):
+        lanes = slice(slot * half, (slot + 1) * half)
+        both = d_o[:, lanes].astype(F32) * o_acc[slot]
+        for h in range(HEADS):
+            d_sc[slot, h : h + 1, :] = jnp.sum(
+                both[64 * h : 64 * h + 64, :], axis=0, keepdims=True
+            )
+
+    dq[...] = jnp.zeros_like(dq)
+    gwqkv[...] = jnp.zeros_like(gwqkv)
+    gain_acc[0] = jnp.zeros((feat, 128), F32)
+    s_rc, r_rc = ids("s", 4), ids("r", 4)
+    s_rz, r_rz = ids("s", 4), ids("r", 4)
+    s_fin, r_fin = ids("s", 4), ids("r", 2)
+
+    def backward_step(slot, kb):
+        hq = hq_at(slot)
+        bias = bias_of(hq, kb)
+        lanes = pl.ds(pl.multiple_of(slot * half, half), half)
+        for h in range(HEADS):
+            part = slice(64 * h, 64 * h + 64)
+            key = k_t[kb, part, :]
+            query = q_t[slot, part, :]
+            grad_o = d_o[part, lanes]
+            s = mm(key, query, TN) * score_scale + bias
+            prob = jnp.exp2(s - m_sc[slot, h : h + 1, :])
+            grad_prob = mm(v_t[kb, part, :], grad_o, TN)
+            grad_s = (prob * (grad_prob - d_sc[slot, h : h + 1, :])).astype(BF16)
+            dv[part, :] += mm(grad_o, prob.astype(BF16), NT)
+            dk[part, :] += mm(query, grad_s, NT)
+            dq[slot, part, :] += mm(key, grad_s, NN)
+
+    att_scale = HEAD_DIM ** (-0.5)
+
+    def rc_copy(kb):
+        zb = lax.div(kb, 2)
+        return Copy(
+            ppart.at[kb],
+            rc.at[zb],
+            ss.at[s_rc + zb],
+            rs.at[r_rc + zb],
+            sib,
+            lax.rem(kb, 2) != c,
+        )
+
+    def is_final(zb):
+        return jnp.where(lax.div(zb, 2) == g, z == zb, is_near)
+
+    def rz_copy(zb):
+        return Copy(
+            ppart.at[2 * zb + c],
+            rz.at[zb],
+            ss.at[s_rz + zb],
+            rs.at[r_rz + zb],
+            dev(c, zo),
+            jnp.logical_not(is_final(zb)),
+        )
+
+    def fin_copy(zb):
+        here = jnp.logical_and(zb == z, g == c)
+        return Copy(
+            ppart.at[2 * zb + c],
+            gfin.at[c],
+            ss.at[s_fin + zb],
+            rs.at[r_fin + c],
+            dev(g, zb),
+            jnp.logical_and(is_final(zb), jnp.logical_not(here)),
+        )
+
+    def combine(zb):
+        kb = 2 * zb + c
+        Copy(rc.at[zb], rc.at[zb], ss.at[0], rs.at[r_rc + zb], sib).wait_recv()
+        ppart[kb] = ppart[kb] + rc[zb]
+        rz_copy(zb).start()
+
+    def deliver(zb):
+        kb = 2 * zb + c
+        final = is_final(zb)
+        Copy(rz.at[zb], rz.at[zb], ss.at[0], rs.at[r_rz + zb], sib, final).wait_recv()
+
+        @pl.when(final)
+        def _():
+            ppart[kb] = ppart[kb] + rz[zb]
+
+        @pl.when(jnp.logical_and(zb == z, g == c))
+        def _():
+            gfin[c] = ppart[kb]
+
+        fin_copy(zb).start()
+
+    schedule = {
+        0: [(0, 2), (1, 1)],
+        1: [(0, 3)],
+        2: [(1, 2)],
+        3: [(0, 4), (1, 3)],
+        4: [(0, 5)],
+        5: [(0, 6), (1, 4)],
+        6: [],
+        7: [(0, 7), (1, 5)],
+    }
+
+    def key_block(kb, carry):
+        @pl.when(kb <= 7 - w)
+        def _():
+            dk[...] = jnp.zeros_like(dk)
+            dv[...] = jnp.zeros_like(dv)
+
+            def one(i, carry):
+                slot = 1 - i
+                backward_step(slot, kb)
+                return carry
+
+            lax.fori_loop(0, jnp.where(kb <= w, 2, 1), one, 0)
+            grad_key = turned(dk[...] * att_scale, kb, -1.0)
+            grad_value = dv[...].astype(BF16)
+            normed = n1[kb]
+            gwqkv[1] += mm(normed, grad_key, NT)
+            gwqkv[2] += mm(normed, grad_value, NT)
+            big[0, :, 0:half] = mm(weights[1], grad_key, NN) + mm(weights[2], grad_value, NN)
+
+            @pl.when(jnp.logical_or(kb == w, kb == 7 - w))
+            def _():
+                slot = jnp.where(kb == w, 0, 1)
+                grad_query = turned(dq[slot] * att_scale, kb, -1.0)
+                gwqkv[0] += mm(normed, grad_query, NT)
+                big[0, :, 0:half] += mm(weights[0], grad_query, NN)
+
+            grad_n1 = big[0, :, 0:half]
+            unit, inverse = norm_parts(p_all[kb].astype(F32))
+            gain_acc[0] += lane_fold(grad_n1 * unit)
+            e = grad_n1 * gcol[0]
+            big[0, :, 0:half] = inverse * (
+                e
+                - jnp.mean(e, axis=0, keepdims=True)
+                - unit * jnp.mean(e * unit, axis=0, keepdims=True)
+            )
+
+            @pl.when(jnp.logical_or(kb == w, kb == 7 - w))
+            def _():
+                slot = jnp.where(kb == w, 0, 1)
+                big[0, :, 0:half] += gmid[slot]
+
+            ppart[kb] = big[0, :, 0:half].astype(BF16)
+
+        @pl.when(kb > 7 - w)
+        def _():
+            ppart[kb] = jnp.zeros(ppart.shape[1:], BF16)
+
+        rc_copy(kb).start()
+
+        @pl.when(lax.rem(kb, 2) == 1)
+        def _():
+            combine(lax.div(kb, 2))
+
+        @pl.when(jnp.logical_and(lax.rem(kb, 2) == 1, kb > 1))
+        def _():
+            deliver(lax.div(kb, 2) - 1)
+
+        for i, todo in schedule.items():
+            if todo:
+
+                @pl.when(kb == i)
+                def _():
+                    for chunk, phase in todo:
+                        red[chunk].step(phase)
+
+        return carry
+
+    lax.fori_loop(0, 8, key_block, 0)
+
+    for i in range(3):
+        wg[9 + i] = gwqkv[i].astype(BF16)
+    red[2].start(1)
+    for i in range(2):
+        gain_s[0, i : i + 1, :] = jnp.sum(gain_acc[i].T, axis=0, keepdims=True)
+    gain_s[0, 2:8, :] = jnp.zeros((6, feat), F32)
+    s_gain, r_gain = ids("s", 6), ids("r", 6)
+
+    def gain_list(phase):
+        if phase < 4:
+            device = (sib, xnb, ynb)[phase - 1]
+            k = phase - 1
+            return [
+                Copy(gain_s.at[k], gain_r.at[k], ss.at[s_gain + k], rs.at[r_gain + k], device)
+            ]
+        return [
+            Copy(
+                gain_s.at[3],
+                gain_r.at[2 + k],
+                ss.at[s_gain + 2 + k],
+                rs.at[r_gain + 2 + k],
+                (dp, lax.rem(z + k, nblk)),
+            )
+            for k in range(1, 4)
+        ]
+
+    def gain_finish(phase):
+        for one in gain_list(phase):
+            one.wait_recv()
+        if phase < 4:
+            gain_s[phase] = gain_s[phase - 1] + gain_r[phase - 1]
+            for one in gain_list(phase + 1):
+                one.start()
+        else:
+            total = jnp.zeros((8, feat), F32)
+            for zz in range(nblk):
+                k = lax.rem(z - zz + nblk, nblk)
+                part = gain_s[3]
+                for i in range(1, 4):
+                    part = jnp.where(k == i, gain_r[2 + i], part)
+                total = total + part
+            ggain_ref[...] = total
+
+    gain_list(1)[0].start()
+    deliver(3)
+    red[0].step(8)
+    red[1].step(6)
+    red[2].step(1)
+    gain_finish(1)
+
+    for i in range(2):
+        mine = out_from_self(i, c, z)
+        Copy(
+            out_r.at[i], out_r.at[i], ss.at[0], rs.at[r_out + i], sib, jnp.logical_not(mine)
+        ).wait_recv()
+        live = rdiv[1:2, i * half : (i + 1) * half]
+        out_ref[i * half : (i + 1) * half, :] = (out_r[i].astype(F32) * live).T
+
+    red[1].step(7)
+    red[2].step(2)
+    gain_finish(2)
+
+    for i in range(2):
+        mine = jnp.logical_and(own_worker, c == i)
+        Copy(
+            gfin.at[i], gfin.at[i], ss.at[0], rs.at[r_fin + i], sib, jnp.logical_not(mine)
+        ).wait_recv()
+        grad_sums = gfin[i].astype(F32) * rdiv[0:1, i * half : (i + 1) * half]
+        gs_ref[i * half : (i + 1) * half, :] = grad_sums.T.astype(BF16)
+
+    is_last = jnp.where(iota((16, feat), 1).astype(F32) == cnt - 1.0, 1.0, 0.0).astype(BF16)
+    last_s[...] = mm(is_last, gs_ref[...], NN).astype(BF16)
+    s_last, r_last = ids("s", 1), ids("r", 1)
+    copy_last = Copy(
+        last_s,
+        last_r,
+        ss.at[s_last],
+        rs.at[r_last],
+        (dp, lax.rem(z + 1, nblk)),
+        z < nblk - 1,
+    )
+    go(copy_last)
+
+    red[2].step(3)
+    gain_finish(3)
+    red[1].step(8)
+    red[2].step(4)
+    gain_finish(4)
+    Copy(last_r, last_r, ss.at[0], rs.at[r_last], sib, z > 0).wait_recv()
+
+    @pl.when(z == 0)
+    def _():
+        last_r[...] = jnp.zeros_like(last_r)
+
+    came_ref[...] = last_r[...]
+    for phase in range(5, 9):
+        red[2].step(phase)
+
+    for one in sends:
+        one.wait_send()
+
+    def close_key(kb, carry):
+        rc_copy(kb).wait_send()
+        return carry
+
+    lax.fori_loop(0, 8, close_key, 0)
+
+    def close_block(zb, carry):
+        rz_copy(zb).wait_send()
+        fin_copy(zb).wait_send()
+        return carry
+
+    lax.fori_loop(0, 4, close_block, 0)
+    for phase in range(1, 5):
+        for one in gain_list(phase):
+            one.wait_send()
+    for one in red:
+        one.wait_sends()
+        one.store().wait()
+
+
+def out_from_self(i, c, z):
+    chip = 2 * c + jnp.where(z < 2, z, 3 - z)
+    core = jnp.where(z < 2, i, 1 - i)
+    return jnp.logical_and(core == c, chip == z)
+
+
+def expand_kernel(
+    slots_ref, gs_ref, came_ref, dn_ref, up0, up1, up2, up3, wo_ref, wq_ref, wk_ref, wv_ref,
+    bytes_out, dn_out, up_out, wo_out, wq_out, wk_out, wv_out,
+):
+    rows = slots_ref[0]
+    slot_iota = iota((512, 128), 0).astype(F32)
+    member = jnp.concatenate(
+        [(slot_iota == rows[r : r + 1, :]).astype(F32).astype(BF16) for r in range(4)], axis=1
+    )
+    first = iota((16, 128), 0) == 0
+    lead = jnp.concatenate(
+        [
+            jnp.where(jnp.logical_and(first, rows[r : r + 1, :] < -0.5), 1.0, 0.0).astype(BF16)
+            for r in range(4)
+        ],
+        axis=1,
+    )
+    bytes_out[...] = mm(member, gs_ref[...], TN) + mm(lead, came_ref[...], TN)
+    dn_out[...] = dn_ref[0].astype(F32)
+    for j, up in enumerate((up0, up1, up2, up3)):
+        up_out[:, 512 * j : 512 * (j + 1)] = up[0].astype(F32)
+    for src, dst in ((wo_ref, wo_out), (wq_ref, wq_out), (wk_ref, wk_out), (wv_ref, wv_out)):
+        dst[...] = src[0].astype(F32)
+
+
+def fast_local(
+    bytes_in, flags, lengths, cotangent, w_query, w_key, w_value, w_out, w_up, w_down, gain_attn, gain_ffn
+):
+    meta_flags = flags.reshape(32, 128)
+    meta_lengths = jnp.pad(lengths, ((0, 7), (0, 124)))
+    gains = jnp.stack([gain_attn, gain_ffn])
+    freqs = ROTARY_BASE ** (-2.0 * jnp.arange(32, dtype=jnp.float32) / 64)
+    freq = jnp.broadcast_to(freqs[:, None], (32, 128))
+    vm = pl.BlockSpec(memory_space=pltpu.VMEM)
+    hbm = pl.BlockSpec(memory_space=pl.ANY)
+    hb = lambda n: pltpu.VMEM((n, 512, 256), BF16)
+    hbf = lambda n: pltpu.VMEM((n, 512, 256), F32)
+    sq = lambda n, t: pltpu.VMEM((n, 512, 512), t)
+    scratch = dict(
+        bytes_v=sq(8, BF16),
+        weights=sq(4, BF16),
+        wup=sq(4, BF16),
+        wdn=sq(4, BF16),
+        meta=pltpu.VMEM((2, 4, 40, 128), jnp.int32),
+        tail=pltpu.VMEM((16, 512), BF16),
+        slot_sc=pltpu.VMEM((8, 4, 128), F32),
+        p_own=hb(2),
+        relay=pltpu.VMEM((512, 256), BF16),
+        p_all=hb(8),
+        n1=hb(8),
+        k_t=hb(8),
+        v_t=hb(8),
+        q_t=hb(2),
+        tab_c=pltpu.VMEM((8, 32, 256), F32),
+        tab_s=pltpu.VMEM((8, 32, 256), F32),
+        pos=pltpu.VMEM((8, 8, 256), F32),
+        gcol=hbf(2),
+        cot_own=hb(2),
+        cot_w=hb(2),
+        o_acc=hbf(2),
+        m_sc=pltpu.VMEM((2, 8, 256), F32),
+        l_sc=pltpu.VMEM((2, 8, 256), F32),
+        att=pltpu.VMEM((512, 512), BF16),
+        gb=pltpu.VMEM((512, 512), BF16),
+        hat2=pltpu.VMEM((512, 512), F32),
+        d_o=pltpu.VMEM((512, 512), BF16),
+        d_sc=pltpu.VMEM((2, 8, 256), F32),
+        gmid=hbf(2),
+        dk=pltpu.VMEM((512, 256), F32),
+        dv=pltpu.VMEM((512, 256), F32),
+        dq=hbf(2),
+        gwqkv=sq(3, F32),
+        big=sq(2, F32),
+        wg=sq(12, BF16),
+        r1=pltpu.VMEM((12, 256, 512), BF16),
+        r2=pltpu.VMEM((12, 128, 512), BF16),
+        r3=pltpu.VMEM((12, 64, 512), BF16),
+        r4=pltpu.VMEM((3, 12, 16, 512), BF16),
+        ppart=hb(8),
+        rc=hb(4),
+        rz=hb(4),
+        gfin=hb(2),
+        out_s=hb(2),
+        out_r=hb(2),
+        rdiv=pltpu.VMEM((16, 512), F32),
+        last_s=pltpu.VMEM((16, 512), BF16),
+        last_r=pltpu.VMEM((16, 512), BF16),
+        gain_acc=pltpu.VMEM((2, 512, 128), F32),
+        gain_s=pltpu.VMEM((4, 8, 512), F32),
+        gain_r=pltpu.VMEM((6, 8, 512), F32),
+        ss=pltpu.SemaphoreType.DMA((128,)),
+        rs=pltpu.SemaphoreType.DMA((128,)),
+        ls=pltpu.SemaphoreType.DMA((32,)),
+    )
+    out, gs, came, slots, wgrad, ggain = pl.pallas_call(
+        layer_kernel,
+        out_shape=(
+            jax.ShapeDtypeStruct((512, 512), F32),
+            jax.ShapeDtypeStruct((512, 512), BF16),
+            jax.ShapeDtypeStruct((16, 512), BF16),
+            jax.ShapeDtypeStruct((32, 128), F32),
+            jax.ShapeDtypeStruct((12, 512, 512), BF16),
+            jax.ShapeDtypeStruct((8, 512), F32),
+        ),
+        in_specs=[hbm, vm, vm, hbm, hbm, hbm, hbm, hbm, hbm, hbm, vm, vm],
+        out_specs=(vm, vm, vm, vm, hbm, vm),
+        scratch_shapes=list(scratch.values()),
+        compiler_params=pltpu.CompilerParams(
+            collective_id=0, has_side_effects=True, vmem_limit_bytes=60 * 2**20
+        ),
+        name="layer",
+    )(
+        bytes_in, meta_flags, meta_lengths, cotangent, w_query, w_key, w_value, w_out, w_up, w_down,
+        gains, freq,
+    )
+    block = lambda rows, cols, index: pl.BlockSpec((1, rows, cols), index)
+    ups = [block(64, 512, functools.partial(lambda j, i: (2 * j + 1, i, 0), j)) for j in range(4)]
+    rest = [block(64, 512, functools.partial(lambda j, i: (j, i, 0), j)) for j in range(8, 12)]
+    whole = lambda shape: pl.BlockSpec(shape, lambda i: (0, 0))
+    flat = lambda rows, cols: pl.BlockSpec((rows, cols), lambda i: (i, 0))
+    grad_bytes, dn, up, wo, wq, wk, wv = pl.pallas_call(
+        expand_kernel,
+        grid=(8,),
+        out_shape=(
+            jax.ShapeDtypeStruct((4096, 512), F32),
+            jax.ShapeDtypeStruct((2048, 512), F32),
+            jax.ShapeDtypeStruct((512, 2048), F32),
+        )
+        + (jax.ShapeDtypeStruct((512, 512), F32),) * 4,
+        in_specs=[
+            block(4, 128, lambda i: (i, 0, 0)),
+            whole((512, 512)),
+            whole((16, 512)),
+            block(256, 512, lambda i: (2 * lax.div(i, 2), lax.rem(i, 2), 0)),
+        ]
+        + ups
+        + rest,
+        out_specs=(flat(512, 512), flat(256, 512), flat(64, 2048)) + (flat(64, 512),) * 4,
+        compiler_params=pltpu.CompilerParams(vmem_limit_bytes=40 * 2**20),
+        name="expand",
+    )(slots.reshape(8, 4, 128), gs, came, wgrad, wgrad, wgrad, wgrad, wgrad, wgrad, wgrad, wgrad, wgrad)
+    return out, grad_bytes, wq, wk, wv, wo, up, dn, ggain[0], ggain[1]
 
 
 def passed_along(block, axis, distance):
@@ -341,8 +1525,9 @@
 
 
 def solution(mesh):
+    fits = mesh.shape["blk"] == 4 and mesh.shape["dp"] == 8
     return jax.shard_map(
-        local,
+        fast_local if fits else local,
         mesh=mesh,
         in_specs=(
             P(("dp", "blk"), None),

time: 746 us -> 207 us (0.28); the launches traced: 736 us -> 205 us
  waiting for transfers between devices: 371 us -> 0 us
  Pallas kernels: 0 us -> 193 us
  matrix products: 104 us -> 0 us
  starting transfers between devices: 69.8 us -> 0 us
  other arithmetic: 69.7 us -> 1.31 us
  blocking collectives: 51.7 us -> 0 us
  local copies, waits for them, and re-layouts: 48.9 us -> 9.54 us
  between operations: 17 us -> 0.67 us
    pallas_call x0 -> x2, Pallas kernels: none -> 193 us  [the longest x1 184 us: fast_local(): pl.pallas_call(layer_kernel, out_shape=(jax.ShapeDtypeStruct((512, 512),...]
    psum x1 -> x0, waiting for transfers between devices: 160 us -> none  [local(): lax.psum((grad_w_query, grad_w_key, grad_w_value, grad_w_out, grad_w_up,...]
    ppermute x19 -> x0, waiting for transfers between devices: 129 us -> none  [the longest x11 81.3 us: from_behind(): return lax.ppermute(value, axis, pairs)]
    dot_general x33 -> x0, matrix products: 104 us -> none  [the longest x1 16.3 us: absorb_update(): jnp.einsum('hqk,khe->qhe', weights.astype(jnp.bfloat16), value_piece.resh...]
    all_gather x2 -> x0, waiting for transfers between devices: 81.9 us -> none  [the longest x1 46.8 us: local(): value_piece = lax.all_gather(value_low, 'blk', axis=0, tiled=True)]
    ppermute x19 -> x0, starting transfers between devices: 69.7 us -> none  [the longest x11 37.2 us: from_behind(): return lax.ppermute(value, axis, pairs)]
    psum x1 -> x0, blocking collectives: 45 us -> none  [local(): lax.psum((grad_w_query, grad_w_key, grad_w_value, grad_w_out, grad_w_up,...]
    convert_element_type x23 -> x0, other arithmetic: 26.5 us -> none  [the longest x4 8.56 us: pass_grads(): passed_along(grad_value.astype(jnp.bfloat16), 'blk', 1)]
  transfers between devices with their start and end apart: 22 -> 0, of which waited for: 18 -> 0; matrix products, arithmetic and copies ran while one was open for 9% -> 0% of each run, Pallas kernels for 0% -> 0%
where the time goes in v1:
time: 207 us; the launch traced here: 205 us
  Pallas kernels  193 us (93%)
  local copies, waits for them, and re-layouts  9.54 us (5%)
    pallas_call x1, Pallas kernels, fast_local(): pl.pallas_call(layer_kernel, out_shape=(jax.ShapeDtypeStruct((512, 512),...  184 us
    pallas_call x1, Pallas kernels, fast_local(): pl.pallas_call(expand_kernel, grid=(8,), out_shape=(jax.ShapeDtypeStruct(...  9.01 us
    unnamed x11, local copies, waits for them, and re-layouts  6.24 us

profile of v1, /device:TPU:9, one launch (start us, length us, event | category | flops | bytes accessed | tf_op | source)
XLA Modules:
  0.0 204.7 jit_solution(11769885231016005222)
XLA Ops:
  0.7 1.3 pad.4.lengths_ref
  1.9 1.3 pad_maximum_fusion.gains_ref
  3.2 0.7 broadcast_in_dim.2.freq_ref
  3.9 184.2 %layer.1 = (f32[512,512]{1,0:T(8,128)}, bf16[512,512]{1,0:T(8,128)(2,1)}, bf16[16,512]{1,0:T(8,128)(2,1)}, f32[32,128]{1,0:T(8,128)}, bf16[12,512,512]{2,1,0:T(8,128)(2,1)}, /*index=5*/f32[8,512]{1,0:T(8,128)}) custom-call(bf16[4096,512]{1,0:T(8,128)(2,1)} %bytes_hbm.1, s32[32,128]{1,0:T(8,128)} %bitcast.7, s32[8,128]{1,0:T(8,128)} %pad.4.lengths_ref, ...), custom_call_target="tpu_custom_call" | custom-call | tf_op jit(solution)/shard_map/layer/pallas_call | solution.py:1149
  188.1 1.4 fusion
  189.4 0.0 copy-start
  189.4 2.8 %copy-done = bf16[12,512,512]{2,1,0:T(8,128)(2,1)S(1)} copy-done((bf16[12,512,512]{2,1,0:T(8,128)(2,1)S(1)}, bf16[12,512,512]{2,1,0:T(8,128)(2,1)}, u32[]{:S(2)}) %copy-start) | copy-done | bytes 6291480
  192.2 0.0 copy-start.1
  192.2 1.0 copy-done.1
  193.3 0.0 copy-start.2
  193.3 0.7 copy-done.2
  194.0 0.0 copy-start.3
  194.0 0.7 copy-done.3
  194.7 0.0 copy-start.4
  194.7 9.0 %expand.1 = (f32[4096,512]{1,0:T(8,128)}, f32[2048,512]{1,0:T(8,128)}, f32[512,2048]{1,0:T(8,128)}, f32[512,512]{1,0:T(8,128)}, f32[512,512]{1,0:T(8,128)}, /*index=5*/f32[512,512]{1,0:T(8,128)}, f32[512,512]{1,0:T(8,128)}) custom-call(f32[8,4,128]{2,1,0:T(4,128)S(1)} %bitcast.6, bf16[512,512]{1,0:T(8,128)(2,1)S(1)} %copy-done.1, ...), custom_call_target="tpu_custom_call" | custom-call | tf_op jit(solution)/shard_map/expand/pallas_call | solution.py:1175
  203.7 0.0 copy-done.4
  203.7 1.0 copy.23
  (1 shorter events, 0.0 us)
Async XLA Ops:
  189.4 2.8 %copy-start = (bf16[12,512,512]{2,1,0:T(8,128)(2,1)S(1)}, bf16[12,512,512]{2,1,0:T(8,128)(2,1)}, u32[]{:S(2)}) copy-start(bf16[12,512,512]{2,1,0:T(8,128)(2,1)} %get-tuple-element.27.dn_ref.up0.up1.up2.up3.wo_ref.wq_ref.wk_ref.wv_ref) | copy-start | bytes 18874372
  192.2 1.0 copy-start.1
  193.3 0.7 copy-start.2
  194.0 0.7 copy-start.3
  194.7 9.0 %copy-start.4 = (f32[512,512]{1,0:T(8,128)S(1)}, f32[512,512]{1,0:T(8,128)}, u32[]{:S(2)}) copy-start(f32[512,512]{1,0:T(8,128)} %get-tuple-element.48) | copy-start | bytes 3145732

commit v2 on v1

--- a/solution.py
+++ b/solution.py
@@ -82,7 +82,8 @@
     wo_hbm,
     wup_hbm,
     wdn_hbm,
-    gains_ref,
+    gain_attn_ref,
+    gain_ffn_ref,
     freq_ref,
     out_ref,
     gs_ref,
@@ -230,7 +231,8 @@
     pl.semaphore_wait(barrier, 9)
 
     meta[c, z, 0:32, :] = flags_ref[...]
-    meta[c, z, 32:40, :] = lengths_ref[...]
+    meta[c, z, 32:40, :] = jnp.zeros((8, 128), jnp.int32)
+    meta[c, z, 32:33, 0:4] = lengths_ref[...]
     s_meta, r_meta = ids("s", 7), ids("r", 8)
     for k, (core, zz) in enumerate(line):
         go(
@@ -294,8 +296,8 @@
 
     lax.fori_loop(0, 8, pool, 0)
 
-    for i in range(2):
-        row = jnp.broadcast_to(gains_ref[i : i + 1, :], (128, feat))
+    for i, gain in enumerate((gain_attn_ref, gain_ffn_ref)):
+        row = jnp.broadcast_to(gain[...], (128, feat))
         col = row.T
         gcol[i] = jnp.concatenate([col, col], axis=1)
 
@@ -494,26 +496,38 @@
     l_sc[...] = jnp.zeros_like(l_sc)
     m_sc[...] = jnp.full(m_sc.shape, NEGATIVE, F32)
 
+    def s_at(h):
+        return gwqkv.at[h // 4, pl.ds(half * ((h // 2) % 2), half), pl.ds(half * (h % 2), half)]
+
+    o_new = big.at[1, :, pl.ds(0, half)]
+
     def forward_step(t, carry):
         low_half = t <= w
         slot = jnp.where(low_half, 0, 1)
         kb = jnp.where(low_half, t, t - w - 1)
         hq = hq_at(slot)
         bias = bias_of(hq, kb)
+        old = m_sc[slot]
+        old_sum = l_sc[slot]
         for h in range(HEADS):
             part = slice(64 * h, 64 * h + 64)
-            s = mm(k_t[kb, part, :], q_t[slot, part, :], TN) * score_scale + bias
-            old = m_sc[slot, h : h + 1, :]
-            new = jnp.maximum(old, jnp.max(s, axis=0, keepdims=True))
-            prob = jnp.exp2(s - new)
-            shrink = jnp.exp2(old - new)
-            l_sc[slot, h : h + 1, :] = l_sc[slot, h : h + 1, :] * shrink + jnp.sum(
-                prob, axis=0, keepdims=True
-            )
-            m_sc[slot, h : h + 1, :] = new
-            o_acc[slot, part, :] = o_acc[slot, part, :] * shrink + mm(
-                v_t[kb, part, :], prob.astype(BF16), NN
-            )
+            s_at(h)[...] = mm(k_t[kb, part, :], q_t[slot, part, :], TN)
+        tops, sums = [], []
+        for h in range(HEADS):
+            part = slice(64 * h, 64 * h + 64)
+            s = s_at(h)[...] * score_scale + bias
+            top = jnp.maximum(old[h : h + 1, :], jnp.max(s, axis=0, keepdims=True))
+            prob = jnp.exp2(s - top)
+            tops.append(top)
+            sums.append(jnp.sum(prob, axis=0, keepdims=True))
+            o_new[part, :] = mm(v_t[kb, part, :], prob.astype(BF16), NN)
+        new = jnp.concatenate(tops, axis=0)
+        shrink = jnp.exp2(old - new)
+        m_sc[slot] = new
+        l_sc[slot] = old_sum * shrink + jnp.concatenate(sums, axis=0)
+        for h in range(HEADS):
+            part = slice(64 * h, 64 * h + 64)
+            o_acc[slot, part, :] = o_acc[slot, part, :] * shrink[h : h + 1, :] + o_new[part, :]
         return carry
 
     lax.fori_loop(0, 9, forward_step, 0)
@@ -770,22 +784,28 @@
     s_rz, r_rz = ids("s", 4), ids("r", 4)
     s_fin, r_fin = ids("s", 4), ids("r", 2)
 
+    def sd_at(which, h):
+        return big.at[which, pl.ds(half * ((h // 2) % 2), half), pl.ds(half * (h % 2), half)]
+
     def backward_step(slot, kb):
         hq = hq_at(slot)
         bias = bias_of(hq, kb)
         lanes = pl.ds(pl.multiple_of(slot * half, half), half)
-        for h in range(HEADS):
-            part = slice(64 * h, 64 * h + 64)
-            key = k_t[kb, part, :]
-            query = q_t[slot, part, :]
-            grad_o = d_o[part, lanes]
-            s = mm(key, query, TN) * score_scale + bias
-            prob = jnp.exp2(s - m_sc[slot, h : h + 1, :])
-            grad_prob = mm(v_t[kb, part, :], grad_o, TN)
-            grad_s = (prob * (grad_prob - d_sc[slot, h : h + 1, :])).astype(BF16)
-            dv[part, :] += mm(grad_o, prob.astype(BF16), NT)
-            dk[part, :] += mm(query, grad_s, NT)
-            dq[slot, part, :] += mm(key, grad_s, NN)
+        lse = m_sc[slot]
+        dots = d_sc[slot]
+        for first in (0, 4):
+            for h in range(first, first + 4):
+                part = slice(64 * h, 64 * h + 64)
+                grad_o = d_o[part, lanes]
+                sd_at(0, h)[...] = mm(k_t[kb, part, :], q_t[slot, part, :], TN)
+                sd_at(1, h)[...] = mm(v_t[kb, part, :], grad_o, TN)
+            for h in range(first, first + 4):
+                part = slice(64 * h, 64 * h + 64)
+                prob = jnp.exp2(sd_at(0, h)[...] * score_scale + bias - lse[h : h + 1, :])
+                grad_s = (prob * (sd_at(1, h)[...] - dots[h : h + 1, :])).astype(BF16)
+                dv[part, :] += mm(d_o[part, lanes], prob.astype(BF16), NT)
+                dk[part, :] += mm(q_t[slot, part, :], grad_s, NT)
+                dq[slot, part, :] += mm(k_t[kb, part, :], grad_s, NN)
 
     att_scale = HEAD_DIM ** (-0.5)
 
@@ -845,16 +865,13 @@
 
         fin_copy(zb).start()
 
-    schedule = {
-        0: [(0, 2), (1, 1)],
-        1: [(0, 3)],
-        2: [(1, 2)],
-        3: [(0, 4), (1, 3)],
-        4: [(0, 5)],
-        5: [(0, 6), (1, 4)],
-        6: [],
-        7: [(0, 7), (1, 5)],
-    }
+    def ticks(at, schedule):
+        for i, todo in schedule.items():
+
+            @pl.when(at == i)
+            def _():
+                for chunk, phase in todo:
+                    red[chunk].step(phase)
 
     def key_block(kb, carry):
         @pl.when(kb <= 7 - w)
@@ -863,41 +880,72 @@
             dv[...] = jnp.zeros_like(dv)
 
             def one(i, carry):
-                slot = 1 - i
-                backward_step(slot, kb)
+                backward_step(1 - i, kb)
                 return carry
 
             lax.fori_loop(0, jnp.where(kb <= w, 2, 1), one, 0)
             grad_key = turned(dk[...] * att_scale, kb, -1.0)
             grad_value = dv[...].astype(BF16)
             normed = n1[kb]
+            k_t[kb] = grad_key
+            v_t[kb] = grad_value
             gwqkv[1] += mm(normed, grad_key, NT)
             gwqkv[2] += mm(normed, grad_value, NT)
-            big[0, :, 0:half] = mm(weights[1], grad_key, NN) + mm(weights[2], grad_value, NN)
 
             @pl.when(jnp.logical_or(kb == w, kb == 7 - w))
             def _():
                 slot = jnp.where(kb == w, 0, 1)
                 grad_query = turned(dq[slot] * att_scale, kb, -1.0)
+                q_t[slot] = grad_query
                 gwqkv[0] += mm(normed, grad_query, NT)
-                big[0, :, 0:half] += mm(weights[0], grad_query, NN)
+
+        ticks(
+            kb,
+            {
+                0: [(1, 1)],
+                1: [(0, 2)],
+                2: [(0, 3)],
+                3: [(1, 2)],
+                4: [(0, 4)],
+                5: [(1, 3)],
+                6: [(0, 5)],
+                7: [(0, 6)],
+            },
+        )
+        return carry
+
+    lax.fori_loop(0, 8, key_block, 0)
+    for i in range(3):
+        wg[9 + i] = gwqkv[i].astype(BF16)
+    red[2].start(1)
+
+    def block_at(j):
+        return jnp.where(g == 0, 3 - j, j)
+
+    def row_block(i, carry):
+        j = lax.div(i, 2)
+        kb = 2 * block_at(j) + lax.rem(i, 2)
+
+        @pl.when(kb <= 7 - w)
+        def _():
+            big[0, :, 0:half] = mm(weights[1], k_t[kb], NN) + mm(weights[2], v_t[kb], NN)
+            own = jnp.logical_or(kb == w, kb == 7 - w)
+            slot = jnp.where(kb == w, 0, 1)
+
+            @pl.when(own)
+            def _():
+                big[0, :, 0:half] += mm(weights[0], q_t[slot], NN)
 
             grad_n1 = big[0, :, 0:half]
             unit, inverse = norm_parts(p_all[kb].astype(F32))
             gain_acc[0] += lane_fold(grad_n1 * unit)
             e = grad_n1 * gcol[0]
-            big[0, :, 0:half] = inverse * (
+            total = inverse * (
                 e
                 - jnp.mean(e, axis=0, keepdims=True)
                 - unit * jnp.mean(e * unit, axis=0, keepdims=True)
             )
-
-            @pl.when(jnp.logical_or(kb == w, kb == 7 - w))
-            def _():
-                slot = jnp.where(kb == w, 0, 1)
-                big[0, :, 0:half] += gmid[slot]
-
-            ppart[kb] = big[0, :, 0:half].astype(BF16)
+            ppart[kb] = (total + jnp.where(own, 1.0, 0.0) * gmid[slot]).astype(BF16)
 
         @pl.when(kb > 7 - w)
         def _():
@@ -905,29 +953,31 @@
 
         rc_copy(kb).start()
 
-        @pl.when(lax.rem(kb, 2) == 1)
+        @pl.when(lax.rem(i, 2) == 1)
         def _():
-            combine(lax.div(kb, 2))
-
-        @pl.when(jnp.logical_and(lax.rem(kb, 2) == 1, kb > 1))
+            combine(block_at(j))
+
+        @pl.when(jnp.logical_and(lax.rem(i, 2) == 1, i > 1))
         def _():
-            deliver(lax.div(kb, 2) - 1)
-
-        for i, todo in schedule.items():
-            if todo:
-
-                @pl.when(kb == i)
-                def _():
-                    for chunk, phase in todo:
-                        red[chunk].step(phase)
-
+            deliver(block_at(j - 1))
+
+        ticks(
+            i,
+            {
+                0: [(2, 1)],
+                1: [(1, 4)],
+                2: [(0, 7)],
+                3: [(2, 2)],
+                4: [(1, 5)],
+                5: [(0, 8)],
+                6: [(2, 3)],
+                7: [(1, 6)],
+            },
+        )
         return carry
 
-    lax.fori_loop(0, 8, key_block, 0)
-
-    for i in range(3):
-        wg[9 + i] = gwqkv[i].astype(BF16)
-    red[2].start(1)
+    lax.fori_loop(0, 8, row_block, 0)
+
     for i in range(2):
         gain_s[0, i : i + 1, :] = jnp.sum(gain_acc[i].T, axis=0, keepdims=True)
     gain_s[0, 2:8, :] = jnp.zeros((6, feat), F32)
@@ -969,11 +1019,10 @@
             ggain_ref[...] = total
 
     gain_list(1)[0].start()
-    deliver(3)
-    red[0].step(8)
-    red[1].step(6)
-    red[2].step(1)
+    red[2].step(4)
+    deliver(block_at(3))
     gain_finish(1)
+    red[1].step(7)
 
     for i in range(2):
         mine = out_from_self(i, c, z)
@@ -981,11 +1030,10 @@
             out_r.at[i], out_r.at[i], ss.at[0], rs.at[r_out + i], sib, jnp.logical_not(mine)
         ).wait_recv()
         live = rdiv[1:2, i * half : (i + 1) * half]
-        out_ref[i * half : (i + 1) * half, :] = (out_r[i].astype(F32) * live).T
-
-    red[1].step(7)
-    red[2].step(2)
+        out_ref[i * half : (i + 1) * half, :] = (out_r[i].astype(F32) * live).T.astype(BF16)
+
     gain_finish(2)
+    red[2].step(5)
 
     for i in range(2):
         mine = jnp.logical_and(own_worker, c == i)
@@ -1008,10 +1056,9 @@
     )
     go(copy_last)
 
-    red[2].step(3)
+    red[1].step(8)
     gain_finish(3)
-    red[1].step(8)
-    red[2].step(4)
+    red[2].step(6)
     gain_finish(4)
     Copy(last_r, last_r, ss.at[0], rs.at[r_last], sib, z > 0).wait_recv()
 
@@ -1020,7 +1067,7 @@
         last_r[...] = jnp.zeros_like(last_r)
 
     came_ref[...] = last_r[...]
-    for phase in range(5, 9):
+    for phase in range(7, 9):
         red[2].step(phase)
 
     for one in sends:
@@ -1053,8 +1100,8 @@
 
 
 def expand_kernel(
-    slots_ref, gs_ref, came_ref, dn_ref, up0, up1, up2, up3, wo_ref, wq_ref, wk_ref, wv_ref,
-    bytes_out, dn_out, up_out, wo_out, wq_out, wk_out, wv_out,
+    slots_ref, gs_ref, came_ref, out_ref, ggain_ref, dn_ref, up0, up1, up2, up3, wo_ref, wq_ref, wk_ref, wv_ref,
+    bytes_out, out_out, ga_out, gf_out, dn_out, up_out, wo_out, wq_out, wk_out, wv_out,
 ):
     rows = slots_ref[0]
     slot_iota = iota((512, 128), 0).astype(F32)
@@ -1070,6 +1117,9 @@
         axis=1,
     )
     bytes_out[...] = mm(member, gs_ref[...], TN) + mm(lead, came_ref[...], TN)
+    out_out[...] = out_ref[...].astype(F32)
+    ga_out[...] = ggain_ref[0:1, :]
+    gf_out[...] = ggain_ref[1:2, :]
     dn_out[...] = dn_ref[0].astype(F32)
     for j, up in enumerate((up0, up1, up2, up3)):
         up_out[:, 512 * j : 512 * (j + 1)] = up[0].astype(F32)
@@ -1081,10 +1131,8 @@
     bytes_in, flags, lengths, cotangent, w_query, w_key, w_value, w_out, w_up, w_down, gain_attn, gain_ffn
 ):
     meta_flags = flags.reshape(32, 128)
-    meta_lengths = jnp.pad(lengths, ((0, 7), (0, 124)))
-    gains = jnp.stack([gain_attn, gain_ffn])
-    freqs = ROTARY_BASE ** (-2.0 * jnp.arange(32, dtype=jnp.float32) / 64)
-    freq = jnp.broadcast_to(freqs[:, None], (32, 128))
+    freqs = np.float32(ROTARY_BASE) ** (-2.0 * np.arange(32, dtype=np.float32) / np.float32(64))
+    freq = np.ascontiguousarray(np.broadcast_to(freqs.astype(np.float32)[:, None], (32, 128)))
     vm = pl.BlockSpec(memory_space=pltpu.VMEM)
     hbm = pl.BlockSpec(memory_space=pl.ANY)
     hb = lambda n: pltpu.VMEM((n, 512, 256), BF16)
@@ -1149,14 +1197,14 @@
     out, gs, came, slots, wgrad, ggain = pl.pallas_call(
         layer_kernel,
         out_shape=(
-            jax.ShapeDtypeStruct((512, 512), F32),
+            jax.ShapeDtypeStruct((512, 512), BF16),
             jax.ShapeDtypeStruct((512, 512), BF16),
             jax.ShapeDtypeStruct((16, 512), BF16),
             jax.ShapeDtypeStruct((32, 128), F32),
             jax.ShapeDtypeStruct((12, 512, 512), BF16),
             jax.ShapeDtypeStruct((8, 512), F32),
         ),
-        in_specs=[hbm, vm, vm, hbm, hbm, hbm, hbm, hbm, hbm, hbm, vm, vm],
+        in_specs=[hbm, vm, vm, hbm, hbm, hbm, hbm, hbm, hbm, hbm, vm, vm, vm],
         out_specs=(vm, vm, vm, vm, hbm, vm),
         scratch_shapes=list(scratch.values()),
         compiler_params=pltpu.CompilerParams(
@@ -1164,19 +1212,22 @@
         ),
         name="layer",
     )(
-        bytes_in, meta_flags, meta_lengths, cotangent, w_query, w_key, w_value, w_out, w_up, w_down,
-        gains, freq,
+        bytes_in, meta_flags, lengths, cotangent, w_query, w_key, w_value, w_out, w_up, w_down,
+        gain_attn.reshape(1, 512), gain_ffn.reshape(1, 512), freq,
     )
     block = lambda rows, cols, index: pl.BlockSpec((1, rows, cols), index)
     ups = [block(64, 512, functools.partial(lambda j, i: (2 * j + 1, i, 0), j)) for j in range(4)]
     rest = [block(64, 512, functools.partial(lambda j, i: (j, i, 0), j)) for j in range(8, 12)]
     whole = lambda shape: pl.BlockSpec(shape, lambda i: (0, 0))
     flat = lambda rows, cols: pl.BlockSpec((rows, cols), lambda i: (i, 0))
-    grad_bytes, dn, up, wo, wq, wk, wv = pl.pallas_call(
+    grad_bytes, out, g_attn, g_ffn, dn, up, wo, wq, wk, wv = pl.pallas_call(
         expand_kernel,
         grid=(8,),
         out_shape=(
             jax.ShapeDtypeStruct((4096, 512), F32),
+            jax.ShapeDtypeStruct((512, 512), F32),
+            jax.ShapeDtypeStruct((1, 512), F32),
+            jax.ShapeDtypeStruct((1, 512), F32),
             jax.ShapeDtypeStruct((2048, 512), F32),
             jax.ShapeDtypeStruct((512, 2048), F32),
         )
@@ -1185,15 +1236,17 @@
             block(4, 128, lambda i: (i, 0, 0)),
             whole((512, 512)),
             whole((16, 512)),
+            flat(64, 512),
+            whole((8, 512)),
             block(256, 512, lambda i: (2 * lax.div(i, 2), lax.rem(i, 2), 0)),
         ]
         + ups
         + rest,
-        out_specs=(flat(512, 512), flat(256, 512), flat(64, 2048)) + (flat(64, 512),) * 4,
-        compiler_params=pltpu.CompilerParams(vmem_limit_bytes=40 * 2**20),
+        out_specs=(flat(512, 512), flat(64, 512), whole((1, 512)), whole((1, 512)), flat(256, 512), flat(64, 2048)) + (flat(64, 512),) * 4,
+        compiler_params=pltpu.CompilerParams(vmem_limit_bytes=60 * 2**20),
         name="expand",
-    )(slots.reshape(8, 4, 128), gs, came, wgrad, wgrad, wgrad, wgrad, wgrad, wgrad, wgrad, wgrad, wgrad)
-    return out, grad_bytes, wq, wk, wv, wo, up, dn, ggain[0], ggain[1]
+    )(slots.reshape(8, 4, 128), gs, came, out, ggain, wgrad, wgrad, wgrad, wgrad, wgrad, wgrad, wgrad, wgrad, wgrad)
+    return out, grad_bytes, wq, wk, wv, wo, up, dn, g_attn.reshape(512), g_ffn.reshape(512)
 
 
 def passed_along(block, axis, distance):

time: 207 us -> 177 us (0.86)
  Pallas kernels: 193 us -> 173 us
  local copies, waits for them, and re-layouts: 9.54 us -> 0 us
    pallas_call x1, Pallas kernels: 184 us -> 161 us  [fast_local(): pl.pallas_call(layer_kernel, out_shape=(jax.ShapeDtypeStruct((512, 512),...]
    unnamed x11 -> x0, local copies, waits for them, and re-layouts: 6.24 us -> none
    pallas_call x1, Pallas kernels: 9.01 us -> 12.5 us  [fast_local(): pl.pallas_call(expand_kernel, grid=(8,), out_shape=(jax.ShapeDtypeStruct(...]
where the time goes in v2:
time: 177 us; the launch traced here: 174 us
  Pallas kernels  173 us (98%)
    pallas_call x1, Pallas kernels, fast_local(): pl.pallas_call(layer_kernel, out_shape=(jax.ShapeDtypeStruct((512, 512),...  161 us
    pallas_call x1, Pallas kernels, fast_local(): pl.pallas_call(expand_kernel, grid=(8,), out_shape=(jax.ShapeDtypeStruct(...  12.5 us

profile of v2, /device:TPU:9, one launch (start us, length us, event | category | flops | bytes accessed | tf_op | source)
XLA Modules:
  0.0 174.1 jit_solution(5234454674336637536)
XLA Ops:
  0.6 160.8 %layer.1 = (bf16[512,512]{1,0:T(8,128)(2,1)}, bf16[512,512]{1,0:T(8,128)(2,1)}, bf16[16,512]{1,0:T(8,128)(2,1)}, f32[32,128]{1,0:T(8,128)}, bf16[12,512,512]{2,1,0:T(8,128)(2,1)}, /*index=5*/f32[8,512]{1,0:T(8,128)}) custom-call(bf16[4096,512]{1,0:T(8,128)(2,1)} %bytes_hbm.1, s32[32,128]{1,0:T(8,128)} %bitcast.6, s32[1,4]{1,0:T(1,128)} %lengths_ref.1, ...), custom_call_target="tpu_custom_call" | custom-call | tf_op jit(solution)/shard_map/layer/pallas_call | solution.py:1197
  161.5 12.5 %expand.1 = (f32[4096,512]{1,0:T(8,128)}, f32[512,512]{1,0:T(8,128)}, f32[1,512]{1,0:T(1,128)}, f32[1,512]{1,0:T(1,128)}, f32[2048,512]{1,0:T(8,128)}, /*index=5...) custom-call(f32[8,4,128]{2,1,0:T(4,128)} %bitcast.7, ...), custom_call_target="tpu_custom_call" | custom-call | tf_op jit(solution)/shard_map/expand/pallas_call | solution.py:1223

commit v3 on v2

--- a/solution.py
+++ b/solution.py
@@ -97,7 +97,6 @@
     wdn,
     meta,
     tail,
-    slot_sc,
     p_own,
     relay,
     p_all,
@@ -160,7 +159,7 @@
     ynb = (dp + 4 - 8 * y, z)
     g = lax.div(z, 2)
     zl = lax.rem(z, 2)
-    w = 2 * zl + c
+    w = 2 * (1 - zl) + c
     zo = 4 * g + 1 - z
     near = 1 + g
     is_near = z == near
@@ -184,6 +183,9 @@
 
     l_bytes = ids("l", 8)
     rows_chunk = bytes_v.shape[1]
+    l_cot = ids("l", 1)
+    load_cot = pltpu.make_async_copy(cot_hbm, cot_v, ls.at[l_cot])
+    load_cot.start()
     loads_bytes = [
         pltpu.make_async_copy(
             bytes_hbm.at[pl.ds(i * rows_chunk, rows_chunk)], bytes_v.at[i], ls.at[l_bytes + i]
@@ -192,16 +194,11 @@
     ]
     for d in loads_bytes:
         d.start()
-    l_cot = ids("l", 1)
-    load_cot = pltpu.make_async_copy(cot_hbm, cot_v, ls.at[l_cot])
-    load_cot.start()
     l_w = ids("l", 4)
     loads_w = [
         pltpu.make_async_copy(src, weights.at[i], ls.at[l_w + i])
         for i, src in enumerate((wq_hbm, wk_hbm, wv_hbm, wo_hbm))
     ]
-    for d in loads_w:
-        d.start()
     l_f = ids("l", 8)
     loads_f = []
     for j in range(4):
@@ -215,8 +212,6 @@
                 wdn_hbm.at[pl.ds(j * feat, feat)], wdn.at[j], ls.at[l_f + 2 * j + 1]
             )
         )
-    for d in loads_f:
-        d.start()
 
     barrier = pltpu.get_barrier_semaphore()
     me_line = c * nblk + z
@@ -259,6 +254,14 @@
     def _():
         tail[...] = jnp.zeros_like(tail)
 
+    cnt = jnp.sum(flags_ref[...].astype(F32))
+    lane_row = iota((1, feat), 1).astype(F32)
+    live_row = jnp.where(lane_row < cnt, 1.0, 0.0)
+    for d in loads_w:
+        d.start()
+    for d in loads_f:
+        d.start()
+
     upper = (iota((128, 128), 0) <= iota((128, 128), 1)).astype(F32).astype(BF16)
     ones_sq = jnp.ones((128, 128), BF16)
     below = (iota((32, 32), 1) < iota((32, 32), 0)).astype(F32).astype(BF16)
@@ -268,33 +271,32 @@
     row_sums = mm(flags_low, ones_sq, NN)
     row_base = mm(below, row_sums.astype(BF16), NN)
     slot_of = within + row_base - 1.0
-    for k in range(8):
-        slot_sc[k] = slot_of[4 * k : 4 * k + 4, :]
     slots_ref[...] = slot_of
-    cnt = jnp.sum(own_flags)
 
     acc[...] = jnp.zeros_like(acc)
     rdiv[...] = jnp.zeros_like(rdiv)
     slot_iota = iota((feat, 128), 0).astype(F32)
     ones_rows = jnp.ones((16, feat), BF16)
 
-    def pool(k, carry):
-        pltpu.make_async_copy(
-            bytes_hbm.at[pl.ds(0, rows_chunk)], bytes_v.at[k], ls.at[l_bytes + k]
-        ).wait()
-        rows = slot_sc[k]
+    cells = rows_chunk // 8
+    for k in range(8):
+        loads_bytes[k].wait()
+        reach = cells * (k + 1)
         member = jnp.concatenate(
             [
-                (slot_iota == rows[r : r + 1, :]).astype(F32).astype(BF16)
-                for r in range(4)
+                (slot_iota[0:reach] == slot_of[r : r + 1, :]).astype(F32).astype(BF16)
+                for r in range(4 * k, 4 * k + 4)
             ],
             axis=1,
         )
-        acc[...] += mm(member, bytes_v[k], NN)
-        rdiv[...] += mm(ones_rows, member, NT)
-        return carry
-
-    lax.fori_loop(0, 8, pool, 0)
+        acc[0:reach, :] += mm(member, bytes_v[k], NN)
+        rdiv[:, 0:feat] += mm(
+            ones_rows,
+            jnp.concatenate([member, jnp.zeros((feat - reach, rows_chunk), BF16)], axis=0)
+            if reach < feat
+            else member,
+            NT,
+        )
 
     for i, gain in enumerate((gain_attn_ref, gain_ffn_ref)):
         row = jnp.broadcast_to(gain[...], (128, feat))
@@ -318,74 +320,77 @@
     is_last16 = iota((feat, 16), 0).astype(F32) == cnt - 1.0
     member_tail = jnp.where(is_last16, lead[:, 0:16], 0.0).astype(BF16)
     sums = acc[...] + mm(member_tail, tail[...], NN)
-    lane_row = iota((1, feat), 1).astype(F32)
     tally = rdiv[0:1, :] + jnp.where(lane_row == cnt - 1.0, jnp.sum(lead), 0.0)
     inverse_tally = 1.0 / jnp.maximum(tally, 1.0)
     rdiv[0:1, :] = inverse_tally
-    live_row = jnp.where(lane_row < cnt, 1.0, 0.0)
     rdiv[1:2, :] = live_row
     pooled_t = (sums.T * inverse_tally).astype(BF16)
     p_own[0] = pooled_t[:, 0:half]
     p_own[1] = pooled_t[:, half:]
 
-    s_p, r_p, r_relay = ids("s", 9), ids("r", 8), ids("r", 1)
+    s_p, r_p, r_relay = ids("s", 22), ids("r", 16), ids("r", 1)
     near_c = 1 + c
-
-    def p_copy(src, hb, slot, device, cond=None):
-        return Copy(src, p_all.at[hb], ss.at[s_p + slot], rs.at[r_p + hb], device, cond)
+    pieces = (pl.ds(0, half), pl.ds(half, half))
+
+    def p_piece(src, hb, piece, slot, device, cond=None):
+        at = pieces[piece]
+        return Copy(
+            src.at[at],
+            p_all.at[hb, at],
+            ss.at[s_p + slot],
+            rs.at[r_p + 2 * hb + piece],
+            device,
+            cond,
+        )
+
+    def p_whole(src, hb, slot, device, cond=None):
+        return Copy(src, p_all.at[hb], ss.at[s_p + slot], rs.at[r_p + 2 * hb], device, cond)
 
     other_worker = jnp.logical_not(own_worker)
-    go(p_copy(p_own.at[c], 2 * z + c, 0, dev(c, zo), own_worker))
-    go(p_copy(p_own.at[1 - c], 2 * z + 1 - c, 1, sib, own_worker))
-    go(p_copy(p_own.at[c], 2 * z + c, 2, sib, own_worker))
-    go(
-        Copy(p_own.at[1 - c], relay, ss.at[s_p + 1], rs.at[r_relay], sib, other_worker)
-    )
-    go(p_copy(p_own.at[c], 2 * z + c, 2, dev(c, near_c), other_worker))
+    to_pair = z != nblk - 1
+    inner = jnp.logical_or(z == 1, z == 2)
+
+    outer = jnp.logical_not(inner)
+
+    def outside_copies(cond):
+        own_out = jnp.logical_and(other_worker, cond)
+        relayed = jnp.logical_and(own_worker, cond)
+        return [
+            p_piece(p_own.at[c], 2 * z + c, i, 4 + i, dev(c, near_c), own_out) for i in range(2)
+        ] + [p_piece(relay, 2 * z + c, i, 4 + i, dev(c, 2 - c), relayed) for i in range(2)]
+
+    outside_late = outside_copies(outer)
+
+    go(Copy(p_own.at[1 - c], relay, ss.at[s_p + 3], rs.at[r_relay], sib, other_worker))
+    for i in range(2):
+        own_pair = jnp.logical_and(own_worker, to_pair)
+        go(p_piece(p_own.at[c], 2 * z + c, i, i, dev(c, zo), own_pair))
+    go(p_whole(p_own.at[1 - c], 2 * z + 1 - c, 3, sib, own_worker))
+    go(p_whole(p_own.at[c], 2 * z + c, 2, sib, own_worker))
 
     @pl.when(own_worker)
     def _():
         p_all[2 * z] = p_own[0]
         p_all[2 * z + 1] = p_own[1]
 
+    def p_wait(hb, cond=None):
+        Copy(p_all.at[hb], p_all.at[hb], ss.at[0], rs.at[r_p + 2 * hb], sib, cond).wait_recv()
+
     Copy(relay, relay, ss.at[0], rs.at[r_relay], sib, own_worker).wait_recv()
-    go(p_copy(relay, 2 * z + c, 3, dev(c, 2 - c), own_worker))
-
-    def p_wait(hb, cond=None):
-        Copy(p_all.at[hb], p_all.at[hb], ss.at[0], rs.at[r_p + hb], sib, cond).wait_recv()
-
+    for one in outside_copies(inner):
+        go(one)
     p_wait(2 * z + c, other_worker)
-    go(p_copy(p_all.at[2 * z + c], 2 * z + c, 0, dev(c, zo), other_worker))
+    for i in range(2):
+        passed = jnp.logical_and(other_worker, to_pair)
+        go(p_piece(p_all.at[2 * z + c], 2 * z + c, i, i, dev(c, zo), passed))
     p_wait(2 * z + 1 - c, other_worker)
 
     load_cot.wait()
     cot_t = (cot_v[...].T * live_row).astype(BF16)
     cot_own[0] = cot_t[:, 0:half]
     cot_own[1] = cot_t[:, half:]
-    s_cot, r_cot = ids("s", 2), ids("r", 2)
-    early = z < 2
-    slot_to = jnp.where(early, 0, 1)
-    chip_to = 2 * c + jnp.where(early, z, 3 - z)
-    for i in range(2):
-        core_to = jnp.where(early, i, 1 - i)
-        here = jnp.logical_and(core_to == c, chip_to == z)
-        go(
-            Copy(
-                cot_own.at[i],
-                cot_w.at[slot_to],
-                ss.at[s_cot + i],
-                rs.at[r_cot + slot_to],
-                dev(core_to, chip_to),
-                jnp.logical_not(here),
-            )
-        )
-
-        @pl.when(here)
-        def _():
-            cot_w[slot_to] = cot_own[i]
-
-    lo_here = jnp.logical_and(g == c, zl == z)
-    hi_here = jnp.logical_and(g == c, 3 - zl == z)
+    lo_here = False
+    hi_here = jnp.logical_and(g == c, z >= 2)
 
     counts = []
     for b in range(nblk):
@@ -457,30 +462,38 @@
         k_t[hb] = turned(mm(weights[1], normed, TN), hb, 1.0)
         v_t[hb] = mm(weights[2], normed, TN).astype(BF16)
 
-    def both_halves(block):
-        def one(i, carry):
-            keys_values(2 * block + i)
-            return carry
-
-        lax.fori_loop(0, 2, one, 0)
-
-    both_halves(z)
-    for n, block in enumerate((zo, 2 - g, 3 - 3 * g)):
-        p_wait(2 * block + c)
-        if n > 0:
-            go(p_copy(p_all.at[2 * block + c], 2 * block + c, 6 + n, dev(c, zo), is_near))
-        go(p_copy(p_all.at[2 * block + c], 2 * block + c, 4 + n, sib))
-        p_wait(2 * block + 1 - c)
-        both_halves(block)
+    s_cot, r_cot = ids("s", 2), ids("r", 2)
+    early = z < 2
+    slot_to = jnp.where(early, 0, 1)
+    chip_to = 2 * c + 1 - jnp.where(early, z, 3 - z)
+
+    def cot_copy(i):
+        core_to = jnp.where(early, i, 1 - i)
+        here = jnp.logical_and(core_to == c, chip_to == z)
+        return here, Copy(
+            cot_own.at[i],
+            cot_w.at[slot_to],
+            ss.at[s_cot + i],
+            rs.at[r_cot + slot_to],
+            dev(core_to, chip_to),
+            jnp.logical_not(here),
+        )
+
+    def send_cot():
+        for i in range(2):
+            here, copy = cot_copy(i)
+            copy.start()
+
+            @pl.when(here)
+            def _():
+                cot_w[slot_to] = cot_own[i]
 
     hq_of = (w, 7 - w)
+    first_far, second_far = 2 - g, 3 - 3 * g
+    score_scale = HEAD_DIM ** (-0.5) * LOG2E
 
     def hq_at(slot):
         return jnp.where(slot == 0, w, 7 - w)
-
-    for slot in range(2):
-        q_t[slot] = turned(mm(weights[0], n1[hq_of[slot]], TN), hq_of[slot], 1.0)
-    score_scale = HEAD_DIM ** (-0.5) * LOG2E
 
     def bias_of(hq, kb):
         b = lax.div(kb, 2)
@@ -501,10 +514,7 @@
 
     o_new = big.at[1, :, pl.ds(0, half)]
 
-    def forward_step(t, carry):
-        low_half = t <= w
-        slot = jnp.where(low_half, 0, 1)
-        kb = jnp.where(low_half, t, t - w - 1)
+    def forward_step(slot, kb):
         hq = hq_at(slot)
         bias = bias_of(hq, kb)
         old = m_sc[slot]
@@ -528,9 +538,119 @@
         for h in range(HEADS):
             part = slice(64 * h, 64 * h + 64)
             o_acc[slot, part, :] = o_acc[slot, part, :] * shrink[h : h + 1, :] + o_new[part, :]
+
+    def block_nth(n):
+        swapped = jnp.where(n < 2, 1 - n, n)
+        return jnp.where(z == 0, n, jnp.where(z == 1, swapped, z - n))
+
+    def pass_on(block, slot, cond, onward=None):
+        hb = 2 * block + c
+
+        @pl.when(cond)
+        def _():
+            for i in range(2):
+                there = p_all.at[hb, pieces[i]]
+                Copy(there, there, ss.at[0], rs.at[r_p + 2 * hb + i], sib).wait_recv()
+                if onward is not None:
+                    p_piece(p_all.at[hb], hb, i, slot + 2 + i, dev(c, zo), onward).start()
+                p_piece(p_all.at[hb], hb, i, slot + i, sib).start()
+
+    def pass_on_sent():
+        for block, slot, cond, onward in passes:
+            hb = 2 * block + c
+
+            @pl.when(cond)
+            def _(hb=hb, slot=slot, onward=onward):
+                for i in range(2):
+                    if onward is not None:
+                        p_piece(p_all.at[hb], hb, i, slot + 2 + i, dev(c, zo), onward).wait_send()
+                    p_piece(p_all.at[hb], hb, i, slot + i, sib).wait_send()
+
+    second_near = z == 2
+    passes = (
+        (zo, 6, z != 2),
+        (first_far, 8, is_near, is_near),
+        (first_far, 12, jnp.logical_not(is_near)),
+        (second_far, 14, second_near, second_near),
+        (second_far, 18, zl == 1),
+    )
+    passes = tuple(p if len(p) == 4 else p + (None,) for p in passes)
+
+    def arrival(n, carry):
+        block = block_nth(n)
+
+        @pl.when(n == 1)
+        def _():
+            for one in outside_late:
+                one.start()
+            pass_on(*passes[0])
+            pass_on(*passes[1])
+
+        @pl.when(n == 2)
+        def _():
+            pass_on(*passes[2])
+            pass_on(*passes[3])
+
+        @pl.when(n == 3)
+        def _():
+            pass_on(*passes[4])
+            send_cot()
+
+        @pl.when(jnp.logical_and(n > 0, n < 3 + zl))
+        def _():
+            for i in range(2):
+                there = p_all.at[2 * block + 1 - c, pieces[i]]
+                Copy(
+                    there, there, ss.at[0], rs.at[r_p + 2 * (2 * block + 1 - c) + i], sib
+                ).wait_recv()
+
+        @pl.when(n < 3 + zl)
+        def _():
+            def one(i, carry):
+                keys_values(2 * block + i)
+                return carry
+
+            lax.fori_loop(0, 2, one, 0)
+
+            def query(slot, carry):
+                hq = hq_at(slot)
+
+                @pl.when(lax.div(hq, 2) == block)
+                def _():
+                    q_t[slot] = turned(mm(weights[0], n1[hq], TN), hq, 1.0)
+
+                return carry
+
+            lax.fori_loop(0, 2, query, 0)
+
+            def pair(i, carry):
+                slot, kb = lax.div(i, 8), lax.rem(i, 8)
+                hq = hq_at(slot)
+                q_block, k_block = lax.div(hq, 2), lax.div(kb, 2)
+
+                def came_by(b, m):
+                    found = block_nth(0) == b
+                    for k in range(1, 4):
+                        found = jnp.logical_or(
+                            found, jnp.logical_and(block_nth(k) == b, k <= m)
+                        )
+                    return found
+
+                new_query = jnp.logical_and(q_block == block, came_by(k_block, n))
+                new_keys = jnp.logical_and(k_block == block, came_by(q_block, n))
+                new = jnp.logical_or(new_query, new_keys)
+
+                @pl.when(jnp.logical_and(kb <= hq, new))
+                def _():
+                    forward_step(slot, kb)
+
+                return carry
+
+            lax.fori_loop(0, 16, pair, 0)
+
         return carry
 
-    lax.fori_loop(0, 9, forward_step, 0)
+    lax.fori_loop(0, 4, arrival, 0)
 
     for slot in range(2):
         total = l_sc[slot]
@@ -548,9 +668,6 @@
     n2 = (unit2 * gain_col2).astype(BF16)
     big[0] = middle
     big[1] = jnp.zeros((feat, feat), F32)
-    Copy(cot_w.at[0], cot_w.at[0], ss.at[0], rs.at[r_cot], sib, jnp.logical_not(lo_here)).wait_recv()
-    Copy(cot_w.at[1], cot_w.at[1], ss.at[0], rs.at[r_cot + 1], sib, jnp.logical_not(hi_here)).wait_recv()
-    gb[...] = jnp.concatenate([cot_w[0], cot_w[1]], axis=1)
     n2_ref = d_o
     n2_ref[...] = n2
 
@@ -697,7 +814,7 @@
     for d in loads_f:
         d.wait()
 
-    def ffn_chunk(j, carry):
+    def ffn_forward(j, carry):
         up = mm(wup[j], n2_ref[...], TN)
         size = jnp.abs(up) * (0.5**0.5)
         t = 1.0 / (1.0 + 0.3275911 * size)
@@ -710,9 +827,20 @@
         phi = jnp.where(up < 0.0, far, 1.0 - far)
         slope = phi + up * decay * (1.0 / math.sqrt(2.0 * math.pi))
         act = (up * phi).astype(BF16)
-        wg[2 * j] = mm(act, gb[...], NT).astype(BF16)
+        bytes_v[j] = act
+        bytes_v[4 + j] = slope.astype(BF16)
         big[0] += mm(wdn[j], act, TN)
-        grad_up = (mm(wdn[j], gb[...], NN) * slope).astype(BF16)
+        return carry
+
+    lax.fori_loop(0, 4, ffn_forward, 0)
+
+    Copy(cot_w.at[0], cot_w.at[0], ss.at[0], rs.at[r_cot], sib).wait_recv()
+    Copy(cot_w.at[1], cot_w.at[1], ss.at[0], rs.at[r_cot + 1], sib, jnp.logical_not(hi_here)).wait_recv()
+    gb[...] = jnp.concatenate([cot_w[0], cot_w[1]], axis=1)
+
+    def ffn_backward(j, carry):
+        wg[2 * j] = mm(bytes_v[j], gb[...], NT).astype(BF16)
+        grad_up = (mm(wdn[j], gb[...], NN) * bytes_v[4 + j].astype(F32)).astype(BF16)
         wg[2 * j + 1] = mm(n2_ref[...], grad_up, NT).astype(BF16)
         big[1] += mm(wup[j], grad_up, NN)
 
@@ -722,12 +850,12 @@
 
         return carry
 
-    lax.fori_loop(0, 4, ffn_chunk, 0)
+    lax.fori_loop(0, 4, ffn_backward, 0)
     red[0].step(1)
 
     s_out, r_out = ids("s", 2), ids("r", 2)
     res = big[0].astype(BF16)
-    owners = ((zl, c, lo_here), (3 - zl, 1 - c, hi_here))
+    owners = ((1 - zl, c, lo_here), (2 + zl, 1 - c, hi_here))
     for slot, (chip, i, here) in enumerate(owners):
         out_s[slot] = res[:, slot * half : (slot + 1) * half]
         go(
@@ -737,13 +865,14 @@
                 ss.at[s_out + slot],
                 rs.at[r_out + i],
                 dev(g, chip),
-                jnp.logical_not(here),
+                None if here is False else jnp.logical_not(here),
             )
         )
-
-        @pl.when(here)
-        def _():
-            out_r[i] = out_s[slot]
+        if here is not False:
+
+            @pl.when(here)
+            def _():
+                out_r[i] = out_s[slot]
 
     grad_n2 = big[1]
     unit2 = hat2[...]
@@ -830,7 +959,7 @@
             ss.at[s_rz + zb],
             rs.at[r_rz + zb],
             dev(c, zo),
-            jnp.logical_not(is_final(zb)),
+            jnp.logical_and(jnp.logical_not(is_final(zb)), zb < nblk - 1),
         )
 
     def fin_copy(zb):
@@ -852,7 +981,7 @@
 
     def deliver(zb):
         kb = 2 * zb + c
-        final = is_final(zb)
+        final = jnp.logical_and(is_final(zb), zb < nblk - 1)
         Copy(rz.at[zb], rz.at[zb], ss.at[0], rs.at[r_rz + zb], sib, final).wait_recv()
 
         @pl.when(final)
@@ -1072,6 +1201,11 @@
 
     for one in sends:
         one.wait_send()
+    pass_on_sent()
+    for one in outside_late:
+        one.wait_send()
+    for i in range(2):
+        cot_copy(i)[1].wait_send()
 
     def close_key(kb, carry):
         rc_copy(kb).wait_send()
@@ -1094,7 +1228,7 @@
 
 
 def out_from_self(i, c, z):
-    chip = 2 * c + jnp.where(z < 2, z, 3 - z)
+    chip = 2 * c + 1 - jnp.where(z < 2, z, 3 - z)
     core = jnp.where(z < 2, i, 1 - i)
     return jnp.logical_and(core == c, chip == z)
 
@@ -1145,7 +1279,6 @@
         wdn=sq(4, BF16),
         meta=pltpu.VMEM((2, 4, 40, 128), jnp.int32),
         tail=pltpu.VMEM((16, 512), BF16),
-        slot_sc=pltpu.VMEM((8, 4, 128), F32),
         p_own=hb(2),
         relay=pltpu.VMEM((512, 256), BF16),
         p_all=hb(8),
@@ -1190,8 +1323,8 @@
         gain_acc=pltpu.VMEM((2, 512, 128), F32),
         gain_s=pltpu.VMEM((4, 8, 512), F32),
         gain_r=pltpu.VMEM((6, 8, 512), F32),
-        ss=pltpu.SemaphoreType.DMA((128,)),
-        rs=pltpu.SemaphoreType.DMA((128,)),
+        ss=pltpu.SemaphoreType.DMA((160,)),
+        rs=pltpu.SemaphoreType.DMA((160,)),
         ls=pltpu.SemaphoreType.DMA((32,)),
     )
     out, gs, came, slots, wgrad, ggain = pl.pallas_call(

time: 177 us -> 162 us (0.915)
  Pallas kernels: 173 us -> 158 us
    pallas_call x1, Pallas kernels: 161 us -> 146 us  [fast_local(): pl.pallas_call(layer_kernel, out_shape=(jax.ShapeDtypeStruct((512, 512),...]
where the time goes in v3:
time: 162 us; the launch traced here: 159 us
  Pallas kernels  158 us (98%)
    pallas_call x1, Pallas kernels, fast_local(): pl.pallas_call(layer_kernel, out_shape=(jax.ShapeDtypeStruct((512, 512),...  146 us
    pallas_call x1, Pallas kernels, fast_local(): pl.pallas_call(expand_kernel, grid=(8,), out_shape=(jax.ShapeDtypeStruct(...  12.5 us

profile of v3, /device:TPU:9, one launch (start us, length us, event | category | flops | bytes accessed | tf_op | source)
XLA Modules:
  0.0 159.1 jit_solution(17308169017540973529)
XLA Ops:
  0.6 145.8 %layer.1 = (bf16[512,512]{1,0:T(8,128)(2,1)}, bf16[512,512]{1,0:T(8,128)(2,1)}, bf16[16,512]{1,0:T(8,128)(2,1)}, f32[32,128]{1,0:T(8,128)}, bf16[12,512,512]{2,1,0:T(8,128)(2,1)}, /*index=5*/f32[8,512]{1,0:T(8,128)}) custom-call(bf16[4096,512]{1,0:T(8,128)(2,1)} %bytes_hbm.1, s32[32,128]{1,0:T(8,128)} %bitcast.6, s32[1,4]{1,0:T(1,128)} %lengths_ref.1, ...), custom_call_target="tpu_custom_call" | custom-call | tf_op jit(solution)/shard_map/layer/pallas_call | solution.py:1330
  146.5 12.5 %expand.1 = (f32[4096,512]{1,0:T(8,128)}, f32[512,512]{1,0:T(8,128)}, f32[1,512]{1,0:T(1,128)}, f32[1,512]{1,0:T(1,128)}, f32[2048,512]{1,0:T(8,128)}, /*index=5...) custom-call(f32[8,4,128]{2,1,0:T(4,128)} %bitcast.7, ...), custom_call_target="tpu_custom_call" | custom-call | tf_op jit(solution)/shard_map/expand/pallas_call | solution.py:1356

commit v4 on v3

--- a/solution.py
+++ b/solution.py
@@ -67,8 +67,30 @@
         self._do(lambda d: d.wait_recv())
 
 
-CHUNKS = ((0, 4), (4, 9), (9, 12))
-SEMS_AR = 22
+CHUNKS = (
+    (0, 2, "F0"),
+    (2, 4, "F1"),
+    (4, 6, "F2"),
+    (6, 9, "post"),
+    (9, 10, "W"),
+    (10, 12, "W"),
+)
+SEMS_AR = 18
+EARLY = 4
+SCHEDULE = {
+    "F2": ((0, 1), (1, 1)),
+    "F3": ((2, 1),),
+    "K0": ((3, 1),),
+    "K1": ((0, 2), (1, 2)),
+    "K2": ((2, 2),),
+    "K3": ((0, 3), (1, 3)),
+    "K4": ((2, 3), (3, 2)),
+    "K5": ((0, 4), (1, 4), (3, 3)),
+    "K6": ((2, 4),),
+    "K7": ((0, 5), (1, 5), (2, 5), (3, 4), "deliver0"),
+    "R6": ((4, 1), (5, 1)),
+    "end": ("gain0", (0, 6), "deliver1", "out", (1, 6), "gain1", (2, 6), "deliver3", (3, 5), (4, 2), "gain2", (5, 2), (4, 3), (0, 7), "gain3", (1, 7), (2, 7), (4, 4), (5, 3), "gain4", (0, 8), "deliver2", (3, 6), (1, 8), (5, 4), (2, 8), (4, 5), (3, 7), "sums", (4, 6), (5, 5), (0, 9), "came", (0, 10), (4, 7), (5, 6), (1, 9), (3, 8), (2, 9), (4, 8), (1, 10), (5, 7), (2, 10), (4, 9), (5, 8), (4, 10), (3, 9), (3, 10), (5, 9), (5, 10)),
+}
 
 
 def layer_kernel(
@@ -129,6 +151,7 @@
     r2,
     r3,
     r4,
+    r5,
     ppart,
     rc,
     rz,
@@ -676,6 +699,11 @@
     keep2y, give2y = base1 + y * 128, base1 + (1 - y) * 128
     keep3x, give3x = keep2x + y * 64, keep2x + (1 - y) * 64
     keep3y, give3y = keep2y + x * 64, keep2y + (1 - x) * 64
+    keep4x, give4x = keep3x + 32 * zl, keep3x + 32 * (1 - zl)
+    keep4y, give4y = keep3y + 32 * zl, keep3y + 32 * (1 - zl)
+    keep5x, give5x = keep4x + 16 * g, keep4x + 16 * (1 - g)
+    keep5y, give5y = keep4y + 16 * g, keep4y + 16 * (1 - g)
+    znb, zfar = (dp, z + 1 - 2 * zl), (dp, lax.rem(z + 2, nblk))
     lanes_x, lanes_y = pl.ds(0, 256), pl.ds(256, 256)
 
     def rows_of(first, n):
@@ -683,7 +711,7 @@
 
     class Reduce:
         def __init__(self, chunk):
-            self.b0, self.b1 = CHUNKS[chunk]
+            self.b0, self.b1 = CHUNKS[chunk][:2]
             self.nb = self.b1 - self.b0
             self.s0, self.r0 = ids("s", SEMS_AR), ids("r", SEMS_AR)
             self.blocks = pl.ds(self.b0, self.nb)
@@ -712,41 +740,26 @@
                     copy(4, self._w(give3y, 64, lanes_y), r3.at[b, :, lanes_y], xnb),
                 ]
             if phase == 4:
-                out = []
-                for k in range(1, 4):
-                    zt = lax.rem(z + k, nblk)
-                    out.append(
-                        copy(
-                            3 + 2 * k,
-                            self._w(keep3x + 16 * zt, 16, lanes_x),
-                            r4.at[k - 1, b, :, lanes_x],
-                            (dp, zt),
-                        )
-                    )
-                    out.append(
-                        copy(
-                            4 + 2 * k,
-                            self._w(keep3y + 16 * zt, 16, lanes_y),
-                            r4.at[k - 1, b, :, lanes_y],
-                            (dp, zt),
-                        )
-                    )
-                return out
+                return [
+                    copy(5, self._w(give4x, 32, lanes_x), r4.at[b, :, lanes_x], znb),
+                    copy(6, self._w(give4y, 32, lanes_y), r4.at[b, :, lanes_y], znb),
+                ]
             if phase == 5:
-                out = []
-                for k in range(1, 4):
-                    zt = lax.rem(z + k, nblk)
-                    for i, (keep, lanes) in enumerate(((keep3x, lanes_x), (keep3y, lanes_y))):
-                        mine = self._f(keep + 16 * z, 16, lanes)
-                        out.append(copy(9 + 2 * k + i, mine, mine, (dp, zt)))
-                return out
-            if phase == 6:
-                mine_x, mine_y = self._f(keep3x, 64, lanes_x), self._f(keep3y, 64, lanes_y)
-                return [copy(17, mine_x, mine_x, ynb), copy(18, mine_y, mine_y, xnb)]
-            if phase == 7:
-                mine_x, mine_y = self._f(keep2x, 128, lanes_x), self._f(keep2y, 128, lanes_y)
-                return [copy(19, mine_x, mine_x, xnb), copy(20, mine_y, mine_y, ynb)]
-            return [copy(21, r1.at[b], self._out(base1), sib)]
+                return [
+                    copy(7, self._w(give5x, 16, lanes_x), r5.at[b, :, lanes_x], zfar),
+                    copy(8, self._w(give5y, 16, lanes_y), r5.at[b, :, lanes_y], zfar),
+                ]
+            if phase < 10:
+                keep_x, keep_y, n, to_x, to_y = (
+                    (keep5x, keep5y, 16, zfar, zfar),
+                    (keep4x, keep4y, 32, znb, znb),
+                    (keep3x, keep3y, 64, ynb, xnb),
+                    (keep2x, keep2y, 128, xnb, ynb),
+                )[phase - 6]
+                mine_x, mine_y = self._f(keep_x, n, lanes_x), self._f(keep_y, n, lanes_y)
+                first = 2 * phase - 3
+                return [copy(first, mine_x, mine_x, to_x), copy(first + 1, mine_y, mine_y, to_y)]
+            return [copy(17, r1.at[b], self._out(base1), sib)]
 
         def _f(self, first, n, lanes):
             return r1.at[self.blocks, rows_of(first - base1, n), lanes]
@@ -759,13 +772,13 @@
                 one.start()
 
         def finish(self, phase):
-            if phase == 8:
+            if phase == 10:
                 other = self._out((1 - c) * 256)
-                Copy(other, other, ss.at[0], rs.at[self.r0 + 21], sib).wait_recv()
+                Copy(other, other, ss.at[0], rs.at[self.r0 + 17], sib).wait_recv()
                 return
             for one in self._list(phase):
                 one.wait_recv()
-            if phase > 4:
+            if phase > 5:
                 return
 
             def add(i, carry):
@@ -782,37 +795,74 @@
                         here = (b, rows_of(keep, 64), slice(lo, lo + 256))
                         wg[here] = wg[here] + r3[b, :, lo : lo + 256]
                 if phase == 4:
-                    for keep, lo in ((keep3x, 0), (keep3y, 256)):
-                        here = (b, rows_of(keep + 16 * z, 16), slice(lo, lo + 256))
-                        total = wg[here].astype(F32)
-                        for k in range(3):
-                            total = total + r4[k, b, :, lo : lo + 256].astype(F32)
-                        r1[b, rows_of(keep - base1 + 16 * z, 16), lo : lo + 256] = total.astype(BF16)
+                    for keep, lo in ((keep4x, 0), (keep4y, 256)):
+                        here = (b, rows_of(keep, 32), slice(lo, lo + 256))
+                        wg[here] = wg[here] + r4[b, :, lo : lo + 256]
+                if phase == 5:
+                    for keep, lo in ((keep5x, 0), (keep5y, 256)):
+                        total = wg[b, rows_of(keep, 16), lo : lo + 256] + r5[b, :, lo : lo + 256]
+                        r1[b, rows_of(keep - base1, 16), lo : lo + 256] = total
                 return carry
 
             lax.fori_loop(0, self.nb, add, 0)
 
         def step(self, phase):
             self.finish(phase)
-            if phase < 8:
-                self.start(phase + 1)
-            if phase == 7:
+            if phase < 10:
+                self.begin(phase + 1)
+
+        def begin(self, phase):
+            self.start(phase)
+            if phase == 10:
                 self.store().start()
 
         def store(self):
             return pltpu.make_async_copy(r1.at[self.blocks], self._out(base1), ls.at[self.store_sem])
 
         def wait_sends(self):
-            for phase in range(1, 9):
+            for phase in range(1, 11):
                 for one in self._list(phase):
                     one.wait_send()
 
-    red = [Reduce(i) for i in range(3)]
+    red = [Reduce(i) for i in range(len(CHUNKS))]
     for one in red:
         one.store_sem = ids("l", 1)
 
     for d in loads_f:
         d.wait()
+
+    def do(item):
+        if not isinstance(item, str):
+            if item[0] == "f":
+                red[item[1]].finish(item[2])
+            elif item[0] == "s":
+                red[item[1]].begin(item[2])
+            else:
+                red[item[0]].step(item[1])
+        elif item == "gain0":
+            gains_start()
+        elif item.startswith("gain"):
+            gain_finish(int(item[4:]))
+        elif item.startswith("deliver"):
+            deliver(int(item[7:]))
+        else:
+            {"out": finish_output, "sums": finish_sums, "came": finish_came}[item]()
+
+    def run_after(name, index=None):
+        if index is None:
+            for (_, _, when), one in zip(CHUNKS, red):
+                if when == name:
+                    one.start(1)
+            for item in SCHEDULE.get(name, ()):
+                do(item)
+            return
+        for i in range(9):
+            full = name + str(i)
+            if full in SCHEDULE or any(when == full for _, _, when in CHUNKS):
+
+                @pl.when(index == i)
+                def _():
+                    run_after(full)
 
     def ffn_forward(j, carry):
         up = mm(wup[j], n2_ref[...], TN)
@@ -843,15 +893,10 @@
         grad_up = (mm(wdn[j], gb[...], NN) * bytes_v[4 + j].astype(F32)).astype(BF16)
         wg[2 * j + 1] = mm(n2_ref[...], grad_up, NT).astype(BF16)
         big[1] += mm(wup[j], grad_up, NN)
-
-        @pl.when(j == 1)
-        def _():
-            red[0].start(1)
-
+        run_after("F", j)
         return carry
 
     lax.fori_loop(0, 4, ffn_backward, 0)
-    red[0].step(1)
 
     s_out, r_out = ids("s", 2), ids("r", 2)
     res = big[0].astype(BF16)
@@ -895,7 +940,7 @@
     gmid[1] = grad_mid[:, half:]
     branch = grad_mid.astype(BF16)
     wg[8] = mm(att[...], branch, NT).astype(BF16)
-    red[1].start(1)
+    run_after("post")
     grad_att = mm(weights[3], branch, NN)
     d_o[...] = grad_att.astype(BF16)
     for slot in range(2):
@@ -994,122 +1039,6 @@
 
         fin_copy(zb).start()
 
-    def ticks(at, schedule):
-        for i, todo in schedule.items():
-
-            @pl.when(at == i)
-            def _():
-                for chunk, phase in todo:
-                    red[chunk].step(phase)
-
-    def key_block(kb, carry):
-        @pl.when(kb <= 7 - w)
-        def _():
-            dk[...] = jnp.zeros_like(dk)
-            dv[...] = jnp.zeros_like(dv)
-
-            def one(i, carry):
-                backward_step(1 - i, kb)
-                return carry
-
-            lax.fori_loop(0, jnp.where(kb <= w, 2, 1), one, 0)
-            grad_key = turned(dk[...] * att_scale, kb, -1.0)
-            grad_value = dv[...].astype(BF16)
-            normed = n1[kb]
-            k_t[kb] = grad_key
-            v_t[kb] = grad_value
-            gwqkv[1] += mm(normed, grad_key, NT)
-            gwqkv[2] += mm(normed, grad_value, NT)
-
-            @pl.when(jnp.logical_or(kb == w, kb == 7 - w))
-            def _():
-                slot = jnp.where(kb == w, 0, 1)
-                grad_query = turned(dq[slot] * att_scale, kb, -1.0)
-                q_t[slot] = grad_query
-                gwqkv[0] += mm(normed, grad_query, NT)
-
-        ticks(
-            kb,
-            {
-                0: [(1, 1)],
-                1: [(0, 2)],
-                2: [(0, 3)],
-                3: [(1, 2)],
-                4: [(0, 4)],
-                5: [(1, 3)],
-                6: [(0, 5)],
-                7: [(0, 6)],
-            },
-        )
-        return carry
-
-    lax.fori_loop(0, 8, key_block, 0)
-    for i in range(3):
-        wg[9 + i] = gwqkv[i].astype(BF16)
-    red[2].start(1)
-
-    def block_at(j):
-        return jnp.where(g == 0, 3 - j, j)
-
-    def row_block(i, carry):
-        j = lax.div(i, 2)
-        kb = 2 * block_at(j) + lax.rem(i, 2)
-
-        @pl.when(kb <= 7 - w)
-        def _():
-            big[0, :, 0:half] = mm(weights[1], k_t[kb], NN) + mm(weights[2], v_t[kb], NN)
-            own = jnp.logical_or(kb == w, kb == 7 - w)
-            slot = jnp.where(kb == w, 0, 1)
-
-            @pl.when(own)
-            def _():
-                big[0, :, 0:half] += mm(weights[0], q_t[slot], NN)
-
-            grad_n1 = big[0, :, 0:half]
-            unit, inverse = norm_parts(p_all[kb].astype(F32))
-            gain_acc[0] += lane_fold(grad_n1 * unit)
-            e = grad_n1 * gcol[0]
-            total = inverse * (
-                e
-                - jnp.mean(e, axis=0, keepdims=True)
-                - unit * jnp.mean(e * unit, axis=0, keepdims=True)
-            )
-            ppart[kb] = (total + jnp.where(own, 1.0, 0.0) * gmid[slot]).astype(BF16)
-
-        @pl.when(kb > 7 - w)
-        def _():
-            ppart[kb] = jnp.zeros(ppart.shape[1:], BF16)
-
-        rc_copy(kb).start()
-
-        @pl.when(lax.rem(i, 2) == 1)
-        def _():
-            combine(block_at(j))
-
-        @pl.when(jnp.logical_and(lax.rem(i, 2) == 1, i > 1))
-        def _():
-            deliver(block_at(j - 1))
-
-        ticks(
-            i,
-            {
-                0: [(2, 1)],
-                1: [(1, 4)],
-                2: [(0, 7)],
-                3: [(2, 2)],
-                4: [(1, 5)],
-                5: [(0, 8)],
-                6: [(2, 3)],
-                7: [(1, 6)],
-            },
-        )
-        return carry
-
-    lax.fori_loop(0, 8, row_block, 0)
-
-    for i in range(2):
-        gain_s[0, i : i + 1, :] = jnp.sum(gain_acc[i].T, axis=0, keepdims=True)
-    gain_s[0, 2:8, :] = jnp.zeros((6, feat), F32)
     s_gain, r_gain = ids("s", 6), ids("r", 6)
 
     def gain_list(phase):
@@ -1147,33 +1076,12 @@
                 total = total + part
             ggain_ref[...] = total
 
-    gain_list(1)[0].start()
-    red[2].step(4)
-    deliver(block_at(3))
-    gain_finish(1)
-    red[1].step(7)
-
-    for i in range(2):
-        mine = out_from_self(i, c, z)
-        Copy(
-            out_r.at[i], out_r.at[i], ss.at[0], rs.at[r_out + i], sib, jnp.logical_not(mine)
-        ).wait_recv()
-        live = rdiv[1:2, i * half : (i + 1) * half]
-        out_ref[i * half : (i + 1) * half, :] = (out_r[i].astype(F32) * live).T.astype(BF16)
-
-    gain_finish(2)
-    red[2].step(5)
-
-    for i in range(2):
-        mine = jnp.logical_and(own_worker, c == i)
-        Copy(
-            gfin.at[i], gfin.at[i], ss.at[0], rs.at[r_fin + i], sib, jnp.logical_not(mine)
-        ).wait_recv()
-        grad_sums = gfin[i].astype(F32) * rdiv[0:1, i * half : (i + 1) * half]
-        gs_ref[i * half : (i + 1) * half, :] = grad_sums.T.astype(BF16)
-
-    is_last = jnp.where(iota((16, feat), 1).astype(F32) == cnt - 1.0, 1.0, 0.0).astype(BF16)
-    last_s[...] = mm(is_last, gs_ref[...], NN).astype(BF16)
+    def gains_start():
+        for i in range(2):
+            gain_s[0, i : i + 1, :] = jnp.sum(gain_acc[i].T, axis=0, keepdims=True)
+        gain_s[0, 2:8, :] = jnp.zeros((6, feat), F32)
+        gain_list(1)[0].start()
+
     s_last, r_last = ids("s", 1), ids("r", 1)
     copy_last = Copy(
         last_s,
@@ -1183,25 +1091,126 @@
         (dp, lax.rem(z + 1, nblk)),
         z < nblk - 1,
     )
-    go(copy_last)
-
-    red[1].step(8)
-    gain_finish(3)
-    red[2].step(6)
-    gain_finish(4)
-    Copy(last_r, last_r, ss.at[0], rs.at[r_last], sib, z > 0).wait_recv()
-
-    @pl.when(z == 0)
-    def _():
-        last_r[...] = jnp.zeros_like(last_r)
-
-    came_ref[...] = last_r[...]
-    for phase in range(7, 9):
-        red[2].step(phase)
+
+    def finish_output():
+        for i in range(2):
+            mine = out_from_self(i, c, z)
+            Copy(
+                out_r.at[i], out_r.at[i], ss.at[0], rs.at[r_out + i], sib, jnp.logical_not(mine)
+            ).wait_recv()
+            live = rdiv[1:2, i * half : (i + 1) * half]
+            out_ref[i * half : (i + 1) * half, :] = (out_r[i].astype(F32) * live).T.astype(BF16)
+
+    def finish_sums():
+        for i in range(2):
+            mine = jnp.logical_and(own_worker, c == i)
+            Copy(
+                gfin.at[i], gfin.at[i], ss.at[0], rs.at[r_fin + i], sib, jnp.logical_not(mine)
+            ).wait_recv()
+            grad_sums = gfin[i].astype(F32) * rdiv[0:1, i * half : (i + 1) * half]
+            gs_ref[i * half : (i + 1) * half, :] = grad_sums.T.astype(BF16)
+
+        is_last = jnp.where(iota((16, feat), 1).astype(F32) == cnt - 1.0, 1.0, 0.0).astype(BF16)
+        last_s[...] = mm(is_last, gs_ref[...], NN).astype(BF16)
+        copy_last.start()
+
+    def finish_came():
+        Copy(last_r, last_r, ss.at[0], rs.at[r_last], sib, z > 0).wait_recv()
+
+        @pl.when(z == 0)
+        def _():
+            last_r[...] = jnp.zeros_like(last_r)
+
+        came_ref[...] = last_r[...]
+
+    def key_step(t, carry):
+        both = t < 2 * w + 2
+        kb = jnp.where(both, lax.div(t, 2), t - w - 1)
+        slot = jnp.where(both, 1 - lax.rem(t, 2), 1)
+        first = jnp.logical_or(jnp.logical_not(both), lax.rem(t, 2) == 0)
+        last = jnp.logical_or(jnp.logical_not(both), lax.rem(t, 2) == 1)
+
+        @pl.when(first)
+        def _():
+            dk[...] = jnp.zeros_like(dk)
+            dv[...] = jnp.zeros_like(dv)
+
+        backward_step(slot, kb)
+
+        @pl.when(last)
+        def _():
+            grad_key = turned(dk[...] * att_scale, kb, -1.0)
+            grad_value = dv[...].astype(BF16)
+            normed = n1[kb]
+            k_t[kb] = grad_key
+            v_t[kb] = grad_value
+            gwqkv[1] += mm(normed, grad_key, NT)
+            gwqkv[2] += mm(normed, grad_value, NT)
+
+            @pl.when(jnp.logical_or(kb == w, kb == 7 - w))
+            def _():
+                slot = jnp.where(kb == w, 0, 1)
+                grad_query = turned(dq[slot] * att_scale, kb, -1.0)
+                q_t[slot] = grad_query
+                gwqkv[0] += mm(normed, grad_query, NT)
+
+
+        @pl.when(jnp.logical_and(lax.rem(t, 2) == 1, t < 2 * EARLY))
+        def _():
+            row_block(lax.div(t, 2))
+
+        run_after("K", t)
+        return carry
+
+    def row_block(kb):
+        @pl.when(kb <= 7 - w)
+        def _():
+            big[0, :, 0:half] = mm(weights[1], k_t[kb], NN) + mm(weights[2], v_t[kb], NN)
+            own = jnp.logical_or(kb == w, kb == 7 - w)
+            slot = jnp.where(kb == w, 0, 1)
+
+            @pl.when(own)
+            def _():
+                big[0, :, 0:half] += mm(weights[0], q_t[slot], NN)
+
+            grad_n1 = big[0, :, 0:half]
+            unit, inverse = norm_parts(p_all[kb].astype(F32))
+            gain_acc[0] += lane_fold(grad_n1 * unit)
+            e = grad_n1 * gcol[0]
+            total = inverse * (
+                e
+                - jnp.mean(e, axis=0, keepdims=True)
+                - unit * jnp.mean(e * unit, axis=0, keepdims=True)
+            )
+            ppart[kb] = (total + jnp.where(own, 1.0, 0.0) * gmid[slot]).astype(BF16)
+
+        @pl.when(kb > 7 - w)
+        def _():
+            ppart[kb] = jnp.zeros(ppart.shape[1:], BF16)
+
+        rc_copy(kb).start()
+
+        @pl.when(lax.rem(kb, 2) == 1)
+        def _():
+            combine(lax.div(kb, 2))
+
+    def late_row_block(kb, carry):
+        row_block(kb)
+        run_after("R", kb)
+        return carry
+
+    lax.fori_loop(0, 9, key_step, 0)
+    for i in range(3):
+        wg[9 + i] = gwqkv[i].astype(BF16)
+    run_after("W")
+    lax.fori_loop(EARLY, 8, late_row_block, 0)
+
+    run_after("end")
 
     for one in sends:
         one.wait_send()
     pass_on_sent()
+    copy_last.wait_send()
     for one in outside_late:
         one.wait_send()
     for i in range(2):
@@ -1310,7 +1319,8 @@
         r1=pltpu.VMEM((12, 256, 512), BF16),
         r2=pltpu.VMEM((12, 128, 512), BF16),
         r3=pltpu.VMEM((12, 64, 512), BF16),
-        r4=pltpu.VMEM((3, 12, 16, 512), BF16),
+        r4=pltpu.VMEM((12, 32, 512), BF16),
+        r5=pltpu.VMEM((12, 16, 512), BF16),
         ppart=hb(8),
         rc=hb(4),
         rz=hb(4),
@@ -1323,8 +1333,8 @@
         gain_acc=pltpu.VMEM((2, 512, 128), F32),
         gain_s=pltpu.VMEM((4, 8, 512), F32),
         gain_r=pltpu.VMEM((6, 8, 512), F32),
-        ss=pltpu.SemaphoreType.DMA((160,)),
-        rs=pltpu.SemaphoreType.DMA((160,)),
+        ss=pltpu.SemaphoreType.DMA((224,)),
+        rs=pltpu.SemaphoreType.DMA((224,)),
         ls=pltpu.SemaphoreType.DMA((32,)),
     )
     out, gs, came, slots, wgrad, ggain = pl.pallas_call(

time: 162 us -> 154 us (0.951); the launches traced: 159 us -> 154 us
  Pallas kernels: 158 us -> 153 us
    pallas_call x1, Pallas kernels: 146 us -> 140 us  [fast_local(): pl.pallas_call(layer_kernel, out_shape=(jax.ShapeDtypeStruct((512, 512),...]
where the time goes in v4:
time: 154 us
  Pallas kernels  153 us (99%)
    pallas_call x1, Pallas kernels, fast_local(): pl.pallas_call(layer_kernel, out_shape=(jax.ShapeDtypeStruct((512, 512),...  140 us
    pallas_call x1, Pallas kernels, fast_local(): pl.pallas_call(expand_kernel, grid=(8,), out_shape=(jax.ShapeDtypeStruct(...  12.5 us

profile of v4, /device:TPU:9, one launch (start us, length us, event | category | flops | bytes accessed | tf_op | source)
XLA Modules:
  0.0 153.5 jit_solution(12702045752159866975)
XLA Ops:
  0.6 140.2 %layer.1 = (bf16[512,512]{1,0:T(8,128)(2,1)}, bf16[512,512]{1,0:T(8,128)(2,1)}, bf16[16,512]{1,0:T(8,128)(2,1)}, f32[32,128]{1,0:T(8,128)}, bf16[12,512,512]{2,1,0:T(8,128)(2,1)}, /*index=5*/f32[8,512]{1,0:T(8,128)}) custom-call(bf16[4096,512]{1,0:T(8,128)(2,1)} %bytes_hbm.1, s32[32,128]{1,0:T(8,128)} %bitcast.6, s32[1,4]{1,0:T(1,128)} %lengths_ref.1, ...), custom_call_target="tpu_custom_call" | custom-call | tf_op jit(solution)/shard_map/layer/pallas_call | solution.py:1340
  140.9 12.5 %expand.1 = (f32[4096,512]{1,0:T(8,128)}, f32[512,512]{1,0:T(8,128)}, f32[1,512]{1,0:T(1,128)}, f32[1,512]{1,0:T(1,128)}, f32[2048,512]{1,0:T(8,128)}, /*index=5...) custom-call(f32[8,4,128]{2,1,0:T(4,128)} %bitcast.7, ...), custom_call_target="tpu_custom_call" | custom-call | tf_op jit(solution)/shard_map/expand/pallas_call | solution.py:1366

commit v5 on v4

--- a/solution.py
+++ b/solution.py
@@ -87,9 +87,10 @@
     "K4": ((2, 3), (3, 2)),
     "K5": ((0, 4), (1, 4), (3, 3)),
     "K6": ((2, 4),),
-    "K7": ((0, 5), (1, 5), (2, 5), (3, 4), "deliver0"),
+    "K7": ((0, 5), (3, 4), "deliver0", (2, 5)),
+    "R4": ((1, 5),),
     "R6": ((4, 1), (5, 1)),
-    "end": ("gain0", (0, 6), "deliver1", "out", (1, 6), "gain1", (2, 6), "deliver3", (3, 5), (4, 2), "gain2", (5, 2), (4, 3), (0, 7), "gain3", (1, 7), (2, 7), (4, 4), (5, 3), "gain4", (0, 8), "deliver2", (3, 6), (1, 8), (5, 4), (2, 8), (4, 5), (3, 7), "sums", (4, 6), (5, 5), (0, 9), "came", (0, 10), (4, 7), (5, 6), (1, 9), (3, 8), (2, 9), (4, 8), (1, 10), (5, 7), (2, 10), (4, 9), (5, 8), (4, 10), (3, 9), (3, 10), (5, 9), (5, 10)),
+    "end": ("gain0", (0, 6), "deliver1", "out", (1, 6), "deliver3", "gain1", (2, 6), (3, 5), (4, 2), "gain2", (5, 2), (4, 3), (0, 7), "gain3", (1, 7), (2, 7), (4, 4), (5, 3), "gain4", (0, 8), "deliver2", (3, 6), (1, 8), (5, 4), (2, 8), (4, 5), (3, 7), "sums", (4, 6), (5, 5), (0, 9), "came", (0, 10), (4, 7), (5, 6), (1, 9), (3, 8), (2, 9), (4, 8), (1, 10), (5, 7), (2, 10), (4, 9), (5, 8), (4, 10), (3, 9), (3, 10), (5, 9), (5, 10)),
 }
 
 
@@ -246,23 +247,27 @@
         pl.semaphore_signal(barrier, inc=1, device_id=dev(core, zz), device_id_type=MESH)
     for d in (xnb, ynb):
         pl.semaphore_signal(barrier, inc=1, device_id=d, device_id_type=MESH)
-    pl.semaphore_wait(barrier, 9)
-
-    meta[c, z, 0:32, :] = flags_ref[...]
-    meta[c, z, 32:40, :] = jnp.zeros((8, 128), jnp.int32)
-    meta[c, z, 32:33, 0:4] = lengths_ref[...]
+
+    cnt = jnp.sum(flags_ref[...].astype(F32))
+    lane_row = iota((1, feat), 1).astype(F32)
+    live_row = jnp.where(lane_row < cnt, 1.0, 0.0)
+    for d in loads_w:
+        d.start()
+    for d in loads_f:
+        d.start()
+
     s_meta, r_meta = ids("s", 7), ids("r", 8)
-    for k, (core, zz) in enumerate(line):
-        go(
-            Copy(
-                meta.at[c, z],
-                meta.at[c, z],
-                ss.at[s_meta + k],
-                rs.at[r_meta + me_line],
-                dev(core, zz),
-            )
-        )
     s_tail, r_tail = ids("s", 1), ids("r", 1)
+    copies_meta = [
+        Copy(
+            meta.at[c, z],
+            meta.at[c, z],
+            ss.at[s_meta + k],
+            rs.at[r_meta + me_line],
+            dev(core, zz),
+        )
+        for k, (core, zz) in enumerate(line)
+    ]
     copy_tail = Copy(
         bytes_hbm.at[pl.ds(0, 16)],
         tail,
@@ -271,19 +276,19 @@
         (dp, lax.rem(z + nblk - 1, nblk)),
         z > 0,
     )
-    go(copy_tail)
-
-    @pl.when(z == nblk - 1)
-    def _():
-        tail[...] = jnp.zeros_like(tail)
-
-    cnt = jnp.sum(flags_ref[...].astype(F32))
-    lane_row = iota((1, feat), 1).astype(F32)
-    live_row = jnp.where(lane_row < cnt, 1.0, 0.0)
-    for d in loads_w:
-        d.start()
-    for d in loads_f:
-        d.start()
+
+    def enter():
+        pl.semaphore_wait(barrier, 9)
+        meta[c, z, 0:32, :] = flags_ref[...]
+        meta[c, z, 32:40, :] = jnp.zeros((8, 128), jnp.int32)
+        meta[c, z, 32:33, 0:4] = lengths_ref[...]
+        for one in copies_meta:
+            go(one)
+        go(copy_tail)
+
+        @pl.when(z == nblk - 1)
+        def _():
+            tail[...] = jnp.zeros_like(tail)
 
     upper = (iota((128, 128), 0) <= iota((128, 128), 1)).astype(F32).astype(BF16)
     ones_sq = jnp.ones((128, 128), BF16)
@@ -300,6 +305,8 @@
     rdiv[...] = jnp.zeros_like(rdiv)
     slot_iota = iota((feat, 128), 0).astype(F32)
     ones_rows = jnp.ones((16, feat), BF16)
+
+    enter()
 
     cells = rows_chunk // 8
     for k in range(8):
@@ -1243,31 +1250,60 @@
 
 
 def expand_kernel(
-    slots_ref, gs_ref, came_ref, out_ref, ggain_ref, dn_ref, up0, up1, up2, up3, wo_ref, wq_ref, wk_ref, wv_ref,
+    slots_ref, gs_ref, came_ref, out_ref, ggain_ref, w_hbm,
     bytes_out, out_out, ga_out, gf_out, dn_out, up_out, wo_out, wq_out, wk_out, wv_out,
+    w_v, bytes_v, out_v, dn_v, up_v, rest_v, sem_in, sem_out,
 ):
-    rows = slots_ref[0]
-    slot_iota = iota((512, 128), 0).astype(F32)
-    member = jnp.concatenate(
-        [(slot_iota == rows[r : r + 1, :]).astype(F32).astype(BF16) for r in range(4)], axis=1
-    )
-    first = iota((16, 128), 0) == 0
-    lead = jnp.concatenate(
-        [
-            jnp.where(jnp.logical_and(first, rows[r : r + 1, :] < -0.5), 1.0, 0.0).astype(BF16)
-            for r in range(4)
-        ],
-        axis=1,
-    )
-    bytes_out[...] = mm(member, gs_ref[...], TN) + mm(lead, came_ref[...], TN)
-    out_out[...] = out_ref[...].astype(F32)
+    loads = [pltpu.make_async_copy(w_hbm.at[i], w_v.at[i], sem_in.at[i]) for i in range(12)]
+    for one in loads:
+        one.start()
+    stores = []
+
+    def store(src, dst):
+        copy = pltpu.make_async_copy(src, dst, sem_out.at[len(stores)])
+        copy.start()
+        stores.append(copy)
+
+    out_v[...] = out_ref[...].astype(F32)
+    store(out_v, out_out)
     ga_out[...] = ggain_ref[0:1, :]
     gf_out[...] = ggain_ref[1:2, :]
-    dn_out[...] = dn_ref[0].astype(F32)
-    for j, up in enumerate((up0, up1, up2, up3)):
-        up_out[:, 512 * j : 512 * (j + 1)] = up[0].astype(F32)
-    for src, dst in ((wo_ref, wo_out), (wq_ref, wq_out), (wk_ref, wk_out), (wv_ref, wv_out)):
-        dst[...] = src[0].astype(F32)
+    slot_iota = iota((512, 128), 0).astype(F32)
+    first = iota((16, 128), 0) == 0
+
+    def weights(j):
+        loads[2 * j].wait()
+        dn_v[j] = w_v[2 * j].astype(F32)
+        store(dn_v.at[j], dn_out.at[pl.ds(512 * j, 512)])
+        loads[2 * j + 1].wait()
+        up_v[j] = w_v[2 * j + 1].astype(F32)
+        store(up_v.at[j], up_out.at[:, pl.ds(512 * j, 512)])
+
+    for k in range(8):
+        rows = [slots_ref[4 * k + r : 4 * k + r + 1, :] for r in range(4)]
+        member = jnp.concatenate(
+            [(slot_iota == row).astype(F32).astype(BF16) for row in rows], axis=1
+        )
+        spread = mm(member, gs_ref[...], TN)
+        if k == 0:
+            lead = jnp.concatenate(
+                [
+                    jnp.where(jnp.logical_and(first, row < -0.5), 1.0, 0.0).astype(BF16)
+                    for row in rows
+                ],
+                axis=1,
+            )
+            spread = spread + mm(lead, came_ref[...], TN)
+        bytes_v[k] = spread
+        store(bytes_v.at[k], bytes_out.at[pl.ds(512 * k, 512)])
+        if k % 2 == 1:
+            weights(k // 2)
+    for i, dst in enumerate((wo_out, wq_out, wk_out, wv_out)):
+        loads[8 + i].wait()
+        rest_v[i] = w_v[8 + i].astype(F32)
+        store(rest_v.at[i], dst)
+    for one in stores:
+        one.wait()
 
 
 def fast_local(
@@ -1358,14 +1394,8 @@
         bytes_in, meta_flags, lengths, cotangent, w_query, w_key, w_value, w_out, w_up, w_down,
         gain_attn.reshape(1, 512), gain_ffn.reshape(1, 512), freq,
     )
-    block = lambda rows, cols, index: pl.BlockSpec((1, rows, cols), index)
-    ups = [block(64, 512, functools.partial(lambda j, i: (2 * j + 1, i, 0), j)) for j in range(4)]
-    rest = [block(64, 512, functools.partial(lambda j, i: (j, i, 0), j)) for j in range(8, 12)]
-    whole = lambda shape: pl.BlockSpec(shape, lambda i: (0, 0))
-    flat = lambda rows, cols: pl.BlockSpec((rows, cols), lambda i: (i, 0))
     grad_bytes, out, g_attn, g_ffn, dn, up, wo, wq, wk, wv = pl.pallas_call(
         expand_kernel,
-        grid=(8,),
         out_shape=(
             jax.ShapeDtypeStruct((4096, 512), F32),
             jax.ShapeDtypeStruct((512, 512), F32),
@@ -1375,20 +1405,21 @@
             jax.ShapeDtypeStruct((512, 2048), F32),
         )
         + (jax.ShapeDtypeStruct((512, 512), F32),) * 4,
-        in_specs=[
-            block(4, 128, lambda i: (i, 0, 0)),
-            whole((512, 512)),
-            whole((16, 512)),
-            flat(64, 512),
-            whole((8, 512)),
-            block(256, 512, lambda i: (2 * lax.div(i, 2), lax.rem(i, 2), 0)),
-        ]
-        + ups
-        + rest,
-        out_specs=(flat(512, 512), flat(64, 512), whole((1, 512)), whole((1, 512)), flat(256, 512), flat(64, 2048)) + (flat(64, 512),) * 4,
+        in_specs=[vm, vm, vm, vm, vm, hbm],
+        out_specs=(hbm, hbm, vm, vm) + (hbm,) * 6,
+        scratch_shapes=[
+            sq(12, BF16),
+            sq(8, F32),
+            pltpu.VMEM((512, 512), F32),
+            sq(4, F32),
+            sq(4, F32),
+            sq(4, F32),
+            pltpu.SemaphoreType.DMA((12,)),
+            pltpu.SemaphoreType.DMA((24,)),
+        ],
         compiler_params=pltpu.CompilerParams(vmem_limit_bytes=60 * 2**20),
         name="expand",
-    )(slots.reshape(8, 4, 128), gs, came, out, ggain, wgrad, wgrad, wgrad, wgrad, wgrad, wgrad, wgrad, wgrad, wgrad)
+    )(slots, gs, came, out, ggain, wgrad)
     return out, grad_bytes, wq, wk, wv, wo, up, dn, g_attn.reshape(512), g_ffn.reshape(512)
 
 

time: 154 us -> 153 us (level)
  no operation moved by 1% of the time
where the time goes in v5:
time: 153 us; the launch traced here: 152 us
  Pallas kernels  152 us (99%)
    pallas_call x1, Pallas kernels, fast_local(): pl.pallas_call(layer_kernel, out_shape=(jax.ShapeDtypeStruct((512, 512),...  140 us
    pallas_call x1, Pallas kernels, fast_local(): pl.pallas_call(expand_kernel, out_shape=(jax.ShapeDtypeStruct((4096, 512)...  11.9 us

profile of v5, /device:TPU:9, one launch (start us, length us, event | category | flops | bytes accessed | tf_op | source)
XLA Modules:
  0.0 152.4 jit_solution(1061824827882112403)
XLA Ops:
  0.6 139.7 %layer.1 = (bf16[512,512]{1,0:T(8,128)(2,1)}, bf16[512,512]{1,0:T(8,128)(2,1)}, bf16[16,512]{1,0:T(8,128)(2,1)}, f32[32,128]{1,0:T(8,128)}, bf16[12,512,512]{2,1,0:T(8,128)(2,1)}, /*index=5*/f32[8,512]{1,0:T(8,128)}) custom-call(bf16[4096,512]{1,0:T(8,128)(2,1)} %bytes_hbm.1, s32[32,128]{1,0:T(8,128)} %bitcast.5, s32[1,4]{1,0:T(1,128)} %lengths_ref.1, ...), custom_call_target="tpu_custom_call" | custom-call | tf_op jit(solution)/shard_map/layer/pallas_call | solution.py:1376
  140.4 11.9 %expand.1 = (f32[4096,512]{1,0:T(8,128)}, f32[512,512]{1,0:T(8,128)}, f32[1,512]{1,0:T(1,128)}, f32[1,512]{1,0:T(1,128)}, f32[2048,512]{1,0:T(8,128)}, /*index=5...) custom-call(f32[32,128]{1,0:T(8,128)} %get-tuple-element.26.slots_ref, ...), custom_call_target="tpu_custom_call" | custom-call | tf_op jit(solution)/shard_map/expand/pallas_call | solution.py:1397

commit v6 on v5

--- a/solution.py
+++ b/solution.py
@@ -1281,10 +1281,11 @@
 
     for k in range(8):
         rows = [slots_ref[4 * k + r : 4 * k + r + 1, :] for r in range(4)]
+        reach = 64 * (k + 1)
         member = jnp.concatenate(
-            [(slot_iota == row).astype(F32).astype(BF16) for row in rows], axis=1
-        )
-        spread = mm(member, gs_ref[...], TN)
+            [(slot_iota[0:reach] == row).astype(F32).astype(BF16) for row in rows], axis=1
+        )
+        spread = mm(member, gs_ref[0:reach, :], TN)
         if k == 0:
             lead = jnp.concatenate(
                 [

time: 153 us -> 152 us (level)
  no operation moved by 1% of the time
where the time goes in v6:
time: 152 us
  Pallas kernels  151 us (99%)
    pallas_call x1, Pallas kernels, fast_local(): pl.pallas_call(layer_kernel, out_shape=(jax.ShapeDtypeStruct((512, 512),...  140 us
    pallas_call x1, Pallas kernels, fast_local(): pl.pallas_call(expand_kernel, out_shape=(jax.ShapeDtypeStruct((4096, 512)...  11.1 us

profile of v6, /device:TPU:9, one launch (start us, length us, event | category | flops | bytes accessed | tf_op | source)
XLA Modules:
  0.0 151.6 jit_solution(542430959980915110)
XLA Ops:
  0.6 139.7 %layer.1 = (bf16[512,512]{1,0:T(8,128)(2,1)}, bf16[512,512]{1,0:T(8,128)(2,1)}, bf16[16,512]{1,0:T(8,128)(2,1)}, f32[32,128]{1,0:T(8,128)}, bf16[12,512,512]{2,1,0:T(8,128)(2,1)}, /*index=5*/f32[8,512]{1,0:T(8,128)}) custom-call(bf16[4096,512]{1,0:T(8,128)(2,1)} %bytes_hbm.1, s32[32,128]{1,0:T(8,128)} %bitcast.5, s32[1,4]{1,0:T(1,128)} %lengths_ref.1, ...), custom_call_target="tpu_custom_call" | custom-call | tf_op jit(solution)/shard_map/layer/pallas_call | solution.py:1377
  140.4 11.1 %expand.1 = (f32[4096,512]{1,0:T(8,128)}, f32[512,512]{1,0:T(8,128)}, f32[1,512]{1,0:T(1,128)}, f32[1,512]{1,0:T(1,128)}, f32[2048,512]{1,0:T(8,128)}, /*index=5...) custom-call(f32[32,128]{1,0:T(8,128)} %get-tuple-element.26.slots_ref, ...), custom_call_target="tpu_custom_call" | custom-call | tf_op jit(solution)/shard_map/expand/pallas_call | solution.py:1398
